TPU v7x, 256 devices: a whole 4x4x8 slice. The times are simulated.
256 devices in a mesh: group: 16 (over z, core), dev: 16 (over y, x).
Axes of the slice: x: 4, y: 4, z: 8, core: 2. Of those that a mesh axis runs over, the one named last changes fastest.
Arguments:
- rhs_fine: float32 [256, 256, 512], P('group', 'dev'), may hold values from -6 to 6
- diag_fine: float32 [256, 256, 512], P('group', 'dev'), may hold values from 2 to 4
- coup_fine: bfloat16 [26, 256, 256, 512], P(None, 'group', 'dev'), may hold values from 0.0039978027 to 0.06982422
- diag_mid: float32 [128, 128, 256], P('group', 'dev'), may hold values from 2 to 4
- coup_mid: bfloat16 [26, 128, 128, 256], P(None, 'group', 'dev'), may hold values from 0.0039978027 to 0.06982422
- diag_coarse: float32 [64, 64, 128], P('group', 'dev'), may hold values from 2 to 4
- coup_coarse: bfloat16 [26, 64, 64, 128], P(None, 'group', 'dev'), may hold values from 0.0039978027 to 0.06982422
- owner_map: int32 [16, 16, 16, 1], P('group', 'dev'), may hold values from 0 to 15; in each aligned block of 16 rows (0 to 15, 16 to 31, ..., all dimensions but the last counted through in order) at most 2 rows name the same one
- inverse_blocks: float32 [16, 16, 32, 128, 128], P('group', 'dev'), may hold values from -0.5 to 0.5
Outputs:
- fine_iterate: float32 [256, 256, 512], P('group', 'dev')
- mid_iterate: float32 [128, 128, 256], P('group', 'dev')
- coarse_correction: float32 [64, 64, 128], P('group', 'dev')
- coarse_residual: float32 [64, 64, 128], P('group', 'dev')
Inputs may be any that keep to these rules, and one draw needn't show every extreme that they name: `owner_map`: owners lie in the block's own part group. On one device no owner is named by more than 2 of its 16 blocks, and in every draw some device names one owner exactly 2 times.
All inputs are finite; a program needn't handle non-finite values.
Results may differ from a plain program's by a relative error of at most 0.0003.
Values sent between devices are 32-bit elements; how exact they have to be, the bound alone decides.
No kernel may reach another device: no remote copies, remote signals or barrier semaphores. Data moves between devices by JAX's collectives and lax.ppermute only.
A program may use at most 128 MiB of HBM per device.

v0:
```python
import jax
import jax.numpy as jnp
from jax import lax
from jax.sharding import PartitionSpec as P

NU = 3


OMEGA = 0.8
HALVING = 0.5
OFFSETS = [
    (shift_x, shift_y, shift_z)
    for shift_x in (-1, 0, 1)
    for shift_y in (-1, 0, 1)
    for shift_z in (-1, 0, 1)
    if (shift_x, shift_y, shift_z) != (0, 0, 0)
]


def extended(x, sides, width):
    for axis, dim in sides:
        size, length = (lax.axis_size(axis), x.shape[dim])
        up = [(i, (i + 1) % size) for i in range(size - 1)]
        down = [(j, i) for i, j in up]
        last = lax.slice_in_dim(x, length - width, length, axis=dim)
        first = lax.slice_in_dim(x, 0, width, axis=dim)
        before = lax.ppermute(last, axis, up)
        after = lax.ppermute(first, axis, down)
        x = jnp.concatenate([before, x, after], axis=dim)
    return x


def stencil(padded, values, diagonal, couplings):
    length_x, length_y, length_z = values.shape[-3:]
    result = diagonal * values
    for position, (shift_x, shift_y, shift_z) in enumerate(OFFSETS):
        beside = padded[
            ...,
            1 + shift_x : 1 + shift_x + length_x,
            1 + shift_y : 1 + shift_y + length_y,
            1 + shift_z : 1 + shift_z + length_z,
        ]
        result = result - couplings[..., position, :, :, :].astype(jnp.float32) * beside
    return result


def frame_zero(values):
    widths = [(0, 0)] * (values.ndim - 3) + [(1, 1)] * 3
    return jnp.pad(values, widths)


def frame_fine(values):
    framed = extended(values, (("group", 0), ("dev", 1)), 1)
    return jnp.pad(framed, ((0, 0), (0, 0), (1, 1)))


def frame_mid(values):
    framed = extended(values, (("group", 0), ("dev", 1)), 1)
    return jnp.pad(framed, ((0, 0), (0, 0), (1, 1)))


def smooth_level(source, diagonal, couplings, framer):
    iterate = OMEGA * source / diagonal
    for sweep_index in range(NU - 1):
        iterate = (
            iterate
            + OMEGA * (source - stencil(framer(iterate), iterate, diagonal, couplings)) / diagonal
        )
    leftover = source - stencil(framer(iterate), iterate, diagonal, couplings)
    return (iterate, leftover)


def coarsen(values):
    length_x, length_y, length_z = values.shape
    grouped = values.reshape(length_x // 2, 2, length_y // 2, 2, length_z // 2, 2)
    return HALVING * jnp.sum(grouped, axis=(1, 3, 5))


def block_ranks(owners):
    blocks_count = owners.shape[-1]
    same_owner = owners[..., :, None] == owners[..., None, :]
    earlier = jnp.arange(blocks_count)[None, :] < jnp.arange(blocks_count)[:, None]
    return jnp.sum((same_owner & earlier).astype(jnp.int32), axis=-1)


def shards(
    rhs_fine,
    diag_fine,
    coup_fine,
    diag_mid,
    coup_mid,
    diag_coarse,
    coup_coarse,
    owner_map,
    inverse_blocks,
):
    fine_iterate, fine_left = smooth_level(rhs_fine, diag_fine, coup_fine, frame_fine)
    mid_iterate, mid_left = smooth_level(coarsen(fine_left), diag_mid, coup_mid, frame_mid)
    coarse_source = coarsen(mid_left)
    quarter_x, quarter_y, quarter_z = coarse_source.shape
    blocks_count = owner_map.shape[2]
    block_z = quarter_z // blocks_count
    block_cells = quarter_x * quarter_y * block_z
    device_count = lax.axis_size("dev")
    slots_total = inverse_blocks.shape[2]
    capacity = slots_total // device_count

    def local_blocks(values):
        return values.reshape(quarter_x, quarter_y, blocks_count, block_z).transpose(2, 0, 1, 3)

    def local_field(flat):
        return (
            flat.reshape(blocks_count, quarter_x, quarter_y, block_z)
            .transpose(1, 2, 0, 3)
            .reshape(quarter_x, quarter_y, quarter_z)
        )

    source_blocks = local_blocks(coarse_source)
    diag_blocks = local_blocks(diag_coarse)
    coup_blocks = coup_coarse.reshape(26, quarter_x, quarter_y, blocks_count, block_z).transpose(
        3, 0, 1, 2, 4
    )
    owners = owner_map.reshape(blocks_count)
    slot_index = owners * capacity + block_ranks(owners)
    outgoing = (
        jnp.zeros((slots_total, block_cells), jnp.float32)
        .at[slot_index]
        .set(source_blocks.reshape(blocks_count, block_cells))
        .reshape(device_count, capacity, block_cells)
    )
    arrived = lax.all_to_all(outgoing, "dev", split_axis=0, concat_axis=0, tiled=True).reshape(
        slots_total, block_cells
    )
    matrices = inverse_blocks.reshape(slots_total, block_cells, block_cells)
    owned = jnp.einsum("qij,qj->qi", matrices, arrived, precision=lax.Precision.HIGHEST)
    returned = lax.all_to_all(
        owned.reshape(device_count, capacity, block_cells),
        "dev",
        split_axis=0,
        concat_axis=0,
        tiled=True,
    ).reshape(slots_total, block_cells)
    correction = returned[slot_index]
    correction_cube = correction.reshape(blocks_count, quarter_x, quarter_y, block_z)
    leftover = source_blocks - stencil(
        frame_zero(correction_cube), correction_cube, diag_blocks, coup_blocks
    )
    mine = jnp.stack([correction, leftover.reshape(blocks_count, block_cells)], axis=1)
    return (fine_iterate, mid_iterate, local_field(mine[:, 0]), local_field(mine[:, 1]))


def solution(mesh):
    return jax.shard_map(
        shards,
        mesh=mesh,
        in_specs=(
            P("group", "dev", None),
            P("group", "dev", None),
            P(None, "group", "dev", None),
            P("group", "dev", None),
            P(None, "group", "dev", None),
            P("group", "dev", None),
            P(None, "group", "dev", None),
            P("group", "dev", None, None),
            P("group", "dev", None, None, None),
        ),
        out_specs=(
            P("group", "dev", None),
            P("group", "dev", None),
            P("group", "dev", None),
            P("group", "dev", None),
        ),
        check_vma=False,
    )
```

profile of v0, /device:TPU:128, one launch (start us, length us, event | category | flops | bytes accessed | tf_op | source)
XLA Modules:
  0.0 218.0 jit_solution(5680714088269024709)
XLA Ops:
  0.6 1.4 multiply_divide_fusion
  2.1 1.9 collective-permute-start
  4.0 4.9 %collective-permute-start.1 = (f32[1,16,512]{2,1,0:T(8,128)S(1)}, f32[1,16,512]{2,1,0:T(8,128)S(1)}, u32[]{:S(2)}, u32[]{:S(2)}) collective-permute-start(f32[1,16,512]{2,1,0:T(8,128)S(1)} %get-tuple-element.25), channel_id=1, source_target_pairs={{16,0},{32,16},{48,32},{64,48},{80,64},{96,80},{112,96},{128,112},... | collective-permute-start | bytes 98312 | tf_op jit(solution)/shard_map/ppermute | solution.py:28
  8.9 1.6 collective-permute-done.1
  10.5 3.4 %collective-permute-start.2 = (f32[18,1,512]{2,1,0:T(1,128)S(1)}, f32[18,1,512]{2,1,0:T(1,128)S(1)}, u32[]{:S(2)}, u32[]{:S(2)}) collective-permute-start(f32[18,1,512]{2,1,0:T(1,128)S(1)} %get-tuple-element.18), channel_id=1, source_target_pairs={{0,1},{1,2},{2,3},{3,4},{4,5},{5,6},{6,7},{7,8},{8,9},{9,10},{10,1... | collective-permute-start | bytes 110600 | tf_op jit(solution)/shard_map/ppermute | solution.py:27
  13.9 1.3 collective-permute-start.3
  15.6 4.2 %collective-permute-done.3 = f32[18,1,512]{2,1,0:T(1,128)S(1)} collective-permute-done((f32[18,1,512]{2,1,0:T(1,128)S(1)}, f32[18,1,512]{2,1,0:T(1,128)S(1)}, u32[]{:S(2)}, u32[]{:S(2)}) %collective-permute-start.3) | collective-permute-done | bytes 36896 | tf_op jit(solution)/shard_map/ppermute | solution.py:28
  21.0 5.6 %fusion.82 = (f32[16,16,512]{2,1,0:T(8,128)S(1)}, f32[16,16,512]{2,1,0:T(8,128)S(1)}) fusion(f32[16,16,512]{2,1,0:T(8,128)S(1)} %copy-done.2, f32[16,16,512]{2,1,0:T(8,128)S(1)} %copy-done.3, f32[18,18,514]{2,1,0:T(8,128)S(1)} %select_maximum_fusion.8, bf16[26,16,16,512]{3,2,1,0:T(8,128)(2,1)} %param.11, f32[18,17,512]{2,1,0:T(8,128)S(1)} %get-tuple-element.17, ...), kind=kLoop, calls=%fused_computation.208 | loop fusion | flops 11403264 | bytes 22085632 | tf_op jit(solution)/shard_map/add | solution.py:66
  26.6 1.9 collective-permute-start.4
  28.5 4.9 %collective-permute-start.5 = (f32[1,16,512]{2,1,0:T(8,128)S(1)}, f32[1,16,512]{2,1,0:T(8,128)S(1)}, u32[]{:S(2)}, u32[]{:S(2)}) collective-permute-start(f32[1,16,512]{2,1,0:T(8,128)S(1)} %get-tuple-element.23), channel_id=1, source_target_pairs={{16,0},{32,16},{48,32},{64,48},{80,64},{96,80},{112,96},{128,112},... | collective-permute-start | bytes 98312 | tf_op jit(solution)/shard_map/ppermute | solution.py:28
  33.4 1.6 collective-permute-done.5
  35.0 3.4 %collective-permute-start.6 = (f32[18,1,512]{2,1,0:T(1,128)S(1)}, f32[18,1,512]{2,1,0:T(1,128)S(1)}, u32[]{:S(2)}, u32[]{:S(2)}) collective-permute-start(f32[18,1,512]{2,1,0:T(1,128)S(1)} %get-tuple-element.14), channel_id=1, source_target_pairs={{0,1},{1,2},{2,3},{3,4},{4,5},{5,6},{6,7},{7,8},{8,9},{9,10},{10,1... | collective-permute-start | bytes 110600 | tf_op jit(solution)/shard_map/ppermute | solution.py:27
  38.4 1.3 collective-permute-start.7
  40.0 4.2 %collective-permute-done.7 = f32[18,1,512]{2,1,0:T(1,128)S(1)} collective-permute-done((f32[18,1,512]{2,1,0:T(1,128)S(1)}, f32[18,1,512]{2,1,0:T(1,128)S(1)}, u32[]{:S(2)}, u32[]{:S(2)}) %collective-permute-start.7) | collective-permute-done | bytes 36896 | tf_op jit(solution)/shard_map/ppermute | solution.py:28
  45.1 3.3 %fusion.87 = f32[16,16,512]{2,1,0:T(8,128)S(1)} fusion(f32[16,16,512]{2,1,0:T(8,128)S(1)} %get-tuple-element.6, f32[16,16,512]{2,1,0:T(8,128)S(1)} %copy-done.2, f32[16,16,512]{2,1,0:T(8,128)S(1)} %copy-done.3, f32[18,18,514]{2,1,0:T(8,128)S(1)} %select_maximum_fusion.4, f32[18,17,512]{2,1,0:T(8,128)S(1)} %get-tuple-element.13, ...), kind=kLoop, calls=%fused_computation.213 | loop fusion | flops 12189696 | bytes 22609920 | tf_op jit(solution)/shard_map/add | solution.py:66
  48.5 1.9 collective-permute-start.8
  50.4 4.9 %collective-permute-start.9 = (f32[1,16,512]{2,1,0:T(8,128)S(1)}, f32[1,16,512]{2,1,0:T(8,128)S(1)}, u32[]{:S(2)}, u32[]{:S(2)}) collective-permute-start(f32[1,16,512]{2,1,0:T(8,128)S(1)} %get-tuple-element.21), channel_id=1, source_target_pairs={{16,0},{32,16},{48,32},{64,48},{80,64},{96,80},{112,96},{128,112},... | collective-permute-start | bytes 98312 | tf_op jit(solution)/shard_map/ppermute | solution.py:28
  55.3 1.6 collective-permute-done.9
  56.9 4.7 %collective-permute-start.10 = (f32[18,1,512]{2,1,0:T(1,128)S(1)}, f32[18,1,512]{2,1,0:T(1,128)S(1)}, u32[]{:S(2)}, u32[]{:S(2)}) collective-permute-start(f32[18,1,512]{2,1,0:T(1,128)S(1)} %get-tuple-element.10), channel_id=1, source_target_pairs={{0,1},{1,2},{2,3},{3,4},{4,5},{5,6},{6,7},{7,8},{8,9},{9,10},{10,1... | collective-permute-start | bytes 110600 | tf_op jit(solution)/shard_map/ppermute | solution.py:27
  61.6 1.3 collective-permute-start.11
  63.3 4.2 %collective-permute-done.11 = f32[18,1,512]{2,1,0:T(1,128)S(1)} collective-permute-done((f32[18,1,512]{2,1,0:T(1,128)S(1)}, f32[18,1,512]{2,1,0:T(1,128)S(1)}, u32[]{:S(2)}, u32[]{:S(2)}) %collective-permute-start.11) | collective-permute-done | bytes 36896 | tf_op jit(solution)/shard_map/ppermute | solution.py:28
  68.3 2.9 %fusion.89 = f32[16,16,512]{2,1,0:T(8,128)S(1)} fusion(f32[16,16,512]{2,1,0:T(8,128)S(1)} %copy-done.3, f32[18,18,514]{2,1,0:T(8,128)S(1)} %select_maximum_fusion, f32[18,17,512]{2,1,0:T(8,128)S(1)} %get-tuple-element.9, f32[1,16,512]{2,1,0:T(8,128)S(1)} %collective-permute-done.9, f32[16,16,512]{2,1,0:T(8,128)S(1)} %fusion.87, ...), kind=kLoop, calls=%fused_computation.215 | loop fusion | flops 10747904 | bytes 21561344 | tf_op jit(solution)/shard_map/sub | solution.py:69
  71.2 34.9 %reshape.236 = f32[8,2,8,2,256,2]{5,4,3,2,1,0:T(8,128)} reshape(f32[16,16,512]{2,1,0:T(8,128)S(1)} %fusion.89) | data formatting | bytes 1048576 | tf_op jit(solution)/shard_map/reshape | solution.py:75
  106.1 12.2 %reduce_sum.29 = f32[8,8,256]{2,1,0:T(8,128)S(1)} reduce(f32[8,2,8,2,256,2]{5,4,3,2,1,0:T(8,128)} %reshape.236, f32[]{:T(128)} %constant.8.clone.1), dimensions={1,3,5}, to_apply=%region_0.1 | reduce | flops 114688 | bytes 589828 | tf_op jit(solution)/shard_map/reduce_sum | solution.py:76
  118.4 2.1 collective-permute-start.12
  120.5 4.9 %collective-permute-start.13 = (f32[1,8,256]{2,1,0:T(8,128)S(1)}, f32[1,8,256]{2,1,0:T(8,128)S(1)}, u32[]{:S(2)}, u32[]{:S(2)}) collective-permute-start(f32[1,8,256]{2,1,0:T(8,128)S(1)} %get-tuple-element.43), channel_id=1, source_target_pairs={{16,0},{32,16},{48,32},{64,48},{80,64},{96,80},{112,96},{128,112},... | collective-permute-start | bytes 24584 | tf_op jit(solution)/shard_map/ppermute | solution.py:28
  125.3 1.3 collective-permute-done.13
  126.7 4.0 %collective-permute-start.14 = (f32[10,1,256]{2,1,0:T(1,128)S(1)}, f32[10,1,256]{2,1,0:T(1,128)S(1)}, u32[]{:S(2)}, u32[]{:S(2)}) collective-permute-start(f32[10,1,256]{2,1,0:T(1,128)S(1)} %get-tuple-element.36), channel_id=1, source_target_pairs={{0,1},{1,2},{2,3},{3,4},{4,5},{5,6},{6,7},{7,8},{8,9},{9,10},{10,1... | collective-permute-start | bytes 30728 | tf_op jit(solution)/shard_map/ppermute | solution.py:27
  130.7 1.3 collective-permute-start.15
  132.1 4.2 %collective-permute-done.15 = f32[10,1,256]{2,1,0:T(1,128)S(1)} collective-permute-done((f32[10,1,256]{2,1,0:T(1,128)S(1)}, f32[10,1,256]{2,1,0:T(1,128)S(1)}, u32[]{:S(2)}, u32[]{:S(2)}) %collective-permute-start.15) | collective-permute-done | bytes 10272 | tf_op jit(solution)/shard_map/ppermute | solution.py:28
  136.9 1.9 collective-permute-start.16
  138.8 4.9 %collective-permute-start.17 = (f32[1,8,256]{2,1,0:T(8,128)S(1)}, f32[1,8,256]{2,1,0:T(8,128)S(1)}, u32[]{:S(2)}, u32[]{:S(2)}) collective-permute-start(f32[1,8,256]{2,1,0:T(8,128)S(1)} %get-tuple-element.41), channel_id=1, source_target_pairs={{16,0},{32,16},{48,32},{64,48},{80,64},{96,80},{112,96},{128,112},... | collective-permute-start | bytes 24584 | tf_op jit(solution)/shard_map/ppermute | solution.py:28
  143.7 1.3 collective-permute-done.17
  145.1 4.0 %collective-permute-start.18 = (f32[10,1,256]{2,1,0:T(1,128)S(1)}, f32[10,1,256]{2,1,0:T(1,128)S(1)}, u32[]{:S(2)}, u32[]{:S(2)}) collective-permute-start(f32[10,1,256]{2,1,0:T(1,128)S(1)} %get-tuple-element.32), channel_id=1, source_target_pairs={{0,1},{1,2},{2,3},{3,4},{4,5},{5,6},{6,7},{7,8},{8,9},{9,10},{10,1... | collective-permute-start | bytes 30728 | tf_op jit(solution)/shard_map/ppermute | solution.py:27
  150.5 4.2 %collective-permute-done.19 = f32[10,1,256]{2,1,0:T(1,128)S(1)} collective-permute-done((f32[10,1,256]{2,1,0:T(1,128)S(1)}, f32[10,1,256]{2,1,0:T(1,128)S(1)}, u32[]{:S(2)}, u32[]{:S(2)}) %collective-permute-start.19) | collective-permute-done | bytes 10272 | tf_op jit(solution)/shard_map/ppermute | solution.py:28
  155.3 1.9 collective-permute-start.20
  157.3 4.9 %collective-permute-start.21 = (f32[1,8,256]{2,1,0:T(8,128)S(1)}, f32[1,8,256]{2,1,0:T(8,128)S(1)}, u32[]{:S(2)}, u32[]{:S(2)}) collective-permute-start(f32[1,8,256]{2,1,0:T(8,128)S(1)} %get-tuple-element.39), channel_id=1, source_target_pairs={{16,0},{32,16},{48,32},{64,48},{80,64},{96,80},{112,96},{128,112},... | collective-permute-start | bytes 24584 | tf_op jit(solution)/shard_map/ppermute | solution.py:28
  163.5 4.0 %collective-permute-start.22 = (f32[10,1,256]{2,1,0:T(1,128)S(1)}, f32[10,1,256]{2,1,0:T(1,128)S(1)}, u32[]{:S(2)}, u32[]{:S(2)}) collective-permute-start(f32[10,1,256]{2,1,0:T(1,128)S(1)} %get-tuple-element.28), channel_id=1, source_target_pairs={{0,1},{1,2},{2,3},{3,4},{4,5},{5,6},{6,7},{7,8},{8,9},{9,10},{10,1... | collective-permute-start | bytes 30728 | tf_op jit(solution)/shard_map/ppermute | solution.py:27
  167.5 1.5 collective-permute-start.23
  169.0 4.1 %collective-permute-done.23 = f32[10,1,256]{2,1,0:T(1,128)S(1)} collective-permute-done((f32[10,1,256]{2,1,0:T(1,128)S(1)}, f32[10,1,256]{2,1,0:T(1,128)S(1)}, u32[]{:S(2)}, u32[]{:S(2)}) %collective-permute-start.23) | collective-permute-done | bytes 10272 | tf_op jit(solution)/shard_map/ppermute | solution.py:28
  173.7 5.5 %reshape.237 = f32[4,2,4,2,128,2]{5,4,3,2,1,0:T(8,128)} reshape(f32[8,8,256]{2,1,0:T(8,128)S(1)} %fusion.232) | data formatting | bytes 131072 | tf_op jit(solution)/shard_map/reshape | solution.py:75
  179.2 2.5 %reduce_sum.32 = f32[4,4,128]{2,1,0:T(4,128)S(1)} reduce(f32[4,2,4,2,128,2]{5,4,3,2,1,0:T(8,128)} %reshape.237, f32[]{:T(128)} %constant.8.clone.1), dimensions={1,3,5}, to_apply=%region_2.3 | reduce | flops 14336 | bytes 73732 | tf_op jit(solution)/shard_map/reduce_sum | solution.py:76
  182.7 16.1 %all_to_all.10 = f32[16,2,128]{2,1,0:T(2,128)S(1)} all-to-all(f32[16,2,128]{2,1,0:T(2,128)S(1)} %bitcast.494), channel_id=1, replica_groups=mesh['group'=16,'dev'=16] {'dev'}, dimensions={0} | all-to-all | bytes 32768 | tf_op jit(solution)/shard_map/all_to_all | solution.py:131
  198.8 4.0 %fusion = f32[32,1,128]{2,1,0:T(1,128)} fusion(f32[32,128,1]{1,2,0:T(1,128)S(1)} %bitcast.493, f32[1,1,32,128,128]{4,3,2,1,0:T(8,128)S(1)} %copy-done), kind=kOutput, calls=%fused_computation.2 | convolution fusion | flops 6291456 | bytes 2129920 | tf_op jit(solution)/shard_map/qij,qj->qi/dot_general | solution.py:135
  202.8 3.4 %all-to-all-start.1 = ((f32[16,2,128]{2,1,0:T(2,128)}), f32[16,2,128]{2,1,0:T(2,128)S(1)}, u32[]{:S(2)}, u32[]{:S(2)}) async-start(f32[16,2,128]{2,1,0:T(2,128)} %bitcast.117), calls=%async_computation.1 | async-start | bytes 32768 | tf_op jit(solution)/shard_map/all_to_all | solution.py:136
  206.6 3.9 %copy.38 = bf16[26,4,4,16,8]{4,3,2,1,0:T(8,128)(2,1)} copy(bf16[26,4,4,16,8]{0,4,3,2,1:T(8,128)(2,1)S(1)} %bitcast.487) | data formatting | bytes 212992 | tf_op jit(solution)/shard_map/reshape | solution.py:120
  210.6 3.1 %all-to-all-done.1 = f32[16,2,128]{2,1,0:T(2,128)S(1)} async-done(((f32[16,2,128]{2,1,0:T(2,128)}), f32[16,2,128]{2,1,0:T(2,128)S(1)}, u32[]{:S(2)}, u32[]{:S(2)}) %all-to-all-start.1) | async-done | bytes 16416 | tf_op jit(solution)/shard_map/all_to_all | solution.py:136
  214.5 2.0 fusion.142
  (83 shorter events, 12.2 us)
Async XLA Ops:
  0.6 198.2 %copy-start = (f32[1,1,32,128,128]{4,3,2,1,0:T(8,128)S(1)}, f32[1,1,32,128,128]{4,3,2,1,0:T(8,128)}, u32[]{:S(2)}) copy-start(f32[1,1,32,128,128]{4,3,2,1,0:T(8,128)} %param.17) | copy-start | bytes 6291460
  2.1 6.8 %collective-permute-start = (f32[1,16,512]{2,1,0:T(8,128)S(1)}, f32[1,16,512]{2,1,0:T(8,128)S(1)}, u32[]{:S(2)}, u32[]{:S(2)}) collective-permute-start(f32[1,16,512]{2,1,0:T(8,128)S(1)} %get-tuple-element.24), channel_id=1, source_target_pairs={{0,16},{16,32},{32,48},{48,64},{64,80},{80,96},{96,112},{112,128},... | collective-permute-start | bytes 98312 | tf_op jit(solution)/shard_map/ppermute | solution.py:27
  4.0 6.4 %collective-permute-start.1 = (f32[1,16,512]{2,1,0:T(8,128)S(1)}, f32[1,16,512]{2,1,0:T(8,128)S(1)}, u32[]{:S(2)}, u32[]{:S(2)}) collective-permute-start(f32[1,16,512]{2,1,0:T(8,128)S(1)} %get-tuple-element.25), channel_id=1, source_target_pairs={{16,0},{32,16},{48,32},{64,48},{80,64},{96,80},{112,96},{128,112},... | collective-permute-start | bytes 98312 | tf_op jit(solution)/shard_map/ppermute | solution.py:28
  10.5 5.0 %collective-permute-start.2 = (f32[18,1,512]{2,1,0:T(1,128)S(1)}, f32[18,1,512]{2,1,0:T(1,128)S(1)}, u32[]{:S(2)}, u32[]{:S(2)}) collective-permute-start(f32[18,1,512]{2,1,0:T(1,128)S(1)} %get-tuple-element.18), channel_id=1, source_target_pairs={{0,1},{1,2},{2,3},{3,4},{4,5},{5,6},{6,7},{7,8},{8,9},{9,10},{10,1... | collective-permute-start | bytes 110600 | tf_op jit(solution)/shard_map/ppermute | solution.py:27
  13.9 5.9 %collective-permute-start.3 = (f32[18,1,512]{2,1,0:T(1,128)S(1)}, f32[18,1,512]{2,1,0:T(1,128)S(1)}, u32[]{:S(2)}, u32[]{:S(2)}) collective-permute-start(f32[18,1,512]{2,1,0:T(1,128)S(1)} %get-tuple-element.19), channel_id=1, source_target_pairs={{1,0},{2,1},{3,2},{4,3},{5,4},{6,5},{7,6},{8,7},{9,8},{10,9},{11,1... | collective-permute-start | bytes 110600 | tf_op jit(solution)/shard_map/ppermute | solution.py:28
  19.8 1.0 copy-start.2
  19.8 1.2 copy-start.3
  20.0 25.1 %slice-start = ((s8[6815744]{0:T(1024)(128)(4,1)}), s8[4194304]{0:T(1024)(128)(4,1)S(1)}, s32[]{:S(2)}) async-start(s8[6815744]{0:T(1024)(128)(4,1)} %bitcast.484), calls=%async_computation.2 | async-start | bytes 8388608
  21.0 24.1 %slice-start.1 = ((s8[6815744]{0:T(1024)(128)(4,1)}), s8[2621440]{0:T(1024)(128)(4,1)S(1)}, s32[]{:S(2)}) async-start(s8[6815744]{0:T(1024)(128)(4,1)} %bitcast.484), calls=%async_computation.3 | async-start | bytes 5242880
  26.6 6.8 %collective-permute-start.4 = (f32[1,16,512]{2,1,0:T(8,128)S(1)}, f32[1,16,512]{2,1,0:T(8,128)S(1)}, u32[]{:S(2)}, u32[]{:S(2)}) collective-permute-start(f32[1,16,512]{2,1,0:T(8,128)S(1)} %get-tuple-element.22), channel_id=1, source_target_pairs={{0,16},{16,32},{32,48},{48,64},{64,80},{80,96},{96,112},{112,128},... | collective-permute-start | bytes 98312 | tf_op jit(solution)/shard_map/ppermute | solution.py:27
  28.5 6.4 %collective-permute-start.5 = (f32[1,16,512]{2,1,0:T(8,128)S(1)}, f32[1,16,512]{2,1,0:T(8,128)S(1)}, u32[]{:S(2)}, u32[]{:S(2)}) collective-permute-start(f32[1,16,512]{2,1,0:T(8,128)S(1)} %get-tuple-element.23), channel_id=1, source_target_pairs={{16,0},{32,16},{48,32},{64,48},{80,64},{96,80},{112,96},{128,112},... | collective-permute-start | bytes 98312 | tf_op jit(solution)/shard_map/ppermute | solution.py:28
  35.0 5.0 %collective-permute-start.6 = (f32[18,1,512]{2,1,0:T(1,128)S(1)}, f32[18,1,512]{2,1,0:T(1,128)S(1)}, u32[]{:S(2)}, u32[]{:S(2)}) collective-permute-start(f32[18,1,512]{2,1,0:T(1,128)S(1)} %get-tuple-element.14), channel_id=1, source_target_pairs={{0,1},{1,2},{2,3},{3,4},{4,5},{5,6},{6,7},{7,8},{8,9},{9,10},{10,1... | collective-permute-start | bytes 110600 | tf_op jit(solution)/shard_map/ppermute | solution.py:27
  38.4 5.9 %collective-permute-start.7 = (f32[18,1,512]{2,1,0:T(1,128)S(1)}, f32[18,1,512]{2,1,0:T(1,128)S(1)}, u32[]{:S(2)}, u32[]{:S(2)}) collective-permute-start(f32[18,1,512]{2,1,0:T(1,128)S(1)} %get-tuple-element.15), channel_id=1, source_target_pairs={{1,0},{2,1},{3,2},{4,3},{5,4},{6,5},{7,6},{8,7},{9,8},{10,9},{11,1... | collective-permute-start | bytes 110600 | tf_op jit(solution)/shard_map/ppermute | solution.py:28
  48.5 19.8 %copy-start.1 = (f32[16,16,512]{2,1,0:T(8,128)}, f32[16,16,512]{2,1,0:T(8,128)S(1)}, u32[]{:S(2)}) copy-start(f32[16,16,512]{2,1,0:T(8,128)S(1)} %fusion.87) | copy-start | bytes 1572868
  48.5 6.8 %collective-permute-start.8 = (f32[1,16,512]{2,1,0:T(8,128)S(1)}, f32[1,16,512]{2,1,0:T(8,128)S(1)}, u32[]{:S(2)}, u32[]{:S(2)}) collective-permute-start(f32[1,16,512]{2,1,0:T(8,128)S(1)} %get-tuple-element.20), channel_id=1, source_target_pairs={{0,16},{16,32},{32,48},{48,64},{64,80},{80,96},{96,112},{112,128},... | collective-permute-start | bytes 98312 | tf_op jit(solution)/shard_map/ppermute | solution.py:27
  50.4 6.4 %collective-permute-start.9 = (f32[1,16,512]{2,1,0:T(8,128)S(1)}, f32[1,16,512]{2,1,0:T(8,128)S(1)}, u32[]{:S(2)}, u32[]{:S(2)}) collective-permute-start(f32[1,16,512]{2,1,0:T(8,128)S(1)} %get-tuple-element.21), channel_id=1, source_target_pairs={{16,0},{32,16},{48,32},{64,48},{80,64},{96,80},{112,96},{128,112},... | collective-permute-start | bytes 98312 | tf_op jit(solution)/shard_map/ppermute | solution.py:28
  56.9 6.3 %collective-permute-start.10 = (f32[18,1,512]{2,1,0:T(1,128)S(1)}, f32[18,1,512]{2,1,0:T(1,128)S(1)}, u32[]{:S(2)}, u32[]{:S(2)}) collective-permute-start(f32[18,1,512]{2,1,0:T(1,128)S(1)} %get-tuple-element.10), channel_id=1, source_target_pairs={{0,1},{1,2},{2,3},{3,4},{4,5},{5,6},{6,7},{7,8},{8,9},{9,10},{10,1... | collective-permute-start | bytes 110600 | tf_op jit(solution)/shard_map/ppermute | solution.py:27
  61.6 5.9 %collective-permute-start.11 = (f32[18,1,512]{2,1,0:T(1,128)S(1)}, f32[18,1,512]{2,1,0:T(1,128)S(1)}, u32[]{:S(2)}, u32[]{:S(2)}) collective-permute-start(f32[18,1,512]{2,1,0:T(1,128)S(1)} %get-tuple-element.11), channel_id=1, source_target_pairs={{1,0},{2,1},{3,2},{4,3},{5,4},{6,5},{7,6},{8,7},{9,8},{10,9},{11,1... | collective-permute-start | bytes 110600 | tf_op jit(solution)/shard_map/ppermute | solution.py:28
  106.1 12.2 %copy-start.6 = (f32[8,8,256]{2,1,0:T(8,128)S(1)}, f32[8,8,256]{2,1,0:T(8,128)}, u32[]{:S(2)}) copy-start(f32[8,8,256]{2,1,0:T(8,128)} %param.12) | copy-start | bytes 196612
  118.4 18.2 %copy-start.4 = (bf16[26,8,8,256]{3,2,1,0:T(8,128)(2,1)S(1)}, bf16[26,8,8,256]{3,2,1,0:T(8,128)(2,1)}, u32[]{:S(2)}) copy-start(bf16[26,8,8,256]{3,2,1,0:T(8,128)(2,1)} %param.13) | copy-start | bytes 2555908
  118.4 6.9 %collective-permute-start.12 = (f32[1,8,256]{2,1,0:T(8,128)S(1)}, f32[1,8,256]{2,1,0:T(8,128)S(1)}, u32[]{:S(2)}, u32[]{:S(2)}) collective-permute-start(f32[1,8,256]{2,1,0:T(8,128)S(1)} %get-tuple-element.42), channel_id=1, source_target_pairs={{0,16},{16,32},{32,48},{48,64},{64,80},{80,96},{96,112},{112,128},... | collective-permute-start | bytes 24584 | tf_op jit(solution)/shard_map/ppermute | solution.py:27
  120.5 6.2 %collective-permute-start.13 = (f32[1,8,256]{2,1,0:T(8,128)S(1)}, f32[1,8,256]{2,1,0:T(8,128)S(1)}, u32[]{:S(2)}, u32[]{:S(2)}) collective-permute-start(f32[1,8,256]{2,1,0:T(8,128)S(1)} %get-tuple-element.43), channel_id=1, source_target_pairs={{16,0},{32,16},{48,32},{64,48},{80,64},{96,80},{112,96},{128,112},... | collective-permute-start | bytes 24584 | tf_op jit(solution)/shard_map/ppermute | solution.py:28
  126.7 5.4 %collective-permute-start.14 = (f32[10,1,256]{2,1,0:T(1,128)S(1)}, f32[10,1,256]{2,1,0:T(1,128)S(1)}, u32[]{:S(2)}, u32[]{:S(2)}) collective-permute-start(f32[10,1,256]{2,1,0:T(1,128)S(1)} %get-tuple-element.36), channel_id=1, source_target_pairs={{0,1},{1,2},{2,3},{3,4},{4,5},{5,6},{6,7},{7,8},{8,9},{9,10},{10,1... | collective-permute-start | bytes 30728 | tf_op jit(solution)/shard_map/ppermute | solution.py:27
  130.7 5.6 %collective-permute-start.15 = (f32[10,1,256]{2,1,0:T(1,128)S(1)}, f32[10,1,256]{2,1,0:T(1,128)S(1)}, u32[]{:S(2)}, u32[]{:S(2)}) collective-permute-start(f32[10,1,256]{2,1,0:T(1,128)S(1)} %get-tuple-element.37), channel_id=1, source_target_pairs={{1,0},{2,1},{3,2},{4,3},{5,4},{6,5},{7,6},{8,7},{9,8},{10,9},{11,1... | collective-permute-start | bytes 30728 | tf_op jit(solution)/shard_map/ppermute | solution.py:28
  136.9 6.8 %collective-permute-start.16 = (f32[1,8,256]{2,1,0:T(8,128)S(1)}, f32[1,8,256]{2,1,0:T(8,128)S(1)}, u32[]{:S(2)}, u32[]{:S(2)}) collective-permute-start(f32[1,8,256]{2,1,0:T(8,128)S(1)} %get-tuple-element.40), channel_id=1, source_target_pairs={{0,16},{16,32},{32,48},{48,64},{64,80},{80,96},{96,112},{112,128},... | collective-permute-start | bytes 24584 | tf_op jit(solution)/shard_map/ppermute | solution.py:27
  138.8 6.2 %collective-permute-start.17 = (f32[1,8,256]{2,1,0:T(8,128)S(1)}, f32[1,8,256]{2,1,0:T(8,128)S(1)}, u32[]{:S(2)}, u32[]{:S(2)}) collective-permute-start(f32[1,8,256]{2,1,0:T(8,128)S(1)} %get-tuple-element.41), channel_id=1, source_target_pairs={{16,0},{32,16},{48,32},{64,48},{80,64},{96,80},{112,96},{128,112},... | collective-permute-start | bytes 24584 | tf_op jit(solution)/shard_map/ppermute | solution.py:28
  145.1 5.4 %collective-permute-start.18 = (f32[10,1,256]{2,1,0:T(1,128)S(1)}, f32[10,1,256]{2,1,0:T(1,128)S(1)}, u32[]{:S(2)}, u32[]{:S(2)}) collective-permute-start(f32[10,1,256]{2,1,0:T(1,128)S(1)} %get-tuple-element.32), channel_id=1, source_target_pairs={{0,1},{1,2},{2,3},{3,4},{4,5},{5,6},{6,7},{7,8},{8,9},{9,10},{10,1... | collective-permute-start | bytes 30728 | tf_op jit(solution)/shard_map/ppermute | solution.py:27
  149.1 5.6 %collective-permute-start.19 = (f32[10,1,256]{2,1,0:T(1,128)S(1)}, f32[10,1,256]{2,1,0:T(1,128)S(1)}, u32[]{:S(2)}, u32[]{:S(2)}) collective-permute-start(f32[10,1,256]{2,1,0:T(1,128)S(1)} %get-tuple-element.33), channel_id=1, source_target_pairs={{1,0},{2,1},{3,2},{4,3},{5,4},{6,5},{7,6},{8,7},{9,8},{10,9},{11,1... | collective-permute-start | bytes 30728 | tf_op jit(solution)/shard_map/ppermute | solution.py:28
  154.9 7.2 %copy-start.9 = (s32[1,1,16,1]{2,3,1,0:T(1,128)S(1)}, s32[1,1,16,1]{2,3,1,0:T(1,128)}, u32[]{:S(2)}) copy-start(s32[1,1,16,1]{2,3,1,0:T(1,128)} %param.16) | copy-start | bytes 196
  155.3 18.4 %copy-start.5 = (f32[8,8,256]{2,1,0:T(8,128)}, f32[8,8,256]{2,1,0:T(8,128)S(1)}, u32[]{:S(2)}) copy-start(f32[8,8,256]{2,1,0:T(8,128)S(1)} %fusion.230) | copy-start | bytes 196612
  155.3 7.0 %collective-permute-start.20 = (f32[1,8,256]{2,1,0:T(8,128)S(1)}, f32[1,8,256]{2,1,0:T(8,128)S(1)}, u32[]{:S(2)}, u32[]{:S(2)}) collective-permute-start(f32[1,8,256]{2,1,0:T(8,128)S(1)} %get-tuple-element.38), channel_id=1, source_target_pairs={{0,16},{16,32},{32,48},{48,64},{64,80},{80,96},{96,112},{112,128},... | collective-permute-start | bytes 24584 | tf_op jit(solution)/shard_map/ppermute | solution.py:27
  157.3 6.2 %collective-permute-start.21 = (f32[1,8,256]{2,1,0:T(8,128)S(1)}, f32[1,8,256]{2,1,0:T(8,128)S(1)}, u32[]{:S(2)}, u32[]{:S(2)}) collective-permute-start(f32[1,8,256]{2,1,0:T(8,128)S(1)} %get-tuple-element.39), channel_id=1, source_target_pairs={{16,0},{32,16},{48,32},{64,48},{80,64},{96,80},{112,96},{128,112},... | collective-permute-start | bytes 24584 | tf_op jit(solution)/shard_map/ppermute | solution.py:28
  163.5 5.5 %collective-permute-start.22 = (f32[10,1,256]{2,1,0:T(1,128)S(1)}, f32[10,1,256]{2,1,0:T(1,128)S(1)}, u32[]{:S(2)}, u32[]{:S(2)}) collective-permute-start(f32[10,1,256]{2,1,0:T(1,128)S(1)} %get-tuple-element.28), channel_id=1, source_target_pairs={{0,1},{1,2},{2,3},{3,4},{4,5},{5,6},{6,7},{7,8},{8,9},{9,10},{10,1... | collective-permute-start | bytes 30728 | tf_op jit(solution)/shard_map/ppermute | solution.py:27
  167.5 5.6 %collective-permute-start.23 = (f32[10,1,256]{2,1,0:T(1,128)S(1)}, f32[10,1,256]{2,1,0:T(1,128)S(1)}, u32[]{:S(2)}, u32[]{:S(2)}) collective-permute-start(f32[10,1,256]{2,1,0:T(1,128)S(1)} %get-tuple-element.29), channel_id=1, source_target_pairs={{1,0},{2,1},{3,2},{4,3},{5,4},{6,5},{7,6},{8,7},{9,8},{10,9},{11,1... | collective-permute-start | bytes 30728 | tf_op jit(solution)/shard_map/ppermute | solution.py:28
  182.7 23.5 %copy-start.7 = (bf16[26,4,4,128]{3,2,1,0:T(4,128)(2,1)S(1)}, bf16[26,4,4,128]{3,2,1,0:T(4,128)(2,1)}, u32[]{:S(2)}) copy-start(bf16[26,4,4,128]{3,2,1,0:T(4,128)(2,1)} %param.15) | copy-start | bytes 319492
  202.8 11.0 %all-to-all-start.1 = ((f32[16,2,128]{2,1,0:T(2,128)}), f32[16,2,128]{2,1,0:T(2,128)S(1)}, u32[]{:S(2)}, u32[]{:S(2)}) async-start(f32[16,2,128]{2,1,0:T(2,128)} %bitcast.117), calls=%async_computation.1 | async-start | bytes 32768 | tf_op jit(solution)/shard_map/all_to_all | solution.py:136
  206.6 3.9 %copy-start.8 = (f32[4,4,128]{2,1,0:T(4,128)S(1)}, f32[4,4,128]{2,1,0:T(4,128)}, u32[]{:S(2)}) copy-start(f32[4,4,128]{2,1,0:T(4,128)} %param.14) | copy-start | bytes 24580
where the time goes:
time: 219 us; the launch traced here: 218 us
  starting transfers between devices  75.7 us (35%)
  local copies, waits for them, and re-layouts  48.4 us (22%)
  waiting for transfers between devices  37.9 us (17%)
  other arithmetic  34.6 us (16%)
  blocking collectives  16.1 us (7%)
  matrix products  3.97 us (2%)
    reshape x2, local copies, waits for them, and re-layouts, coarsen(): values.reshape(length_x // 2, 2, length_y // 2, 2, length_z // 2, 2)  40.4 us
    ppermute x12, starting transfers between devices, extended(): after = lax.ppermute(first, axis, down)  37 us
    ppermute x12, starting transfers between devices, extended(): before = lax.ppermute(last, axis, up)  35.2 us
    ppermute x12, waiting for transfers between devices, extended(): after = lax.ppermute(first, axis, down)  33.7 us
    all_to_all x1, blocking collectives, shards(): lax.all_to_all(outgoing, 'dev', split_axis=0, concat_axis=0, tiled=True)  16.1 us
    reduce_sum x2, other arithmetic, coarsen(): return HALVING * jnp.sum(grouped, axis=(1, 3, 5))  14.8 us
    add x4, other arithmetic, smooth_level(): iterate + OMEGA * (source - stencil(framer(iterate), iterate, diagonal, c...  9.64 us
  transfers between devices with their start and end apart: 25, of which 18 were waited for; matrix products, arithmetic and copies ran while one was open for 2% of the time, Pallas kernels for 0%

commit v1 on v0

v1 whole, which is shorter than its diff:
```python
import functools

import jax
import jax.numpy as jnp
from jax import lax
from jax.experimental import pallas as pl
from jax.experimental.pallas import tpu as pltpu
from jax.sharding import PartitionSpec as P

OMEGA = 0.8
HALVING = 0.5
OFFSETS = [
    (a, b, c)
    for a in (-1, 0, 1)
    for b in (-1, 0, 1)
    for c in (-1, 0, 1)
    if (a, b, c) != (0, 0, 0)
]
TO_YLO = [OFFSETS.index((a, -1, c)) for a in (-1, 0, 1) for c in (-1, 0, 1)]
TO_YHI = [OFFSETS.index((a, 1, c)) for a in (-1, 0, 1) for c in (-1, 0, 1)]
F32 = jnp.float32
HIGHEST = lax.Precision.HIGHEST
VMEM_LIMIT = 20 * 1024 * 1024
XB = 4
WIDE = 3
X_LO, X_HI, Y_LO, Y_HI, X_ODD, Y_ODD = range(6)
LONG = 30_000_000_000
VMEM = pl.BlockSpec(memory_space=pltpu.VMEM)
SMEM = pl.BlockSpec(memory_space=pltpu.SMEM)


def sds(shape, dtype=F32):
    return jax.ShapeDtypeStruct(shape, dtype)


def iota(shape, dim):
    return lax.broadcasted_iota(jnp.int32, shape, dim)


def shift_z(v, c):
    if c == 0:
        return v
    n, dim = v.shape[-1], v.ndim - 1
    edge = 0 if c < 0 else n - 1
    return jnp.where(iota(v.shape, dim) == edge, 0.0, pltpu.roll(v, (-c) % n, dim))


def shift_y(v, b):
    if b == 0:
        return v
    n, dim = v.shape[-2], v.ndim - 2
    edge = 0 if b < 0 else n - 1
    return jnp.where(iota(v.shape, dim) == edge, 0.0, pltpu.roll(v, (-b) % n, dim))


def pair_sum_right(n, scale):
    return jnp.where((iota((n, n // 2), 0) >> 1) == iota((n, n // 2), 1), scale, 0.0).astype(F32)


def pair_sum_left(n):
    return jnp.where((iota((n // 2, n), 1) >> 1) == iota((n // 2, n), 0), 1.0, 0.0).astype(F32)


def dot(a, b):
    return jnp.dot(a, b, precision=HIGHEST, preferred_element_type=F32)


def put_versions(s_ref, x, layer):
    for c in (-1, 0, 1):
        along = shift_z(layer, c)
        for b in (-1, 0, 1):
            s_ref[(b + 1) * 3 + c + 1, x + 1] = shift_y(along, b)


def neighbours(w_ref, s_ref, first, at):
    total = [None] * XB
    for b in (-1, 0, 1):
        for c in (-1, 0, 1):
            k = (b + 1) * 3 + c + 1
            layers = [s_ref[k, first + r, :, at] for r in range(XB + 2)]
            for a in (-1, 0, 1):
                if (a, b, c) == (0, 0, 0):
                    continue
                o = OFFSETS.index((a, b, c))
                for i in range(XB):
                    term = w_ref[o, first + i, :, at].astype(F32) * layers[i + 1 + a]
                    total[i] = term if total[i] is None else total[i] + term
    return total


def lane_chunks(n):
    return [slice(k, k + 128) for k in range(0, n, 128)]


def zero_rims(s_ref):
    for edge in (0, s_ref.shape[1] - 1):
        for k in range(9):
            s_ref[k, edge] = jnp.zeros(s_ref.shape[2:], F32)


def patched(v_ref, new, x, last):
    xlo, xhi, ylo, yhi = new
    layer = v_ref[x]
    row = iota(layer.shape, 0)
    layer = jnp.where(row == 0, ylo[pl.ds(x, 1), :], layer)
    layer = jnp.where(row == layer.shape[0] - 1, yhi[pl.ds(x, 1), :], layer)
    layer = jnp.where(x == 0, xlo[...], layer)
    return jnp.where(x == last, xhi[...], layer)


def put_faces(faces_ref, v_ref):
    nx, ny = v_ref.shape[:2]
    faces_ref[0] = v_ref[0]
    faces_ref[1] = v_ref[nx - 1]
    for x in range(nx):
        faces_ref[2, x : x + 1, :] = v_ref[x, 0:1, :]
        faces_ref[3, x : x + 1, :] = v_ref[x, ny - 1 : ny, :]


def put_next(v_ref, start_ref, q_ref, w_ref, s_ref, j):
    for at in lane_chunks(v_ref.shape[2]):
        for i, total in enumerate(neighbours(w_ref, s_ref, j * XB, at)):
            x = j * XB + i
            centre = (1.0 - OMEGA) * s_ref[4, x + 1, :, at]
            v_ref[x, :, at] = centre + start_ref[x, :, at] + q_ref[x, :, at] * total


def fine_start(flags, f_ref, d_ref, start_ref, q_ref, x_even, x_odd, ylo, yhi):
    nx, ny = f_ref.shape[:2]

    @pl.loop(0, nx)
    def _(x):
        q = OMEGA / d_ref[x]
        q_ref[x] = q
        start_ref[x] = q * f_ref[x]

    put_both(flags[X_ODD] > 0, x_even, x_odd, slice(None), start_ref[0], start_ref[nx - 1])
    for x in range(nx):
        ylo[x : x + 1, :] = start_ref[x, 0:1, :]
        yhi[x : x + 1, :] = start_ref[x, ny - 1 : ny, :]


def fine_first(
    start_ref, q_ref, w_ref, v_ref, faces_ref, qfaces_ref, wfaces_ref, s_ref, wy_ref
):
    nx, ny = v_ref.shape[:2]
    zero_rims(s_ref)

    @pl.loop(0, nx)
    def _(x):
        put_versions(s_ref, x, start_ref[x])

    @pl.loop(0, nx // XB)
    def _(j):
        put_next(v_ref, start_ref, q_ref, w_ref, s_ref, j)
        for i in range(XB):
            x = j * XB + i
            for k in range(9):
                wy_ref[0, k, pl.ds(x, 1), :] = w_ref[TO_YLO[k], x].astype(F32)[0:1, :]
                wy_ref[1, k, pl.ds(x, 1), :] = w_ref[TO_YHI[k], x].astype(F32)[ny - 1 : ny, :]

    wfaces_ref[0] = w_ref[0:9, 0]
    wfaces_ref[1] = w_ref[17:26, nx - 1]
    for k in range(9):
        wfaces_ref[2, k] = wy_ref[0, k].astype(wfaces_ref.dtype)
        wfaces_ref[3, k] = wy_ref[1, k].astype(wfaces_ref.dtype)
    put_faces(faces_ref, v_ref)
    put_faces(qfaces_ref, q_ref)


def fine_next(v_ref, xlo, xhi, ylo, yhi, start_ref, q_ref, w_ref, out_ref, faces_ref, s_ref):
    nx = v_ref.shape[0]
    zero_rims(s_ref)

    @pl.loop(0, nx)
    def _(x):
        put_versions(s_ref, x, patched(v_ref, (xlo, xhi, ylo, yhi), x, nx - 1))

    @pl.loop(0, nx // XB)
    def _(j):
        put_next(out_ref, start_ref, q_ref, w_ref, s_ref, j)

    put_faces(faces_ref, out_ref)


def fine_last(v_ref, xlo, xhi, ylo, yhi, start_ref, q_ref, w_ref, out_ref, g_ref, s_ref, p_ref):
    nx, ny, nz = v_ref.shape
    zero_rims(s_ref)

    @pl.loop(0, nx)
    def _(x):
        layer = patched(v_ref, (xlo, xhi, ylo, yhi), x, nx - 1)
        out_ref[x] = layer
        put_versions(s_ref, x, layer)

    @pl.loop(0, nx // XB)
    def _(j):
        for at in lane_chunks(nz):
            total = neighbours(w_ref, s_ref, j * XB, at)
            for i in range(XB):
                x = j * XB + i
                own = start_ref[x, :, at] - OMEGA * s_ref[4, x + 1, :, at]
                total[i] = total[i] + own / q_ref[x, :, at]
            for i in range(0, XB, 2):
                row = pl.multiple_of((j * (XB // 2) + i // 2) * ny, ny)
                p_ref[pl.ds(row, ny), at] = total[i] + total[i + 1]

    rows = dot(pair_sum_left(nx // 2 * ny), p_ref[...])
    g_ref[...] = dot(rows, pair_sum_right(nz, HALVING)).reshape(g_ref.shape)


def sides(flags, even, odd, lo, hi, parity):
    at_odd = flags[parity] > 0
    below = jnp.where(at_odd, even, odd)
    above = jnp.where(at_odd, odd, even)
    return jnp.where(flags[lo] > 0, below, 0.0), jnp.where(flags[hi] > 0, above, 0.0)


def halo_terms(flags, x_even, x_odd, y_even, y_odd, w_ref):
    xs, ys = [], []
    n = x_even.shape[0]
    x_sides = sides(flags, x_even[...], x_odd[...], X_LO, X_HI, X_ODD)
    y_sides = sides(flags, y_even[...], y_odd[...], Y_LO, Y_HI, Y_ODD)
    for side, halo in enumerate(x_sides):
        total = None
        for c in (-1, 0, 1):
            along = shift_z(halo, c)
            for b in (-1, 0, 1):
                term = w_ref[side, (b + 1) * 3 + c + 1].astype(F32) * shift_y(along, b)
                total = term if total is None else total + term
        xs.append(total)
    for side, halo in enumerate(y_sides):
        total = None
        for c in (-1, 0, 1):
            along = shift_z(halo, c)
            for a in (-1, 0, 1):
                term = w_ref[2 + side, (a + 1) * 3 + c + 1].astype(F32) * along[1 + a : 1 + a + n]
                total = term if total is None else total + term
        ys.append(total)
    return xs, ys


def fine_halo(flags, x_even, x_odd, y_even, y_odd, w_ref, faces_ref, q_ref, *outs):
    xs, ys = halo_terms(flags, x_even, x_odd, y_even, y_odd, w_ref)
    n = xs[0].shape[0]
    row = iota(xs[0].shape, 0)

    def crossed(own, others, place):
        own = jnp.where(row == 0, own + others[0][place : place + 1], own)
        return jnp.where(row == n - 1, own + others[1][place : place + 1], own)

    sums = [
        crossed(xs[0], ys, 0),
        crossed(xs[1], ys, n - 1),
        crossed(ys[0], xs, 0),
        crossed(ys[1], xs, n - 1),
    ]
    new = [faces_ref[k] + q_ref[k] * sums[k] for k in range(4)]
    for k in range(4):
        outs[k][...] = new[k]
    at_odd = flags[X_ODD] > 0
    outs[4][...] = jnp.where(at_odd, new[0], new[1])
    outs[5][...] = jnp.where(at_odd, new[1], new[0])


def fine_halo_last(
    flags, x_even, x_odd, y_even, y_odd, w_ref, g_ref, f_ref, to_even, to_odd, t_ref
):
    xs, ys = halo_terms(flags, x_even, x_odd, y_even, y_odd, w_ref)
    n, nz = xs[0].shape
    for k, part in enumerate(xs + ys):
        t_ref[k * n : (k + 1) * n, :] = part
    rows = dot(pair_sum_left(4 * n), t_ref[...])
    half = n // 2
    coarse = dot(rows, pair_sum_right(nz, HALVING))
    row = iota((half, nz // 2), 0)
    for i in range(half):
        total = g_ref[i]
        total = total + jnp.where(row == 0, coarse[2 * half + i : 2 * half + i + 1], 0.0)
        total = total + jnp.where(row == half - 1, coarse[3 * half + i : 3 * half + i + 1], 0.0)
        if i == 0:
            total = total + coarse[0:half]
        if i == half - 1:
            total = total + coarse[half : 2 * half]
        f_ref[i] = total
    at_odd = flags[X_ODD] > 0
    for k in range(WIDE):
        lo, hi = f_ref[k], f_ref[half - WIDE + k]
        to_even[k] = jnp.where(at_odd, lo, hi)
        to_odd[k] = jnp.where(at_odd, hi, lo)


def put_both(at_odd, even_ref, odd_ref, index, lo, hi):
    even_ref[index] = jnp.where(at_odd, lo, hi)
    odd_ref[index] = jnp.where(at_odd, hi, lo)


def mid_pack(flags, w_ref, d_ref, x_even, x_odd):
    nx = d_ref.shape[0]
    at_odd = flags[X_ODD] > 0

    @pl.loop(0, 26)
    def _(o):
        for k in range(2):
            lo, hi = w_ref[o, k].astype(F32), w_ref[o, nx - 2 + k].astype(F32)
            put_both(at_odd, x_even, x_odd, o * 2 + k, lo, hi)

    for k in range(WIDE):
        put_both(at_odd, x_even, x_odd, 52 + k, d_ref[k], d_ref[nx - WIDE + k])


def mid_assemble(flags, w_ref, d_ref, x_even, x_odd, w_out, q_out):
    nx = d_ref.shape[0]
    at_odd = flags[X_ODD] > 0

    def beyond(index, below):
        first, second = (x_even, x_odd) if below else (x_odd, x_even)
        return jnp.where(at_odd, first[index], second[index])

    @pl.loop(0, 26)
    def _(o):
        for x in range(nx):
            w_out[o, x + 2] = w_ref[o, x]
        for k in range(2):
            w_out[o, k] = beyond(o * 2 + k, True).astype(w_out.dtype)
            w_out[o, nx + 2 + k] = beyond(o * 2 + k, False).astype(w_out.dtype)

    for x in range(nx):
        q_out[x + WIDE] = OMEGA / d_ref[x]
    for k in range(WIDE):
        q_out[k] = OMEGA / beyond(52 + k, True)
        q_out[nx + WIDE + k] = OMEGA / beyond(52 + k, False)


def mid_start(flags, f_ref, e_ref, o_ref, q_ref, start_ref, y_even, y_odd):
    nx, ny = f_ref.shape[:2]
    x_odd, y_is_odd = flags[X_ODD] > 0, flags[Y_ODD] > 0
    for r in range(nx + 2 * WIDE):
        if r < WIDE:
            f = jnp.where(x_odd, e_ref[r], o_ref[r])
            f = jnp.where(flags[X_LO] > 0, f, 0.0)
        elif r >= nx + WIDE:
            k = r - nx - WIDE
            f = jnp.where(x_odd, o_ref[k], e_ref[k])
            f = jnp.where(flags[X_HI] > 0, f, 0.0)
        else:
            f = f_ref[r - WIDE]
        start = q_ref[r] * f
        start_ref[r] = start
        index = (slice(r, r + 1), slice(None))
        put_both(y_is_odd, y_even, y_odd, index, start[0:1], start[ny - 1 : ny])


def mid_neighbours(flags, v_ref, y_even, y_odd, w_ref, s_ref, reach):
    ny = v_ref.shape[1]
    y_lo, y_hi = sides(flags, y_even[...], y_odd[...], Y_LO, Y_HI, Y_ODD)
    row = iota(v_ref.shape[1:], 0)
    for r in range(v_ref.shape[0]):
        layer = v_ref[r]
        below = jnp.where(row == 0, y_lo[r : r + 1], pltpu.roll(layer, 1, 0))
        above = jnp.where(row == ny - 1, y_hi[r : r + 1], pltpu.roll(layer, ny - 1, 0))
        for b, moved in enumerate((below, layer, above)):
            for c in (-1, 0, 1):
                s_ref[b * 3 + c + 1, r] = shift_z(moved, c)

    def neighbours_of(x):
        total = None
        for o, (a, b, c) in enumerate(OFFSETS):
            term = w_ref[o, x + 2].astype(F32) * s_ref[(b + 1) * 3 + c + 1, x + a + reach]
            total = term if total is None else total + term
        return total

    return neighbours_of


def mid_next(
    reach, flags, v_ref, y_even, y_odd, start_ref, q_ref, w_ref, out_ref, to_even, to_odd, s_ref
):
    nx, ny = q_ref.shape[0] - 2 * WIDE, q_ref.shape[1]
    layers = range(1 - reach, nx + reach - 1)
    total = mid_neighbours(flags, v_ref, y_even, y_odd, w_ref, s_ref, reach)
    for k, x in enumerate(layers):
        new = (1.0 - OMEGA) * v_ref[k + 1] + start_ref[x + WIDE] + q_ref[x + WIDE] * total(x)
        if x < 0:
            new = jnp.where(flags[X_LO] > 0, new, 0.0)
        if x >= nx:
            new = jnp.where(flags[X_HI] > 0, new, 0.0)
        out_ref[k] = new
        index = (slice(k, k + 1), slice(None))
        put_both(flags[Y_ODD] > 0, to_even, to_odd, index, new[0:1], new[ny - 1 : ny])


def swap_blocks(values):
    n, lanes = values.shape
    width = lanes // n
    wide = jnp.broadcast_to(values[None], (n, n, lanes))
    wide = jnp.where(iota(wide.shape, 2) // width == iota(wide.shape, 0), wide, 0.0)
    spread = jnp.where(
        iota((lanes, lanes), 0) % width == iota((lanes, lanes), 1) % width, 1.0, 0.0
    ).astype(F32)
    moved = dot(wide.reshape(n * n, lanes), spread).reshape(n, n, lanes)
    moved = jnp.where(iota(moved.shape, 2) // width == iota(moved.shape, 1), moved, 0.0)
    return jnp.sum(moved, axis=1)


def mid_last(
    flags,
    places,
    v_ref,
    y_even,
    y_odd,
    f_ref,
    d_ref,
    w_ref,
    mid_out,
    src_out,
    slot_out,
    s_ref,
    p_ref,
):
    nx, ny, nz = f_ref.shape
    total = mid_neighbours(flags, v_ref, y_even, y_odd, w_ref, s_ref, 1)
    left = []
    for x in range(nx):
        mid_out[x] = v_ref[x + 1]
        left.append(f_ref[x] - d_ref[x] * v_ref[x + 1] + total(x))
    for i in range(nx // 2):
        p_ref[i * ny : (i + 1) * ny, :] = left[2 * i] + left[2 * i + 1]
    rows = dot(pair_sum_left(nx // 2 * ny), p_ref[...])
    source = dot(rows, pair_sum_right(nz, HALVING))
    src_out[...] = source
    blocked = swap_blocks(source)
    slot_out[...] = jnp.zeros(slot_out.shape, F32)
    for k in range(blocked.shape[0]):
        slot_out[pl.ds(places[k], 1), :] = blocked[k : k + 1]


def solve_blocks(m_ref, a_ref, out_ref):
    slots, cells = a_ref.shape
    lane = iota((cells, cells), 1)
    columns = jnp.zeros((cells, cells), F32)
    for q in range(slots):
        product = jnp.sum(m_ref[q] * a_ref[q : q + 1, :], axis=1, keepdims=True)
        columns = jnp.where(lane == q, product, columns)
    out_ref[...] = columns.T[0:slots]


def finish(places, back_ref, src_ref, dc_ref, wc_ref, cor_out, res_out, c_ref):
    blocks, cells = c_ref.shape
    nx, half = cor_out.shape[:2]
    rows = nx * half
    for k in range(blocks):
        c_ref[k : k + 1, :] = back_ref[pl.ds(places[k], 1), :]
    correction = swap_blocks(c_ref[...])
    source = src_ref[...]
    grid_row = iota(source.shape, 0)
    width = cells // blocks
    zpos = iota(source.shape, 1) % width
    residual = source - dc_ref[...] * correction
    for o, (a, b, c) in enumerate(OFFSETS):
        moved = correction
        if c:
            moved = pltpu.roll(moved, (-c) % cells, 1)
            moved = jnp.where(zpos == (0 if c < 0 else width - 1), 0.0, moved)
        if a or b:
            moved = pltpu.roll(moved, (-(a * half + b)) % rows, 0)
            y, x = grid_row % half + b, grid_row // half + a
            ok = (y >= 0) & (y < half) & (x >= 0) & (x < nx)
            moved = jnp.where(ok, moved, 0.0)
        residual = residual + wc_ref[o].astype(F32) * moved
    for x in range(nx):
        cor_out[x] = correction[x * half : (x + 1) * half]
        res_out[x] = residual[x * half : (x + 1) * half]


def block_ranks(owners):
    same = owners[:, None] == owners[None, :]
    count = owners.shape[0]
    earlier = jnp.arange(count)[None, :] < jnp.arange(count)[:, None]
    return jnp.sum((same & earlier).astype(jnp.int32), axis=-1)


def call(body, outs, ins=None, **more):
    flops = more.pop("flops", 1_000_000)
    size = more.pop("size", 1_000_000)
    limit = more.pop("limit", VMEM_LIMIT)
    return pl.pallas_call(
        body,
        out_shape=outs,
        cost_estimate=pl.CostEstimate(flops=flops, bytes_accessed=size, transcendentals=0),
        compiler_params=pltpu.CompilerParams(vmem_limit_bytes=limit),
        **more,
    )


def pairs(axis):
    size = lax.axis_size(axis)
    even = [(i, i ^ 1) for i in range(size)]
    odd = [(i, (i + 1) % size if i % 2 else (i - 1) % size) for i in range(size)]
    return even, odd


def exchange(axis, to_even, to_odd):
    even, odd = pairs(axis)
    return lax.ppermute(to_even, axis, even), lax.ppermute(to_odd, axis, odd)


def shards(
    rhs_fine,
    diag_fine,
    coup_fine,
    diag_mid,
    coup_mid,
    diag_coarse,
    coup_coarse,
    owner_map,
    inverse_blocks,
):
    nx, ny, nz = rhs_fine.shape
    g, d = lax.axis_index("group"), lax.axis_index("dev")
    n_group, n_dev = lax.axis_size("group"), lax.axis_size("dev")
    flags = jnp.stack([g > 0, g < n_group - 1, d > 0, d < n_dev - 1, g % 2 > 0, d % 2 > 0])
    slots, cells = inverse_blocks.shape[2], inverse_blocks.shape[3]
    owners = owner_map.reshape(-1)
    places = owners * (slots // n_dev) + block_ranks(owners)
    flags = lax.optimization_barrier(flags.astype(jnp.int32))

    def on(place):
        return flags[place] > 0

    def by_parity(parity, lo, hi):
        return jnp.where(on(parity), lo, hi), jnp.where(on(parity), hi, lo)

    scratch = [pltpu.VMEM((9, nx + 2, ny, nz), F32)]
    fine = sds((nx, ny, nz))
    faces = sds((4, ny, nz))
    heavy = dict(flops=60 * nx * ny * nz, size=coup_fine.size * 2 + 4 * rhs_fine.size * 4)
    one_face = sds((ny, nz))

    def stage(values_lo, values_hi, ends):
        lo_halo, hi_halo = jnp.where(on(X_ODD), *ends), jnp.where(on(X_ODD), *ends[::-1])
        lo_halo = jnp.where(on(X_LO), lo_halo, 0.0)
        hi_halo = jnp.where(on(X_HI), hi_halo, 0.0)
        to_lo = jnp.concatenate([lo_halo[:1], values_lo, hi_halo[:1]], axis=0)
        to_hi = jnp.concatenate([lo_halo[-1:], values_hi, hi_halo[-1:]], axis=0)
        return by_parity(Y_ODD, to_lo, to_hi)

    hx, hy, hz = nx // 2, ny // 2, nz // 2

    start, q, x_even, x_odd, *new = call(
        fine_start,
        (fine, fine) + (one_face,) * 4,
        in_specs=[SMEM] + [VMEM] * 2,
        out_specs=(VMEM,) * 6,
        flops=LONG,
    )(flags, rhs_fine, diag_fine)
    ends = exchange("group", x_even, x_odd)
    v, v_faces, q_faces, w_faces = call(
        fine_first,
        (fine, faces, faces, sds((4, 9, ny, nz), coup_fine.dtype)),
        in_specs=[VMEM] * 3,
        out_specs=(VMEM,) * 4,
        scratch_shapes=scratch + [pltpu.VMEM((2, 9, nx, nz), F32)],
        **heavy,
    )(start, q, coup_fine)
    ends, new, v_faces = lax.optimization_barrier((ends, new, v_faces))
    messages = stage(new[0], new[1], ends)
    messages, early_d = lax.optimization_barrier((messages, diag_mid))
    halo = ends + exchange("dev", *messages)
    slabs = sds((52 + WIDE, hy, hz))
    wx = call(
        mid_pack, (slabs, slabs), in_specs=[SMEM] + [VMEM] * 2, out_specs=(VMEM,) * 2
    )(flags, coup_mid, early_d)
    wx = exchange("group", *wx)
    halo, wx = lax.optimization_barrier((halo, wx))
    fix = call(
        fine_halo,
        (one_face,) * 6,
        in_specs=[SMEM] + [VMEM] * 7,
        out_specs=(VMEM,) * 6,
    )
    *new, x_even, x_odd = fix(flags, *halo, w_faces, v_faces, q_faces)

    ends = exchange("group", x_even, x_odd)
    v, v_faces = call(
        fine_next,
        (fine, faces),
        in_specs=[VMEM] * 8,
        out_specs=(VMEM,) * 2,
        scratch_shapes=scratch,
        **heavy,
    )(v, *new, start, q, coup_fine)
    ends, v_faces, new = lax.optimization_barrier((ends, v_faces, new))
    messages = stage(new[2], new[3], ends)
    messages, wx = lax.optimization_barrier((messages, wx))
    halo = ends + exchange("dev", *messages)
    w_wide, q_wide = call(
        mid_assemble,
        (sds((26, hx + 4, hy, hz), coup_mid.dtype), sds((hx + 2 * WIDE, hy, hz))),
        in_specs=[SMEM] + [VMEM] * 4,
        out_specs=(VMEM,) * 2,
    )(flags, coup_mid, diag_mid, *wx)
    halo, q_wide = lax.optimization_barrier((halo, q_wide))
    *new, x_even, x_odd = fix(flags, *halo, w_faces, v_faces, q_faces)

    ends = exchange("group", x_even, x_odd)
    fine_iterate, g_mid = call(
        fine_last,
        (fine, sds((hx, hy, hz))),
        in_specs=[VMEM] * 8,
        out_specs=(VMEM,) * 2,
        scratch_shapes=scratch + [pltpu.VMEM((hx * ny, nz), F32)],
        **heavy,
    )(v, *new, start, q, coup_fine)
    ends, g_mid, new = lax.optimization_barrier((ends, g_mid, new))
    halo = ends + exchange("dev", *stage(new[2], new[3], ends))
    f_mid, fx_even, fx_odd = call(
        fine_halo_last,
        (sds((hx, hy, hz)), sds((WIDE, hy, hz)), sds((WIDE, hy, hz))),
        in_specs=[SMEM] + [VMEM] * 6,
        out_specs=(VMEM,) * 3,
        scratch_shapes=[pltpu.VMEM((4 * ny, nz), F32)],
    )(flags, *halo, w_faces, g_mid)

    ex = hx + 2 * WIDE
    fx = exchange("group", fx_even, fx_odd)
    wide = sds((ex, hy, hz))
    mid_scratch = [pltpu.VMEM((9, ex, hy, hz), F32)]
    start_wide, *halo = call(
        mid_start,
        (wide, sds((ex, hz)), sds((ex, hz))),
        in_specs=[SMEM] + [VMEM] * 4,
        out_specs=(VMEM,) * 3,
    )(flags, f_mid, *fx, q_wide)
    v_mid = start_wide
    for reach in (WIDE, WIDE - 1):
        halo = exchange("dev", *halo)
        count = hx + 2 * reach - 2
        v_mid, *halo = call(
            functools.partial(mid_next, reach),
            (sds((count, hy, hz)), sds((count, hz)), sds((count, hz))),
            in_specs=[SMEM] + [VMEM] * 6,
            out_specs=(VMEM,) * 3,
            scratch_shapes=mid_scratch,
        )(flags, v_mid, *halo, start_wide, q_wide, w_wide)
    halo = exchange("dev", *halo)
    qx, qy, qz = hx // 2, hy // 2, hz // 2
    mid_iterate, source, outgoing = call(
        mid_last,
        (sds((hx, hy, hz)), sds((qx * qy, qz)), sds((slots, cells))),
        in_specs=[SMEM] * 2 + [VMEM] * 6,
        out_specs=(VMEM,) * 3,
        scratch_shapes=mid_scratch + [pltpu.VMEM((qx * hy, hz), F32)],
    )(flags, places, v_mid, *halo, f_mid, diag_mid, w_wide)

    arrived = lax.all_to_all(outgoing, "dev", split_axis=0, concat_axis=0, tiled=True)
    owned = call(solve_blocks, sds((slots, cells)), in_specs=[VMEM] * 2, out_specs=VMEM)(
        inverse_blocks.reshape(slots, cells, cells), arrived
    )
    returned = lax.all_to_all(owned, "dev", split_axis=0, concat_axis=0, tiled=True)
    correction, residual = call(
        finish,
        (sds((qx, qy, qz)), sds((qx, qy, qz))),
        in_specs=[SMEM] + [VMEM] * 4,
        out_specs=(VMEM,) * 2,
        scratch_shapes=[pltpu.VMEM((owners.shape[0], cells), F32)],
    )(
        places,
        returned,
        source,
        diag_coarse.reshape(qx * qy, qz),
        coup_coarse.reshape(26, qx * qy, qz),
    )
    return fine_iterate, mid_iterate, correction, residual


def solution(mesh):
    return jax.shard_map(
        shards,
        mesh=mesh,
        in_specs=(
            P("group", "dev", None),
            P("group", "dev", None),
            P(None, "group", "dev", None),
            P("group", "dev", None),
            P(None, "group", "dev", None),
            P("group", "dev", None),
            P(None, "group", "dev", None),
            P("group", "dev", None, None),
            P("group", "dev", None, None, None),
        ),
        out_specs=(
            P("group", "dev", None),
            P("group", "dev", None),
            P("group", "dev", None),
            P("group", "dev", None),
        ),
        check_vma=False,
    )
```

time: 219 us -> 113 us (0.52)
  the two profiles are of different devices: /device:TPU:128 before, /device:TPU:2 now
where the time goes in v1:
time: 113 us
  starting transfers between devices  30.8 us (27%)
  waiting for transfers between devices  25.8 us (23%)
  blocking collectives  25.8 us (23%)
  Pallas kernels  23.1 us (20%)
  between operations  3.61 us (3%)
  local copies, waits for them, and re-layouts  3.22 us (3%)
    ppermute x22, starting transfers between devices, exchange(): return (lax.ppermute(to_even, axis, even), lax.ppermute(to_odd, axis, odd))  30.8 us
    ppermute x22, waiting for transfers between devices, exchange(): return (lax.ppermute(to_even, axis, even), lax.ppermute(to_odd, axis, odd))  25.8 us
    all_to_all x1, blocking collectives, shards(): lax.all_to_all(outgoing, 'dev', split_axis=0, concat_axis=0, tiled=True)  15.3 us
    all_to_all x1, blocking collectives, shards(): lax.all_to_all(owned, 'dev', split_axis=0, concat_axis=0, tiled=True)  10.6 us
    pallas_call x1, Pallas kernels, shards(): call(fine_last, (fine, sds((hx, hy, hz))), in_specs=[VMEM] * 8, out_specs...  4.14 us
    pallas_call x1, Pallas kernels, shards(): call(fine_first, (fine, faces, faces, sds((4, 9, ny, nz), coup_fine.dtype...  3.78 us
    pallas_call x1, Pallas kernels, shards(): call(fine_next, (fine, faces), in_specs=[VMEM] * 8, out_specs=(VMEM,) * 2...  3.44 us
    unnamed x20, local copies, waits for them, and re-layouts  2.49 us
  transfers between devices with their start and end apart: 22, of which 15 were waited for; matrix products, arithmetic and copies ran while one was open for 1% of the time, Pallas kernels for 11%

profile of v1, /device:TPU:2, one launch (start us, length us, event | category | flops | bytes accessed | tf_op | source)
XLA Modules:
  0.0 112.7 jit_solution(16240468923831731844)
XLA Ops:
  0.8 1.2 %copy-done.5 = f32[16,16,512]{2,1,0:T(8,128)S(1)} copy-done((f32[16,16,512]{2,1,0:T(8,128)S(1)}, f32[16,16,512]{2,1,0:T(8,128)}, u32[]{:S(2)}) %copy-start.5) | copy-done | bytes 524312
  2.0 1.3 %copy-done.6 = f32[16,16,512]{2,1,0:T(8,128)S(1)} copy-done((f32[16,16,512]{2,1,0:T(8,128)S(1)}, f32[16,16,512]{2,1,0:T(8,128)}, u32[]{:S(2)}) %copy-start.6) | copy-done | bytes 524312
  3.2 0.8 shard_map.120
  4.1 6.0 %collective-permute-start.1 = (f32[16,512]{1,0:T(8,128)S(1)}, f32[16,512]{1,0:T(8,128)S(1)}, u32[]{:S(2)}, u32[]{:S(2)}) collective-permute-start(f32[16,512]{1,0:T(8,128)S(1)} %get-tuple-element.88), channel_id=1, source_target_pairs={{0,240},{16,32},{32,16},{48,64},{64,48},{80,96},{96,80},{112,128},... | collective-permute-start | bytes 98312 | tf_op jit(solution)/shard_map/ppermute | solution.py:505
  10.1 0.6 fusion.13
  13.3 3.8 %shard_map.121 = (f32[16,16,512]{2,1,0:T(8,128)S(1)}, f32[4,16,512]{2,1,0:T(8,128)S(1)}, f32[4,16,512]{2,1,0:T(8,128)S(1)}, bf16[4,9,16,512]{3,2,1,0:T(8,128)(2,1)S(1)}) custom-call(f32[16,16,512]{2,1,0:T(8,128)S(1)} %get-tuple-element.84.start_ref, f32[16,16,512]{2,1,0:T(8,128)S(1)} %get-tuple-element.85.q_ref, bf16[26,16,16,512]{3,2,1,0:T(8,128)(2,1)S(1)} %bitcast.20), custom_call_target="tpu_custom_call" | custom-call | flops 7864320 | bytes 8912896 | tf_op jit(solution)/shard_map/pallas_call | solution.py:558
  17.2 0.7 shard_map.122
  18.0 1.1 collective-permute-start.5
  19.1 0.5 collective-permute-start.2
  19.7 2.2 %collective-permute-start.3 = (f32[18,512]{1,0:T(8,128)S(1)}, f32[18,512]{1,0:T(8,128)S(1)}, u32[]{:S(2)}, u32[]{:S(2)}) collective-permute-start(f32[18,512]{1,0:T(8,128)S(1)} %get-tuple-element.97), channel_id=1, source_target_pairs={{0,15},{1,2},{2,1},{3,4},{4,3},{5,6},{6,5},{7,8},{8,7},{9,10},{10,... | collective-permute-start | bytes 110600 | tf_op jit(solution)/shard_map/ppermute | solution.py:505
  21.8 1.4 %collective-permute-done.2.y_even = f32[18,512]{1,0:T(8,128)S(1)} collective-permute-done((f32[18,512]{1,0:T(8,128)S(1)}, f32[18,512]{1,0:T(8,128)S(1)}, u32[]{:S(2)}, u32[]{:S(2)}) %collective-permute-start.2) | collective-permute-done | bytes 36896 | tf_op jit(solution)/shard_map/ppermute | solution.py:505
  23.2 0.7 collective-permute-done.3.y_odd
  23.9 3.2 %collective-permute-done.5.x_odd = f32[55,8,256]{2,1,0:T(8,128)S(1)} collective-permute-done((f32[55,8,256]{2,1,0:T(8,128)S(1)}, f32[55,8,256]{2,1,0:T(8,128)S(1)}, u32[]{:S(2)}, u32[]{:S(2)}) %collective-permute-start.5) | collective-permute-done | bytes 450592 | tf_op jit(solution)/shard_map/ppermute | solution.py:505
  27.2 0.8 shard_map.123
  28.1 1.1 collective-permute-start.7
  29.2 3.4 %shard_map.124 = (f32[16,16,512]{2,1,0:T(8,128)S(1)}, f32[4,16,512]{2,1,0:T(8,128)S(1)}) custom-call(f32[16,16,512]{2,1,0:T(8,128)S(1)} %get-tuple-element.86.v_ref, f32[16,512]{1,0:T(8,128)S(1)} %get-tuple-element.108.xlo, f32[16,512]{1,0:T(8,128)S(1)} %get-tuple-element.109.xhi, f32[16,512]{1,0:T(8,128)S(1)} %get-tuple-element.118.ylo, ...), custom_call_target="tpu_custom_call" | custom-call | flops 7864320 | bytes 8912896 | tf_op jit(solution)/shard_map/pallas_call | solution.py:585
  32.8 1.9 %collective-permute-start.8 = (f32[18,512]{1,0:T(8,128)S(1)}, f32[18,512]{1,0:T(8,128)S(1)}, u32[]{:S(2)}, u32[]{:S(2)}) collective-permute-start(f32[18,512]{1,0:T(8,128)S(1)} %get-tuple-element.122), channel_id=1, source_target_pairs={{0,1},{1,0},{2,3},{3,2},{4,5},{5,4},{6,7},{7,6},{8,9},{9,8},{10,11... | collective-permute-start | bytes 110600 | tf_op jit(solution)/shard_map/ppermute | solution.py:505
  34.7 0.9 collective-permute-start.9
  35.6 0.8 shard_map.125
  36.3 0.6 collective-permute-done.8.y_even
  37.0 1.8 %collective-permute-done.9.y_odd = f32[18,512]{1,0:T(8,128)S(1)} collective-permute-done((f32[18,512]{1,0:T(8,128)S(1)}, f32[18,512]{1,0:T(8,128)S(1)}, u32[]{:S(2)}, u32[]{:S(2)}) %collective-permute-start.9) | collective-permute-done | bytes 36896 | tf_op jit(solution)/shard_map/ppermute | solution.py:505
  38.8 0.8 shard_map.126
  39.7 1.1 collective-permute-start.11
  40.8 4.1 %shard_map.127 = (f32[16,16,512]{2,1,0:T(8,128)}, f32[8,8,256]{2,1,0:T(8,128)S(1)}) custom-call(f32[16,16,512]{2,1,0:T(8,128)S(1)} %get-tuple-element.112.v_ref, f32[16,512]{1,0:T(8,128)S(1)} %get-tuple-element.132.xlo, f32[16,512]{1,0:T(8,128)S(1)} %get-tuple-element.133.xhi, f32[16,512]{1,0:T(8,128)S(1)} %get-tuple-element.142.ylo, ...), custom_call_target="tpu_custom_call" | custom-call | flops 7864320 | bytes 8912896 | tf_op jit(solution)/shard_map/pallas_call | solution.py:607
  45.1 3.1 %collective-permute-start.12 = (f32[18,512]{1,0:T(8,128)S(1)}, f32[18,512]{1,0:T(8,128)S(1)}, u32[]{:S(2)}, u32[]{:S(2)}) collective-permute-start(f32[18,512]{1,0:T(8,128)S(1)} %get-tuple-element.165), channel_id=1, source_target_pairs={{0,1},{1,0},{2,3},{3,2},{4,5},{5,4},{6,7},{7,6},{8,9},{9,8},{10,11... | collective-permute-start | bytes 110600 | tf_op jit(solution)/shard_map/ppermute | solution.py:505
  48.4 2.3 %collective-permute-done.12.y_even = f32[18,512]{1,0:T(8,128)S(1)} collective-permute-done((f32[18,512]{1,0:T(8,128)S(1)}, f32[18,512]{1,0:T(8,128)S(1)}, u32[]{:S(2)}, u32[]{:S(2)}) %collective-permute-start.12) | collective-permute-done | bytes 36896 | tf_op jit(solution)/shard_map/ppermute | solution.py:505
  50.6 1.6 %collective-permute-done.13.y_odd = f32[18,512]{1,0:T(8,128)S(1)} collective-permute-done((f32[18,512]{1,0:T(8,128)S(1)}, f32[18,512]{1,0:T(8,128)S(1)}, u32[]{:S(2)}, u32[]{:S(2)}) %collective-permute-start.13) | collective-permute-done | bytes 36896 | tf_op jit(solution)/shard_map/ppermute | solution.py:505
  52.2 1.4 %shard_map.128 = (f32[8,8,256]{2,1,0:T(8,128)S(1)}, f32[3,8,256]{2,1,0:T(8,128)S(1)}, f32[3,8,256]{2,1,0:T(8,128)S(1)}) custom-call(s32[6]{0:T(128)S(1)} %convert_element_type.6.flags, f32[16,512]{1,0:T(8,128)S(1)} %collective-permute-done.10.x_even, f32[16,512]{1,0:T(8,128)S(1)} %collective-permute-done.11.x_odd, ...), custom_call_target="tpu_custom_call" | custom-call | flops 1000000 | bytes 1000000 | tf_op jit(solution)/shard_map/pallas_call | solution.py:617
  53.6 0.3 collective-permute-start.14
  53.9 1.5 %collective-permute-start.15 = (f32[3,8,256]{2,1,0:T(8,128)S(1)}, f32[3,8,256]{2,1,0:T(8,128)S(1)}, u32[]{:S(2)}, u32[]{:S(2)}) collective-permute-start(f32[3,8,256]{2,1,0:T(8,128)S(1)} %get-tuple-element.147), channel_id=1, source_target_pairs={{0,240},{16,32},{32,16},{48,64},{64,48},{80,96},{96,80},{112,128},... | collective-permute-start | bytes 73736 | tf_op jit(solution)/shard_map/ppermute | solution.py:505
  55.4 3.1 %collective-permute-done.15.o_ref = f32[3,8,256]{2,1,0:T(8,128)S(1)} collective-permute-done((f32[3,8,256]{2,1,0:T(8,128)S(1)}, f32[3,8,256]{2,1,0:T(8,128)S(1)}, u32[]{:S(2)}, u32[]{:S(2)}) %collective-permute-start.15) | collective-permute-done | bytes 24608 | tf_op jit(solution)/shard_map/ppermute | solution.py:505
  58.4 0.6 shard_map.129
  59.0 3.7 %collective-permute-start.16 = (f32[14,256]{1,0:T(8,128)S(1)}, f32[14,256]{1,0:T(8,128)S(1)}, u32[]{:S(2)}, u32[]{:S(2)}) collective-permute-start(f32[14,256]{1,0:T(8,128)S(1)} %get-tuple-element.150), channel_id=1, source_target_pairs={{0,1},{1,0},{2,3},{3,2},{4,5},{5,4},{6,7},{7,6},{8,9},{9,8},{10,11... | collective-permute-start | bytes 43016 | tf_op jit(solution)/shard_map/ppermute | solution.py:505
  62.7 1.7 %collective-permute-done.16.y_even = f32[14,256]{1,0:T(8,128)S(1)} collective-permute-done((f32[14,256]{1,0:T(8,128)S(1)}, f32[14,256]{1,0:T(8,128)S(1)}, u32[]{:S(2)}, u32[]{:S(2)}) %collective-permute-start.16) | collective-permute-done | bytes 14368 | tf_op jit(solution)/shard_map/ppermute | solution.py:505
  64.4 2.0 %collective-permute-done.17.y_odd = f32[14,256]{1,0:T(8,128)S(1)} collective-permute-done((f32[14,256]{1,0:T(8,128)S(1)}, f32[14,256]{1,0:T(8,128)S(1)}, u32[]{:S(2)}, u32[]{:S(2)}) %collective-permute-start.17) | collective-permute-done | bytes 14368 | tf_op jit(solution)/shard_map/ppermute | solution.py:505
  66.4 0.9 shard_map.130
  67.4 3.5 %collective-permute-start.18 = (f32[12,256]{1,0:T(8,128)S(1)}, f32[12,256]{1,0:T(8,128)S(1)}, u32[]{:S(2)}, u32[]{:S(2)}) collective-permute-start(f32[12,256]{1,0:T(8,128)S(1)} %get-tuple-element.154), channel_id=1, source_target_pairs={{0,1},{1,0},{2,3},{3,2},{4,5},{5,4},{6,7},{7,6},{8,9},{9,8},{10,11... | collective-permute-start | bytes 36872 | tf_op jit(solution)/shard_map/ppermute | solution.py:505
  71.1 1.5 %collective-permute-done.18.y_even = f32[12,256]{1,0:T(8,128)S(1)} collective-permute-done((f32[12,256]{1,0:T(8,128)S(1)}, f32[12,256]{1,0:T(8,128)S(1)}, u32[]{:S(2)}, u32[]{:S(2)}) %collective-permute-start.18) | collective-permute-done | bytes 12320 | tf_op jit(solution)/shard_map/ppermute | solution.py:505
  72.6 2.0 %collective-permute-done.19.y_odd = f32[12,256]{1,0:T(8,128)S(1)} collective-permute-done((f32[12,256]{1,0:T(8,128)S(1)}, f32[12,256]{1,0:T(8,128)S(1)}, u32[]{:S(2)}, u32[]{:S(2)}) %collective-permute-start.19) | collective-permute-done | bytes 12320 | tf_op jit(solution)/shard_map/ppermute | solution.py:505
  74.6 0.9 shard_map.131
  75.5 3.5 %collective-permute-start.20 = (f32[10,256]{1,0:T(8,128)S(1)}, f32[10,256]{1,0:T(8,128)S(1)}, u32[]{:S(2)}, u32[]{:S(2)}) collective-permute-start(f32[10,256]{1,0:T(8,128)S(1)} %get-tuple-element.157), channel_id=1, source_target_pairs={{0,1},{1,0},{2,3},{3,2},{4,5},{5,4},{6,7},{7,6},{8,9},{9,8},{10,11... | collective-permute-start | bytes 30728 | tf_op jit(solution)/shard_map/ppermute | solution.py:505
  79.0 1.7 %collective-permute-done.20.y_even = f32[10,256]{1,0:T(8,128)S(1)} collective-permute-done((f32[10,256]{1,0:T(8,128)S(1)}, f32[10,256]{1,0:T(8,128)S(1)}, u32[]{:S(2)}, u32[]{:S(2)}) %collective-permute-start.20) | collective-permute-done | bytes 10272 | tf_op jit(solution)/shard_map/ppermute | solution.py:505
  80.8 2.0 %collective-permute-done.21.y_odd = f32[10,256]{1,0:T(8,128)S(1)} collective-permute-done((f32[10,256]{1,0:T(8,128)S(1)}, f32[10,256]{1,0:T(8,128)S(1)}, u32[]{:S(2)}, u32[]{:S(2)}) %collective-permute-start.21) | collective-permute-done | bytes 10272 | tf_op jit(solution)/shard_map/ppermute | solution.py:505
  82.8 1.9 %shard_map.132 = (f32[8,8,256]{2,1,0:T(8,128)}, f32[16,128]{1,0:T(8,128)S(1)}, f32[32,128]{1,0:T(8,128)S(1)}) custom-call(s32[6]{0:T(128)S(1)} %convert_element_type.6.flags, s32[16]{0:T(128)S(1)} %multiply_add_fusion.places, f32[10,8,256]{2,1,0:T(8,128)S(1)} %get-tuple-element.156.v_ref, f32[10,256]{1,0:T(8,128)S(1)} %collective-permute-done.20.y_even, ...), custom_call_target="tpu_custom_call" | custom-call | flops 1000000 | bytes 1000000 | tf_op jit(solution)/shard_map/pallas_call | solution.py:648
  84.7 15.3 %all_to_all.22 = f32[16,2,128]{2,1,0:T(2,128)S(1)} all-to-all(f32[16,2,128]{2,1,0:T(2,128)S(1)} %bitcast.26), channel_id=1, replica_groups=mesh['group'=16,'dev'=16] {'dev'}, dimensions={0} | all-to-all | bytes 32768 | tf_op jit(solution)/shard_map/all_to_all | solution.py:656
  99.9 0.7 shard_map.133
  100.6 10.6 %all_to_all.23 = f32[16,2,128]{2,1,0:T(2,128)S(1)} all-to-all(f32[16,2,128]{2,1,0:T(2,128)S(1)} %bitcast.24), channel_id=1, replica_groups=mesh['group'=16,'dev'=16] {'dev'}, dimensions={0} | all-to-all | bytes 32768 | tf_op jit(solution)/shard_map/all_to_all | solution.py:660
  111.2 1.5 %shard_map.134 = (f32[4,4,128]{2,1,0:T(4,128)}, f32[4,4,128]{2,1,0:T(4,128)}) custom-call(s32[16]{0:T(128)S(1)} %multiply_add_fusion.places, f32[32,128]{1,0:T(8,128)S(1)} %bitcast.25, f32[16,128]{1,0:T(8,128)S(1)} %get-tuple-element.161.src_ref, f32[16,128]{1,0:T(8,128)S(1)} %bitcast.27, bf16[26,16,128]{2,1,0:T(8,128)(2,1)S(1)} %bitcast.22), custom_call_target="tpu_custom_call" | custom-call | flops 1000000 | bytes 1000000 | tf_op jit(solution)/shard_map/pallas_call | solution.py:661
  (50 shorter events, 1.2 us)
Async XLA Ops:
  0.8 12.5 %slice-start = ((s8[6815744]{0:T(1024)(128)(4,1)}), s8[4194304]{0:T(1024)(128)(4,1)S(1)}, s32[]{:S(2)}) async-start(s8[6815744]{0:T(1024)(128)(4,1)} %bitcast.19), calls=%async_computation.2 | async-start | bytes 8388608
  0.8 1.2 %copy-start.5 = (f32[16,16,512]{2,1,0:T(8,128)S(1)}, f32[16,16,512]{2,1,0:T(8,128)}, u32[]{:S(2)}) copy-start(f32[16,16,512]{2,1,0:T(8,128)} %f_ref.1) | copy-start | bytes 1572868
  2.0 1.3 %copy-start.6 = (f32[16,16,512]{2,1,0:T(8,128)S(1)}, f32[16,16,512]{2,1,0:T(8,128)}, u32[]{:S(2)}) copy-start(f32[16,16,512]{2,1,0:T(8,128)} %d_ref.3) | copy-start | bytes 1572868
  3.2 10.0 %slice-start.1 = ((s8[6815744]{0:T(1024)(128)(4,1)}), s8[2621440]{0:T(1024)(128)(4,1)S(1)}, s32[]{:S(2)}) async-start(s8[6815744]{0:T(1024)(128)(4,1)} %bitcast.19), calls=%async_computation.3 | async-start | bytes 5242880
  4.0 13.1 %collective-permute-start = (f32[16,512]{1,0:T(8,128)S(1)}, f32[16,512]{1,0:T(8,128)S(1)}, u32[]{:S(2)}, u32[]{:S(2)}) collective-permute-start(f32[16,512]{1,0:T(8,128)S(1)} %get-tuple-element.87), channel_id=1, source_target_pairs={{0,16},{16,0},{32,48},{48,32},{64,80},{80,64},{96,112},{112,96},{1... | collective-permute-start | bytes 98312 | tf_op jit(solution)/shard_map/ppermute | solution.py:505
  4.1 13.0 %collective-permute-start.1 = (f32[16,512]{1,0:T(8,128)S(1)}, f32[16,512]{1,0:T(8,128)S(1)}, u32[]{:S(2)}, u32[]{:S(2)}) collective-permute-start(f32[16,512]{1,0:T(8,128)S(1)} %get-tuple-element.88), channel_id=1, source_target_pairs={{0,240},{16,32},{32,16},{48,64},{64,48},{80,96},{96,80},{112,128},... | collective-permute-start | bytes 98312 | tf_op jit(solution)/shard_map/ppermute | solution.py:505
  13.3 3.9 %copy-start = (bf16[26,8,8,256]{3,2,1,0:T(8,128)(2,1)S(1)}, bf16[26,8,8,256]{3,2,1,0:T(8,128)(2,1)}, u32[]{:S(2)}) copy-start(bf16[26,8,8,256]{3,2,1,0:T(8,128)(2,1)} %w_ref.8) | copy-start | bytes 2555908
  13.3 3.9 %copy-start.2 = (f32[8,8,256]{2,1,0:T(8,128)S(1)}, f32[8,8,256]{2,1,0:T(8,128)}, u32[]{:S(2)}) copy-start(f32[8,8,256]{2,1,0:T(8,128)} %d_ref.6) | copy-start | bytes 196612
  17.9 6.0 %collective-permute-start.4 = (f32[55,8,256]{2,1,0:T(8,128)S(1)}, f32[55,8,256]{2,1,0:T(8,128)S(1)}, u32[]{:S(2)}, u32[]{:S(2)}) collective-permute-start(f32[55,8,256]{2,1,0:T(8,128)S(1)} %get-tuple-element.99), channel_id=1, source_target_pairs={{0,16},{16,0},{32,48},{48,32},{64,80},{80,64},{96,112},{112,96},{1... | collective-permute-start | bytes 1351688 | tf_op jit(solution)/shard_map/ppermute | solution.py:505
  18.0 9.1 %collective-permute-start.5 = (f32[55,8,256]{2,1,0:T(8,128)S(1)}, f32[55,8,256]{2,1,0:T(8,128)S(1)}, u32[]{:S(2)}, u32[]{:S(2)}) collective-permute-start(f32[55,8,256]{2,1,0:T(8,128)S(1)} %get-tuple-element.100), channel_id=1, source_target_pairs={{0,240},{16,32},{32,16},{48,64},{64,48},{80,96},{96,80},{112,128},... | collective-permute-start | bytes 1351688 | tf_op jit(solution)/shard_map/ppermute | solution.py:505
  19.1 4.1 %collective-permute-start.2 = (f32[18,512]{1,0:T(8,128)S(1)}, f32[18,512]{1,0:T(8,128)S(1)}, u32[]{:S(2)}, u32[]{:S(2)}) collective-permute-start(f32[18,512]{1,0:T(8,128)S(1)} %get-tuple-element.96), channel_id=1, source_target_pairs={{0,1},{1,0},{2,3},{3,2},{4,5},{5,4},{6,7},{7,6},{8,9},{9,8},{10,11... | collective-permute-start | bytes 110600 | tf_op jit(solution)/shard_map/ppermute | solution.py:505
  19.7 4.2 %collective-permute-start.3 = (f32[18,512]{1,0:T(8,128)S(1)}, f32[18,512]{1,0:T(8,128)S(1)}, u32[]{:S(2)}, u32[]{:S(2)}) collective-permute-start(f32[18,512]{1,0:T(8,128)S(1)} %get-tuple-element.97), channel_id=1, source_target_pairs={{0,15},{1,2},{2,1},{3,4},{4,3},{5,6},{6,5},{7,8},{8,7},{9,10},{10,... | collective-permute-start | bytes 110600 | tf_op jit(solution)/shard_map/ppermute | solution.py:505
  28.0 4.7 %collective-permute-start.6 = (f32[16,512]{1,0:T(8,128)S(1)}, f32[16,512]{1,0:T(8,128)S(1)}, u32[]{:S(2)}, u32[]{:S(2)}) collective-permute-start(f32[16,512]{1,0:T(8,128)S(1)} %get-tuple-element.113), channel_id=1, source_target_pairs={{0,16},{16,0},{32,48},{48,32},{64,80},{80,64},{96,112},{112,96},{1... | collective-permute-start | bytes 98312 | tf_op jit(solution)/shard_map/ppermute | solution.py:505
  28.1 4.6 %collective-permute-start.7 = (f32[16,512]{1,0:T(8,128)S(1)}, f32[16,512]{1,0:T(8,128)S(1)}, u32[]{:S(2)}, u32[]{:S(2)}) collective-permute-start(f32[16,512]{1,0:T(8,128)S(1)} %get-tuple-element.114), channel_id=1, source_target_pairs={{0,240},{16,32},{32,16},{48,64},{64,48},{80,96},{96,80},{112,128},... | collective-permute-start | bytes 98312 | tf_op jit(solution)/shard_map/ppermute | solution.py:505
  32.8 4.2 %collective-permute-start.8 = (f32[18,512]{1,0:T(8,128)S(1)}, f32[18,512]{1,0:T(8,128)S(1)}, u32[]{:S(2)}, u32[]{:S(2)}) collective-permute-start(f32[18,512]{1,0:T(8,128)S(1)} %get-tuple-element.122), channel_id=1, source_target_pairs={{0,1},{1,0},{2,3},{3,2},{4,5},{5,4},{6,7},{7,6},{8,9},{9,8},{10,11... | collective-permute-start | bytes 110600 | tf_op jit(solution)/shard_map/ppermute | solution.py:505
  34.7 4.1 %collective-permute-start.9 = (f32[18,512]{1,0:T(8,128)S(1)}, f32[18,512]{1,0:T(8,128)S(1)}, u32[]{:S(2)}, u32[]{:S(2)}) collective-permute-start(f32[18,512]{1,0:T(8,128)S(1)} %get-tuple-element.123), channel_id=1, source_target_pairs={{0,15},{1,2},{2,1},{3,4},{4,3},{5,6},{6,5},{7,8},{8,7},{9,10},{10,... | collective-permute-start | bytes 110600 | tf_op jit(solution)/shard_map/ppermute | solution.py:505
  39.6 5.4 %collective-permute-start.10 = (f32[16,512]{1,0:T(8,128)S(1)}, f32[16,512]{1,0:T(8,128)S(1)}, u32[]{:S(2)}, u32[]{:S(2)}) collective-permute-start(f32[16,512]{1,0:T(8,128)S(1)} %get-tuple-element.137), channel_id=1, source_target_pairs={{0,16},{16,0},{32,48},{48,32},{64,80},{80,64},{96,112},{112,96},{1... | collective-permute-start | bytes 98312 | tf_op jit(solution)/shard_map/ppermute | solution.py:505
  39.7 5.3 %collective-permute-start.11 = (f32[16,512]{1,0:T(8,128)S(1)}, f32[16,512]{1,0:T(8,128)S(1)}, u32[]{:S(2)}, u32[]{:S(2)}) collective-permute-start(f32[16,512]{1,0:T(8,128)S(1)} %get-tuple-element.138), channel_id=1, source_target_pairs={{0,240},{16,32},{32,16},{48,64},{64,48},{80,96},{96,80},{112,128},... | collective-permute-start | bytes 98312 | tf_op jit(solution)/shard_map/ppermute | solution.py:505
  45.0 25.9 %copy-start.7 = (s32[1,1,16,1]{2,3,1,0:T(1,128)S(1)}, s32[1,1,16,1]{2,3,1,0:T(1,128)}, u32[]{:S(2)}) copy-start(s32[1,1,16,1]{2,3,1,0:T(1,128)} %param.16) | copy-start | bytes 196
  45.1 5.6 %collective-permute-start.12 = (f32[18,512]{1,0:T(8,128)S(1)}, f32[18,512]{1,0:T(8,128)S(1)}, u32[]{:S(2)}, u32[]{:S(2)}) collective-permute-start(f32[18,512]{1,0:T(8,128)S(1)} %get-tuple-element.165), channel_id=1, source_target_pairs={{0,1},{1,0},{2,3},{3,2},{4,5},{5,4},{6,7},{7,6},{8,9},{9,8},{10,11... | collective-permute-start | bytes 110600 | tf_op jit(solution)/shard_map/ppermute | solution.py:505
  48.1 4.1 %collective-permute-start.13 = (f32[18,512]{1,0:T(8,128)S(1)}, f32[18,512]{1,0:T(8,128)S(1)}, u32[]{:S(2)}, u32[]{:S(2)}) collective-permute-start(f32[18,512]{1,0:T(8,128)S(1)} %get-tuple-element.164), channel_id=1, source_target_pairs={{0,15},{1,2},{2,1},{3,4},{4,3},{5,6},{6,5},{7,8},{8,7},{9,10},{10,... | collective-permute-start | bytes 110600 | tf_op jit(solution)/shard_map/ppermute | solution.py:505
  53.6 1.8 %collective-permute-start.14 = (f32[3,8,256]{2,1,0:T(8,128)S(1)}, f32[3,8,256]{2,1,0:T(8,128)S(1)}, u32[]{:S(2)}, u32[]{:S(2)}) collective-permute-start(f32[3,8,256]{2,1,0:T(8,128)S(1)} %get-tuple-element.146), channel_id=1, source_target_pairs={{0,16},{16,0},{32,48},{48,32},{64,80},{80,64},{96,112},{112,96},{1... | collective-permute-start | bytes 73736 | tf_op jit(solution)/shard_map/ppermute | solution.py:505
  53.9 4.5 %collective-permute-start.15 = (f32[3,8,256]{2,1,0:T(8,128)S(1)}, f32[3,8,256]{2,1,0:T(8,128)S(1)}, u32[]{:S(2)}, u32[]{:S(2)}) collective-permute-start(f32[3,8,256]{2,1,0:T(8,128)S(1)} %get-tuple-element.147), channel_id=1, source_target_pairs={{0,240},{16,32},{32,16},{48,64},{64,48},{80,96},{96,80},{112,128},... | collective-permute-start | bytes 73736 | tf_op jit(solution)/shard_map/ppermute | solution.py:505
  59.0 5.4 %collective-permute-start.16 = (f32[14,256]{1,0:T(8,128)S(1)}, f32[14,256]{1,0:T(8,128)S(1)}, u32[]{:S(2)}, u32[]{:S(2)}) collective-permute-start(f32[14,256]{1,0:T(8,128)S(1)} %get-tuple-element.150), channel_id=1, source_target_pairs={{0,1},{1,0},{2,3},{3,2},{4,5},{5,4},{6,7},{7,6},{8,9},{9,8},{10,11... | collective-permute-start | bytes 43016 | tf_op jit(solution)/shard_map/ppermute | solution.py:505
  62.7 3.7 %collective-permute-start.17 = (f32[14,256]{1,0:T(8,128)S(1)}, f32[14,256]{1,0:T(8,128)S(1)}, u32[]{:S(2)}, u32[]{:S(2)}) collective-permute-start(f32[14,256]{1,0:T(8,128)S(1)} %get-tuple-element.151), channel_id=1, source_target_pairs={{0,15},{1,2},{2,1},{3,4},{4,3},{5,6},{6,5},{7,8},{8,7},{9,10},{10,... | collective-permute-start | bytes 43016 | tf_op jit(solution)/shard_map/ppermute | solution.py:505
  66.4 33.5 %copy-start.1 = (f32[1,1,32,128,128]{4,3,2,1,0:T(8,128)S(1)}, f32[1,1,32,128,128]{4,3,2,1,0:T(8,128)}, u32[]{:S(2)}) copy-start(f32[1,1,32,128,128]{4,3,2,1,0:T(8,128)} %param.17) | copy-start | bytes 6291460
  67.4 5.2 %collective-permute-start.18 = (f32[12,256]{1,0:T(8,128)S(1)}, f32[12,256]{1,0:T(8,128)S(1)}, u32[]{:S(2)}, u32[]{:S(2)}) collective-permute-start(f32[12,256]{1,0:T(8,128)S(1)} %get-tuple-element.154), channel_id=1, source_target_pairs={{0,1},{1,0},{2,3},{3,2},{4,5},{5,4},{6,7},{7,6},{8,9},{9,8},{10,11... | collective-permute-start | bytes 36872 | tf_op jit(solution)/shard_map/ppermute | solution.py:505
  70.9 3.7 %collective-permute-start.19 = (f32[12,256]{1,0:T(8,128)S(1)}, f32[12,256]{1,0:T(8,128)S(1)}, u32[]{:S(2)}, u32[]{:S(2)}) collective-permute-start(f32[12,256]{1,0:T(8,128)S(1)} %get-tuple-element.155), channel_id=1, source_target_pairs={{0,15},{1,2},{2,1},{3,4},{4,3},{5,6},{6,5},{7,8},{8,7},{9,10},{10,... | collective-permute-start | bytes 36872 | tf_op jit(solution)/shard_map/ppermute | solution.py:505
  75.5 35.7 %copy-start.3 = (bf16[26,4,4,128]{3,2,1,0:T(4,128)(2,1)S(1)}, bf16[26,4,4,128]{3,2,1,0:T(4,128)(2,1)}, u32[]{:S(2)}) copy-start(bf16[26,4,4,128]{3,2,1,0:T(4,128)(2,1)} %param.15) | copy-start | bytes 319492
  75.5 35.7 %copy-start.4 = (f32[4,4,128]{2,1,0:T(4,128)S(1)}, f32[4,4,128]{2,1,0:T(4,128)}, u32[]{:S(2)}) copy-start(f32[4,4,128]{2,1,0:T(4,128)} %param.14) | copy-start | bytes 24580
  75.5 5.2 %collective-permute-start.20 = (f32[10,256]{1,0:T(8,128)S(1)}, f32[10,256]{1,0:T(8,128)S(1)}, u32[]{:S(2)}, u32[]{:S(2)}) collective-permute-start(f32[10,256]{1,0:T(8,128)S(1)} %get-tuple-element.157), channel_id=1, source_target_pairs={{0,1},{1,0},{2,3},{3,2},{4,5},{5,4},{6,7},{7,6},{8,9},{9,8},{10,11... | collective-permute-start | bytes 30728 | tf_op jit(solution)/shard_map/ppermute | solution.py:505
  79.0 3.7 %collective-permute-start.21 = (f32[10,256]{1,0:T(8,128)S(1)}, f32[10,256]{1,0:T(8,128)S(1)}, u32[]{:S(2)}, u32[]{:S(2)}) collective-permute-start(f32[10,256]{1,0:T(8,128)S(1)} %get-tuple-element.158), channel_id=1, source_target_pairs={{0,15},{1,2},{2,1},{3,4},{4,3},{5,6},{6,5},{7,8},{8,7},{9,10},{10,... | collective-permute-start | bytes 30728 | tf_op jit(solution)/shard_map/ppermute | solution.py:505

commit v2 on v1

--- a/solution.py
+++ b/solution.py
@@ -1,5 +1,3 @@
-import functools
-
 import jax
 import jax.numpy as jnp
 from jax import lax
@@ -19,10 +17,10 @@
 TO_YLO = [OFFSETS.index((a, -1, c)) for a in (-1, 0, 1) for c in (-1, 0, 1)]
 TO_YHI = [OFFSETS.index((a, 1, c)) for a in (-1, 0, 1) for c in (-1, 0, 1)]
 F32 = jnp.float32
-HIGHEST = lax.Precision.HIGHEST
 VMEM_LIMIT = 20 * 1024 * 1024
 XB = 4
 WIDE = 3
+SLABS = 52 + WIDE
 X_LO, X_HI, Y_LO, Y_HI, X_ODD, Y_ODD = range(6)
 LONG = 30_000_000_000
 VMEM = pl.BlockSpec(memory_space=pltpu.VMEM)
@@ -61,8 +59,21 @@
     return jnp.where((iota((n // 2, n), 1) >> 1) == iota((n // 2, n), 0), 1.0, 0.0).astype(F32)
 
 
-def dot(a, b):
-    return jnp.dot(a, b, precision=HIGHEST, preferred_element_type=F32)
+def parts_of(v):
+    first = v.astype(jnp.bfloat16)
+    rest = v - first.astype(F32)
+    second = rest.astype(jnp.bfloat16)
+    return first, second, (rest - second.astype(F32)).astype(jnp.bfloat16)
+
+
+def dot_right(v, m):
+    m = m.astype(jnp.bfloat16)
+    return sum(jnp.dot(part, m, preferred_element_type=F32) for part in parts_of(v)[::-1])
+
+
+def dot_left(m, v):
+    m = m.astype(jnp.bfloat16)
+    return sum(jnp.dot(m, part, preferred_element_type=F32) for part in parts_of(v)[::-1])
 
 
 def put_versions(s_ref, x, layer):
@@ -125,7 +136,7 @@
             v_ref[x, :, at] = centre + start_ref[x, :, at] + q_ref[x, :, at] * total
 
 
-def fine_start(flags, f_ref, d_ref, start_ref, q_ref, x_even, x_odd, ylo, yhi):
+def fine_start(f_ref, d_ref, start_ref, q_ref, ylo, yhi):
     nx, ny = f_ref.shape[:2]
 
     @pl.loop(0, nx)
@@ -134,14 +145,13 @@
         q_ref[x] = q
         start_ref[x] = q * f_ref[x]
 
-    put_both(flags[X_ODD] > 0, x_even, x_odd, slice(None), start_ref[0], start_ref[nx - 1])
     for x in range(nx):
         ylo[x : x + 1, :] = start_ref[x, 0:1, :]
         yhi[x : x + 1, :] = start_ref[x, ny - 1 : ny, :]
 
 
 def fine_first(
-    start_ref, q_ref, w_ref, v_ref, faces_ref, qfaces_ref, wfaces_ref, s_ref, wy_ref
+    _, start_ref, q_ref, w_ref, v_ref, faces_ref, qfaces_ref, wfaces_ref, s_ref, wy_ref
 ):
     nx, ny = v_ref.shape[:2]
     zero_rims(s_ref)
@@ -205,8 +215,8 @@
                 row = pl.multiple_of((j * (XB // 2) + i // 2) * ny, ny)
                 p_ref[pl.ds(row, ny), at] = total[i] + total[i + 1]
 
-    rows = dot(pair_sum_left(nx // 2 * ny), p_ref[...])
-    g_ref[...] = dot(rows, pair_sum_right(nz, HALVING)).reshape(g_ref.shape)
+    rows = dot_left(pair_sum_left(nx // 2 * ny), p_ref[...])
+    g_ref[...] = dot_right(rows, pair_sum_right(nz, HALVING)).reshape(g_ref.shape)
 
 
 def sides(flags, even, odd, lo, hi, parity):
@@ -270,9 +280,9 @@
     n, nz = xs[0].shape
     for k, part in enumerate(xs + ys):
         t_ref[k * n : (k + 1) * n, :] = part
-    rows = dot(pair_sum_left(4 * n), t_ref[...])
+    rows = dot_left(pair_sum_left(4 * n), t_ref[...])
     half = n // 2
-    coarse = dot(rows, pair_sum_right(nz, HALVING))
+    coarse = dot_right(rows, pair_sum_right(nz, HALVING))
     row = iota((half, nz // 2), 0)
     for i in range(half):
         total = g_ref[i]
@@ -309,85 +319,81 @@
         put_both(at_odd, x_even, x_odd, 52 + k, d_ref[k], d_ref[nx - WIDE + k])
 
 
-def mid_assemble(flags, w_ref, d_ref, x_even, x_odd, w_out, q_out):
-    nx = d_ref.shape[0]
+def layer_beyond(flags, even, odd, index, below):
     at_odd = flags[X_ODD] > 0
-
-    def beyond(index, below):
-        first, second = (x_even, x_odd) if below else (x_odd, x_even)
-        return jnp.where(at_odd, first[index], second[index])
+    first, second = (even, odd) if below else (odd, even)
+    return jnp.where(at_odd, first[index], second[index])
+
+
+def mid_pack_y(flags, w_ref, d_ref, x_even, x_odd, to_even, to_odd):
+    nx, ny = d_ref.shape[:2]
+    at_odd = flags[Y_ODD] > 0
+
+    def put_row(place, r, lo, hi):
+        put_both(at_odd, to_even, to_odd, (place, slice(r, r + 1), slice(None)), lo, hi)
 
     @pl.loop(0, 26)
     def _(o):
         for x in range(nx):
-            w_out[o, x + 2] = w_ref[o, x]
+            layer = w_ref[o, x].astype(F32)
+            for k in range(2):
+                put_row(o * 2 + k, x, layer[k : k + 1], layer[ny - 2 + k : ny - 1 + k])
+
+    for k in range(WIDE):
+        for x in range(nx):
+            r = ny - WIDE + k
+            put_row(52 + k, x, d_ref[x, k : k + 1, :], d_ref[x, r : r + 1, :])
+
+    @pl.loop(0, 26)
+    def _(o):
+        for e in range(4):
+            layer = layer_beyond(flags, x_even, x_odd, o * 2 + e % 2, e < 2)
+            for k in range(2):
+                lo, hi = layer[k : k + 1], layer[ny - 2 + k : ny - 1 + k]
+                put_row(SLABS + o, k * 4 + e, lo, hi)
+
+    for e in range(2 * WIDE):
+        layer = layer_beyond(flags, x_even, x_odd, 52 + e % WIDE, e < WIDE)
+        for k in range(WIDE):
+            r = ny - WIDE + k
+            put_row(SLABS + 26 + k, e, layer[k : k + 1], layer[r : r + 1])
+
+
+def mid_assemble(flags, w_ref, d_ref, x_even, x_odd, y_even, y_odd, w_out, d_out, t_ref):
+    nx, ny, nz = d_ref.shape
+    at_odd = flags[Y_ODD] > 0
+    t_ref[...] = jnp.zeros(t_ref.shape, F32)
+
+    def put(o, x, layer, place, r):
+        t_ref[x + 2, 3 : 3 + ny, :] = layer
         for k in range(2):
-            w_out[o, k] = beyond(o * 2 + k, True).astype(w_out.dtype)
-            w_out[o, nx + 2 + k] = beyond(o * 2 + k, False).astype(w_out.dtype)
-
-    for x in range(nx):
-        q_out[x + WIDE] = OMEGA / d_ref[x]
-    for k in range(WIDE):
-        q_out[k] = OMEGA / beyond(52 + k, True)
-        q_out[nx + WIDE + k] = OMEGA / beyond(52 + k, False)
-
-
-def mid_start(flags, f_ref, e_ref, o_ref, q_ref, start_ref, y_even, y_odd):
-    nx, ny = f_ref.shape[:2]
-    x_odd, y_is_odd = flags[X_ODD] > 0, flags[Y_ODD] > 0
-    for r in range(nx + 2 * WIDE):
-        if r < WIDE:
-            f = jnp.where(x_odd, e_ref[r], o_ref[r])
-            f = jnp.where(flags[X_LO] > 0, f, 0.0)
-        elif r >= nx + WIDE:
-            k = r - nx - WIDE
-            f = jnp.where(x_odd, o_ref[k], e_ref[k])
-            f = jnp.where(flags[X_HI] > 0, f, 0.0)
+            index = (place(k), slice(r(k), r(k) + 1), slice(None))
+            even, odd = y_even[index], y_odd[index]
+            t_ref[x + 2, 1 + k : 2 + k, :] = jnp.where(at_odd, even, odd)
+            t_ref[x + 2, 3 + ny + k : 4 + ny + k, :] = jnp.where(at_odd, odd, even)
+        w_out[o, x + 2] = t_ref[x + 2].astype(w_out.dtype)
+
+    @pl.loop(0, 26)
+    def _(o):
+        for x in range(nx):
+            put(o, x, w_ref[o, x].astype(F32), lambda k: o * 2 + k, lambda k: x)
+        for e, x in enumerate((-2, -1, nx, nx + 1)):
+            layer = layer_beyond(flags, x_even, x_odd, o * 2 + e % 2, e < 2)
+            put(o, x, layer, lambda k: SLABS + o, lambda k: k * 4 + e)
+
+    d_out[...] = jnp.ones(d_out.shape, F32)
+    for x in range(-WIDE, nx + WIDE):
+        r = x + WIDE
+        if 0 <= x < nx:
+            layer, place, e = d_ref[x], 52, x
         else:
-            f = f_ref[r - WIDE]
-        start = q_ref[r] * f
-        start_ref[r] = start
-        index = (slice(r, r + 1), slice(None))
-        put_both(y_is_odd, y_even, y_odd, index, start[0:1], start[ny - 1 : ny])
-
-
-def mid_neighbours(flags, v_ref, y_even, y_odd, w_ref, s_ref, reach):
-    ny = v_ref.shape[1]
-    y_lo, y_hi = sides(flags, y_even[...], y_odd[...], Y_LO, Y_HI, Y_ODD)
-    row = iota(v_ref.shape[1:], 0)
-    for r in range(v_ref.shape[0]):
-        layer = v_ref[r]
-        below = jnp.where(row == 0, y_lo[r : r + 1], pltpu.roll(layer, 1, 0))
-        above = jnp.where(row == ny - 1, y_hi[r : r + 1], pltpu.roll(layer, ny - 1, 0))
-        for b, moved in enumerate((below, layer, above)):
-            for c in (-1, 0, 1):
-                s_ref[b * 3 + c + 1, r] = shift_z(moved, c)
-
-    def neighbours_of(x):
-        total = None
-        for o, (a, b, c) in enumerate(OFFSETS):
-            term = w_ref[o, x + 2].astype(F32) * s_ref[(b + 1) * 3 + c + 1, x + a + reach]
-            total = term if total is None else total + term
-        return total
-
-    return neighbours_of
-
-
-def mid_next(
-    reach, flags, v_ref, y_even, y_odd, start_ref, q_ref, w_ref, out_ref, to_even, to_odd, s_ref
-):
-    nx, ny = q_ref.shape[0] - 2 * WIDE, q_ref.shape[1]
-    layers = range(1 - reach, nx + reach - 1)
-    total = mid_neighbours(flags, v_ref, y_even, y_odd, w_ref, s_ref, reach)
-    for k, x in enumerate(layers):
-        new = (1.0 - OMEGA) * v_ref[k + 1] + start_ref[x + WIDE] + q_ref[x + WIDE] * total(x)
-        if x < 0:
-            new = jnp.where(flags[X_LO] > 0, new, 0.0)
-        if x >= nx:
-            new = jnp.where(flags[X_HI] > 0, new, 0.0)
-        out_ref[k] = new
-        index = (slice(k, k + 1), slice(None))
-        put_both(flags[Y_ODD] > 0, to_even, to_odd, index, new[0:1], new[ny - 1 : ny])
+            e = r if x < 0 else r - nx
+            layer, place = layer_beyond(flags, x_even, x_odd, 52 + e % WIDE, x < 0), SLABS + 26
+        d_out[r, 3 : 3 + ny, :] = layer
+        for k in range(WIDE):
+            even, odd = y_even[place + k, e : e + 1, :], y_odd[place + k, e : e + 1, :]
+            d_out[r, k : k + 1, :] = jnp.where(at_odd, even, odd)
+            d_out[r, 3 + ny + k : 4 + ny + k, :] = jnp.where(at_odd, odd, even)
 
 
 def swap_blocks(values):
@@ -398,36 +404,83 @@
     spread = jnp.where(
         iota((lanes, lanes), 0) % width == iota((lanes, lanes), 1) % width, 1.0, 0.0
     ).astype(F32)
-    moved = dot(wide.reshape(n * n, lanes), spread).reshape(n, n, lanes)
+    moved = dot_right(wide.reshape(n * n, lanes), spread).reshape(n, n, lanes)
     moved = jnp.where(iota(moved.shape, 2) // width == iota(moved.shape, 1), moved, 0.0)
     return jnp.sum(moved, axis=1)
 
 
-def mid_last(
+def mid_rounds(
     flags,
     places,
-    v_ref,
-    y_even,
-    y_odd,
-    f_ref,
+    fx_ref,
+    fy_even,
+    fy_odd,
     d_ref,
     w_ref,
     mid_out,
     src_out,
     slot_out,
+    f_ref,
+    v_ref,
     s_ref,
     p_ref,
 ):
-    nx, ny, nz = f_ref.shape
-    total = mid_neighbours(flags, v_ref, y_even, y_odd, w_ref, s_ref, 1)
-    left = []
+    ex, ey, nz = f_ref.shape
+    ny = fx_ref.shape[1]
+    nx = ex - 2 * WIDE
+    row = iota((ey, nz), 0)
+
+    def inside(x, reach):
+        lo = jnp.where(flags[Y_LO] > 0, WIDE - reach, WIDE)
+        hi = jnp.where(flags[Y_HI] > 0, WIDE + ny + reach, WIDE + ny)
+        ok = (row >= lo) & (row < hi)
+        if x < 0:
+            ok = ok & (flags[X_LO] > 0)
+        if x >= nx:
+            ok = ok & (flags[X_HI] > 0)
+        return ok
+
+    for r in range(ex):
+        f_ref[r] = jnp.zeros((ey, nz), F32)
+        f_ref[r, WIDE : WIDE + ny, :] = fx_ref[r]
+        even, odd = fy_even[r], fy_odd[r]
+        f_ref[r, 0:WIDE, :] = jnp.where(flags[Y_ODD] > 0, even, odd)
+        f_ref[r, WIDE + ny : 2 * WIDE + ny, :] = jnp.where(flags[Y_ODD] > 0, odd, even)
+        v_ref[r] = jnp.where(inside(r - WIDE, WIDE), OMEGA * f_ref[r] / d_ref[r], 0.0)
+
+    def spread(reach):
+        for r in range(WIDE - reach, WIDE + nx + reach):
+            layer = v_ref[r]
+            for c in (-1, 0, 1):
+                along = shift_z(layer, c)
+                for b in (-1, 0, 1):
+                    s_ref[(b + 1) * 3 + c + 1, r] = shift_y(along, b)
+
+    def leftover(r):
+        total = f_ref[r] - d_ref[r] * v_ref[r]
+        for o, (a, b, c) in enumerate(OFFSETS):
+            total = total + w_ref[o, r - 1].astype(F32) * s_ref[(b + 1) * 3 + c + 1, r + a]
+        return total
+
+    for reach in (2, 1):
+        spread(reach + 1)
+        for r in range(WIDE - reach, WIDE + nx + reach):
+            new = v_ref[r] + OMEGA * leftover(r) / d_ref[r]
+            v_ref[r] = jnp.where(inside(r - WIDE, reach), new, 0.0)
     for x in range(nx):
-        mid_out[x] = v_ref[x + 1]
-        left.append(f_ref[x] - d_ref[x] * v_ref[x + 1] + total(x))
+        mid_out[x] = v_ref[WIDE + x][WIDE : WIDE + ny]
+    spread(1)
     for i in range(nx // 2):
-        p_ref[i * ny : (i + 1) * ny, :] = left[2 * i] + left[2 * i + 1]
-    rows = dot(pair_sum_left(nx // 2 * ny), p_ref[...])
-    source = dot(rows, pair_sum_right(nz, HALVING))
+        r = WIDE + 2 * i
+        p_ref[i * ey : (i + 1) * ey, :] = leftover(r) + leftover(r + 1)
+
+    half = ny // 2
+    rows = nx // 2 * half
+    out_row = iota((rows, nx // 2 * ey), 0)
+    in_row = iota((rows, nx // 2 * ey), 1)
+    first = (out_row // half) * ey + WIDE + 2 * (out_row % half)
+    left_sum = jnp.where((in_row == first) | (in_row == first + 1), 1.0, 0.0).astype(F32)
+    source = dot_right(dot_left(left_sum, p_ref[...]), pair_sum_right(nz, HALVING))
     src_out[...] = source
     blocked = swap_blocks(source)
     slot_out[...] = jnp.zeros(slot_out.shape, F32)
@@ -523,13 +576,16 @@
     slots, cells = inverse_blocks.shape[2], inverse_blocks.shape[3]
     owners = owner_map.reshape(-1)
     places = owners * (slots // n_dev) + block_ranks(owners)
-    flags = lax.optimization_barrier(flags.astype(jnp.int32))
-
-    def on(place):
-        return flags[place] > 0
+    flags = flags.astype(jnp.int32)
+    masks = jnp.broadcast_to(flags.astype(F32)[:, None], (6, rhs_fine.shape[2]))
+    flags, masks = lax.optimization_barrier((flags, masks))
+
+    def on(place, width=nz):
+        return masks[place : place + 1, :width] > 0.5
 
     def by_parity(parity, lo, hi):
-        return jnp.where(on(parity), lo, hi), jnp.where(on(parity), hi, lo)
+        at_odd = on(parity, lo.shape[-1])
+        return jnp.where(at_odd, lo, hi), jnp.where(at_odd, hi, lo)
 
     scratch = [pltpu.VMEM((9, nx + 2, ny, nz), F32)]
     fine = sds((nx, ny, nz))
@@ -547,32 +603,27 @@
 
     hx, hy, hz = nx // 2, ny // 2, nz // 2
 
-    start, q, x_even, x_odd, *new = call(
+    faces_now = [OMEGA / diag_fine[x] * rhs_fine[x] for x in (0, nx - 1)]
+    ends = exchange("group", *by_parity(X_ODD, *faces_now))
+    start, q, *new = call(
         fine_start,
-        (fine, fine) + (one_face,) * 4,
-        in_specs=[SMEM] + [VMEM] * 2,
-        out_specs=(VMEM,) * 6,
+        (fine, fine) + (one_face,) * 2,
+        in_specs=[VMEM] * 2,
+        out_specs=(VMEM,) * 4,
         flops=LONG,
-    )(flags, rhs_fine, diag_fine)
-    ends = exchange("group", x_even, x_odd)
+    )(rhs_fine, diag_fine)
+    ends, new = lax.optimization_barrier((ends, new))
+    messages = stage(new[0], new[1], ends)
+    messages, late = lax.optimization_barrier((messages, flags))
     v, v_faces, q_faces, w_faces = call(
         fine_first,
         (fine, faces, faces, sds((4, 9, ny, nz), coup_fine.dtype)),
-        in_specs=[VMEM] * 3,
+        in_specs=[SMEM] + [VMEM] * 3,
         out_specs=(VMEM,) * 4,
         scratch_shapes=scratch + [pltpu.VMEM((2, 9, nx, nz), F32)],
         **heavy,
-    )(start, q, coup_fine)
-    ends, new, v_faces = lax.optimization_barrier((ends, new, v_faces))
-    messages = stage(new[0], new[1], ends)
-    messages, early_d = lax.optimization_barrier((messages, diag_mid))
+    )(late, start, q, coup_fine)
     halo = ends + exchange("dev", *messages)
-    slabs = sds((52 + WIDE, hy, hz))
-    wx = call(
-        mid_pack, (slabs, slabs), in_specs=[SMEM] + [VMEM] * 2, out_specs=(VMEM,) * 2
-    )(flags, coup_mid, early_d)
-    wx = exchange("group", *wx)
-    halo, wx = lax.optimization_barrier((halo, wx))
     fix = call(
         fine_halo,
         (one_face,) * 6,
@@ -592,15 +643,17 @@
     )(v, *new, start, q, coup_fine)
     ends, v_faces, new = lax.optimization_barrier((ends, v_faces, new))
     messages = stage(new[2], new[3], ends)
-    messages, wx = lax.optimization_barrier((messages, wx))
+    messages, late = lax.optimization_barrier((messages, flags))
     halo = ends + exchange("dev", *messages)
-    w_wide, q_wide = call(
-        mid_assemble,
-        (sds((26, hx + 4, hy, hz), coup_mid.dtype), sds((hx + 2 * WIDE, hy, hz))),
-        in_specs=[SMEM] + [VMEM] * 4,
+    slabs = sds((SLABS, hy, hz))
+    wx = call(
+        mid_pack,
+        (slabs, slabs),
+        in_specs=[SMEM] + [VMEM] * 2,
         out_specs=(VMEM,) * 2,
-    )(flags, coup_mid, diag_mid, *wx)
-    halo, q_wide = lax.optimization_barrier((halo, q_wide))
+        flops=LONG,
+    )(late, coup_mid, diag_mid)
+    wx = exchange("group", *wx)
     *new, x_even, x_odd = fix(flags, *halo, w_faces, v_faces, q_faces)
 
     ends = exchange("group", x_even, x_odd)
@@ -612,8 +665,20 @@
         scratch_shapes=scratch + [pltpu.VMEM((hx * ny, nz), F32)],
         **heavy,
     )(v, *new, start, q, coup_fine)
-    ends, g_mid, new = lax.optimization_barrier((ends, g_mid, new))
-    halo = ends + exchange("dev", *stage(new[2], new[3], ends))
+    ends, g_mid, new, wx = lax.optimization_barrier((ends, g_mid, new, wx))
+    messages = stage(new[2], new[3], ends)
+    messages, late = lax.optimization_barrier((messages, flags))
+    halo = ends + exchange("dev", *messages)
+    strips = sds((SLABS + 26 + WIDE, hx, hz))
+    wy = call(
+        mid_pack_y,
+        (strips, strips),
+        in_specs=[SMEM] + [VMEM] * 4,
+        out_specs=(VMEM,) * 2,
+        flops=LONG,
+    )(late, coup_mid, diag_mid, *wx)
+    halo, wy = lax.optimization_barrier((halo, wy))
+    wy = exchange("dev", *wy)
     f_mid, fx_even, fx_odd = call(
         fine_halo_last,
         (sds((hx, hy, hz)), sds((WIDE, hy, hz)), sds((WIDE, hy, hz))),
@@ -622,36 +687,34 @@
         scratch_shapes=[pltpu.VMEM((4 * ny, nz), F32)],
     )(flags, *halo, w_faces, g_mid)
 
-    ex = hx + 2 * WIDE
-    fx = exchange("group", fx_even, fx_odd)
-    wide = sds((ex, hy, hz))
-    mid_scratch = [pltpu.VMEM((9, ex, hy, hz), F32)]
-    start_wide, *halo = call(
-        mid_start,
-        (wide, sds((ex, hz)), sds((ex, hz))),
-        in_specs=[SMEM] + [VMEM] * 4,
-        out_specs=(VMEM,) * 3,
-    )(flags, f_mid, *fx, q_wide)
-    v_mid = start_wide
-    for reach in (WIDE, WIDE - 1):
-        halo = exchange("dev", *halo)
-        count = hx + 2 * reach - 2
-        v_mid, *halo = call(
-            functools.partial(mid_next, reach),
-            (sds((count, hy, hz)), sds((count, hz)), sds((count, hz))),
-            in_specs=[SMEM] + [VMEM] * 6,
-            out_specs=(VMEM,) * 3,
-            scratch_shapes=mid_scratch,
-        )(flags, v_mid, *halo, start_wide, q_wide, w_wide)
-    halo = exchange("dev", *halo)
+    fx_even, fx_odd = exchange("group", fx_even, fx_odd)
+    fx_even, fx_odd, wy = lax.optimization_barrier((fx_even, fx_odd, wy))
+    at_odd = on(X_ODD, hz)
+    fx_lo, fx_hi = jnp.where(at_odd, fx_even, fx_odd), jnp.where(at_odd, fx_odd, fx_even)
+    fx = jnp.concatenate([fx_lo, f_mid, fx_hi], axis=0)
+    fy = exchange("dev", *by_parity(Y_ODD, fx[:, :WIDE], fx[:, hy - WIDE :]))
+    ex, ey = hx + 2 * WIDE, 16
+    w_wide, d_wide = call(
+        mid_assemble,
+        (sds((26, hx + 4, ey, hz), coup_mid.dtype), sds((ex, ey, hz))),
+        in_specs=[SMEM] + [VMEM] * 6,
+        out_specs=(VMEM,) * 2,
+        scratch_shapes=[pltpu.VMEM((hx + 4, ey, hz), F32)],
+    )(flags, coup_mid, diag_mid, *wx, *wy)
     qx, qy, qz = hx // 2, hy // 2, hz // 2
     mid_iterate, source, outgoing = call(
-        mid_last,
+        mid_rounds,
         (sds((hx, hy, hz)), sds((qx * qy, qz)), sds((slots, cells))),
-        in_specs=[SMEM] * 2 + [VMEM] * 6,
+        in_specs=[SMEM] * 2 + [VMEM] * 5,
         out_specs=(VMEM,) * 3,
-        scratch_shapes=mid_scratch + [pltpu.VMEM((qx * hy, hz), F32)],
-    )(flags, places, v_mid, *halo, f_mid, diag_mid, w_wide)
+        scratch_shapes=[
+            pltpu.VMEM((ex, ey, hz), F32),
+            pltpu.VMEM((ex, ey, hz), F32),
+            pltpu.VMEM((9, ex, ey, hz), F32),
+            pltpu.VMEM((hx // 2 * ey, hz), F32),
+        ],
+        flops=20_000_000,
+    )(flags, places, fx, *fy, d_wide, w_wide)
 
     arrived = lax.all_to_all(outgoing, "dev", split_axis=0, concat_axis=0, tiled=True)
     owned = call(solve_blocks, sds((slots, cells)), in_specs=[VMEM] * 2, out_specs=VMEM)(

time: 113 us -> 105 us (0.929)
  waiting for transfers between devices: 25.8 us -> 20.6 us
  Pallas kernels: 23.1 us -> 25.8 us
  between operations: 3.61 us -> 1.02 us
  blocking collectives: 25.8 us -> 24.3 us
    ppermute x22 -> x20, waiting for transfers between devices: 25.8 us -> 20.6 us  [exchange(): return (lax.ppermute(to_even, axis, even), lax.ppermute(to_odd, axis, odd))]
    pallas_call x6 -> x4, Pallas kernels: 5.86 us -> 7.78 us  [the longest x1 3.46 us: shards(): call(mid_rounds, (sds((hx, hy, hz)), sds((qx * qy, qz)), sds((slots, cell...]
    all_to_all x1, blocking collectives: 15.3 us -> 13.7 us  [shards(): lax.all_to_all(outgoing, 'dev', split_axis=0, concat_axis=0, tiled=True)]
    ppermute x22 -> x20, starting transfers between devices: 30.8 us -> 29.7 us  [exchange(): return (lax.ppermute(to_even, axis, even), lax.ppermute(to_odd, axis, odd))]
  transfers between devices with their start and end apart: 22 -> 20, of which waited for: 15 -> 8; matrix products, arithmetic and copies ran while one was open for 1% -> 0% of each run, Pallas kernels for 11% -> 18%
where the time goes in v2:
time: 105 us
  starting transfers between devices  29.7 us (28%)
  Pallas kernels  25.8 us (25%)
  blocking collectives  24.3 us (23%)
  waiting for transfers between devices  20.6 us (20%)
  local copies, waits for them, and re-layouts  2.33 us (2%)
  other arithmetic  1.25 us (1%)
    ppermute x20, starting transfers between devices, exchange(): return (lax.ppermute(to_even, axis, even), lax.ppermute(to_odd, axis, odd))  29.7 us
    ppermute x20, waiting for transfers between devices, exchange(): return (lax.ppermute(to_even, axis, even), lax.ppermute(to_odd, axis, odd))  20.6 us
    all_to_all x1, blocking collectives, shards(): lax.all_to_all(outgoing, 'dev', split_axis=0, concat_axis=0, tiled=True)  13.7 us
    all_to_all x1, blocking collectives, shards(): lax.all_to_all(owned, 'dev', split_axis=0, concat_axis=0, tiled=True)  10.6 us
    pallas_call x1, Pallas kernels, shards(): call(fine_first, (fine, faces, faces, sds((4, 9, ny, nz), coup_fine.dtype...  4.59 us
    pallas_call x1, Pallas kernels, shards(): call(fine_last, (fine, sds((hx, hy, hz))), in_specs=[VMEM] * 8, out_specs...  4.12 us
    pallas_call x1, Pallas kernels, shards(): call(fine_next, (fine, faces), in_specs=[VMEM] * 8, out_specs=(VMEM,) * 2...  3.71 us
    pallas_call x1, Pallas kernels, shards(): call(mid_rounds, (sds((hx, hy, hz)), sds((qx * qy, qz)), sds((slots, cell...  3.46 us
  transfers between devices with their start and end apart: 20, of which 8 were waited for; matrix products, arithmetic and copies ran while one was open for 0% of the time, Pallas kernels for 18%

profile of v2, /device:TPU:2, one launch (start us, length us, event | category | flops | bytes accessed | tf_op | source)
XLA Modules:
  0.0 105.1 jit_solution(8097731446033590900)
XLA Ops:
  0.7 0.1 stack.27
  0.8 0.1 broadcast_in_dim.124
  0.9 0.8 bitcast_select_fusion
  1.7 0.1 collective-permute-start
  1.8 0.0 slice-start
  1.8 5.9 %collective-permute-start.1 = (f32[16,512]{1,0:T(8,128)S(1)}, f32[16,512]{1,0:T(8,128)S(1)}, u32[]{:S(2)}, u32[]{:S(2)}) collective-permute-start(f32[16,512]{1,0:T(8,128)S(1)} %get-tuple-element.160), channel_id=1, source_target_pairs={{0,240},{16,32},{32,16},{48,64},{64,48},{80,96},{96,80},{112,128},... | collective-permute-start | bytes 98312 | tf_op jit(solution)/shard_map/ppermute | solution.py:558
  7.8 1.0 copy-done.4
  8.8 1.0 copy-done.5
  9.9 0.2 shard_map.120
  10.2 0.6 collective-permute-start.2
  10.8 2.2 %collective-permute-start.3 = (f32[18,512]{1,0:T(8,128)S(1)}, f32[18,512]{1,0:T(8,128)S(1)}, u32[]{:S(2)}, u32[]{:S(2)}) collective-permute-start(f32[18,512]{1,0:T(8,128)S(1)} %get-tuple-element.92), channel_id=1, source_target_pairs={{0,15},{1,2},{2,1},{3,4},{4,3},{5,6},{6,5},{7,8},{8,7},{9,10},{10,... | collective-permute-start | bytes 110600 | tf_op jit(solution)/shard_map/ppermute | solution.py:558
  13.0 4.6 %shard_map.121 = (f32[16,16,512]{2,1,0:T(8,128)S(1)}, f32[4,16,512]{2,1,0:T(8,128)S(1)}, f32[4,16,512]{2,1,0:T(8,128)S(1)}, bf16[4,9,16,512]{3,2,1,0:T(8,128)(2,1)S(1)}) custom-call(s32[6]{0:T(128)S(1)} %get-tuple-element.128._.flags, f32[16,16,512]{2,1,0:T(8,128)S(1)} %get-tuple-element.88.start_ref, f32[16,16,512]{2,1,0:T(8,128)S(1)} %get-tuple-element.89.q_ref, ...), custom_call_target="tpu_custom_call" | custom-call | flops 7864320 | bytes 8912896 | tf_op jit(solution)/shard_map/pallas_call | solution.py:618
  17.6 0.8 shard_map.122
  18.4 0.1 collective-permute-start.4
  18.5 1.7 %collective-permute-start.5 = (f32[16,512]{1,0:T(8,128)S(1)}, f32[16,512]{1,0:T(8,128)S(1)}, u32[]{:S(2)}, u32[]{:S(2)}) collective-permute-start(f32[16,512]{1,0:T(8,128)S(1)} %get-tuple-element.102), channel_id=1, source_target_pairs={{0,240},{16,32},{32,16},{48,64},{64,48},{80,96},{96,80},{112,128},... | collective-permute-start | bytes 98312 | tf_op jit(solution)/shard_map/ppermute | solution.py:558
  20.2 3.7 %shard_map.123 = (f32[16,16,512]{2,1,0:T(8,128)S(1)}, f32[4,16,512]{2,1,0:T(8,128)S(1)}) custom-call(f32[16,16,512]{2,1,0:T(8,128)S(1)} %get-tuple-element.90.v_ref, f32[16,512]{1,0:T(8,128)S(1)} %get-tuple-element.96.xlo, f32[16,512]{1,0:T(8,128)S(1)} %get-tuple-element.97.xhi, f32[16,512]{1,0:T(8,128)S(1)} %get-tuple-element.106.ylo, ...), custom_call_target="tpu_custom_call" | custom-call | flops 7864320 | bytes 8912896 | tf_op jit(solution)/shard_map/pallas_call | solution.py:636
  24.1 0.7 shard_map.126
  24.8 0.1 collective-permute-start.10
  24.9 1.4 %collective-permute-start.11 = (f32[55,8,256]{2,1,0:T(8,128)S(1)}, f32[55,8,256]{2,1,0:T(8,128)S(1)}, u32[]{:S(2)}, u32[]{:S(2)}) collective-permute-start(f32[55,8,256]{2,1,0:T(8,128)S(1)} %get-tuple-element.121), channel_id=1, source_target_pairs={{0,240},{16,32},{32,16},{48,64},{64,48},{80,96},{96,80},{112,128},... | collective-permute-start | bytes 1351688 | tf_op jit(solution)/shard_map/ppermute | solution.py:558
  26.3 3.9 %collective-permute-start.6 = (f32[18,512]{1,0:T(8,128)S(1)}, f32[18,512]{1,0:T(8,128)S(1)}, u32[]{:S(2)}, u32[]{:S(2)}) collective-permute-start(f32[18,512]{1,0:T(8,128)S(1)} %get-tuple-element.108), channel_id=1, source_target_pairs={{0,1},{1,0},{2,3},{3,2},{4,5},{5,4},{6,7},{7,6},{8,9},{9,8},{10,11... | collective-permute-start | bytes 110600 | tf_op jit(solution)/shard_map/ppermute | solution.py:558
  30.2 2.1 %collective-permute-done.6.y_even = f32[18,512]{1,0:T(8,128)S(1)} collective-permute-done((f32[18,512]{1,0:T(8,128)S(1)}, f32[18,512]{1,0:T(8,128)S(1)}, u32[]{:S(2)}, u32[]{:S(2)}) %collective-permute-start.6) | collective-permute-done | bytes 36896 | tf_op jit(solution)/shard_map/ppermute | solution.py:558
  32.3 2.0 %collective-permute-done.7.y_odd = f32[18,512]{1,0:T(8,128)S(1)} collective-permute-done((f32[18,512]{1,0:T(8,128)S(1)}, f32[18,512]{1,0:T(8,128)S(1)}, u32[]{:S(2)}, u32[]{:S(2)}) %collective-permute-start.7) | collective-permute-done | bytes 36896 | tf_op jit(solution)/shard_map/ppermute | solution.py:558
  34.3 0.8 shard_map.124
  35.1 0.1 collective-permute-start.8
  35.2 1.3 %collective-permute-start.9 = (f32[16,512]{1,0:T(8,128)S(1)}, f32[16,512]{1,0:T(8,128)S(1)}, u32[]{:S(2)}, u32[]{:S(2)}) collective-permute-start(f32[16,512]{1,0:T(8,128)S(1)} %get-tuple-element.117), channel_id=1, source_target_pairs={{0,240},{16,32},{32,16},{48,64},{64,48},{80,96},{96,80},{112,128},... | collective-permute-start | bytes 98312 | tf_op jit(solution)/shard_map/ppermute | solution.py:558
  36.5 4.1 %shard_map.125 = (f32[16,16,512]{2,1,0:T(8,128)}, f32[8,8,256]{2,1,0:T(8,128)S(1)}) custom-call(f32[16,16,512]{2,1,0:T(8,128)S(1)} %get-tuple-element.100.v_ref, f32[16,512]{1,0:T(8,128)S(1)} %get-tuple-element.111.xlo, f32[16,512]{1,0:T(8,128)S(1)} %get-tuple-element.112.xhi, f32[16,512]{1,0:T(8,128)S(1)} %get-tuple-element.124.ylo, ...), custom_call_target="tpu_custom_call" | custom-call | flops 7864320 | bytes 8912896 | tf_op jit(solution)/shard_map/pallas_call | solution.py:660
  40.8 0.0 copy-start.7
  40.8 3.1 %collective-permute-start.12 = (f32[18,512]{1,0:T(8,128)S(1)}, f32[18,512]{1,0:T(8,128)S(1)}, u32[]{:S(2)}, u32[]{:S(2)}) collective-permute-start(f32[18,512]{1,0:T(8,128)S(1)} %get-tuple-element.126), channel_id=1, source_target_pairs={{0,1},{1,0},{2,3},{3,2},{4,5},{5,4},{6,7},{7,6},{8,9},{9,8},{10,11... | collective-permute-start | bytes 110600 | tf_op jit(solution)/shard_map/ppermute | solution.py:558
  43.9 1.9 %shard_map.127 = (f32[84,8,256]{2,1,0:T(8,128)S(1)}, f32[84,8,256]{2,1,0:T(8,128)S(1)}) custom-call(s32[6]{0:T(128)S(1)} %get-tuple-element.128._.flags, bf16[26,8,8,256]{3,2,1,0:T(8,128)(2,1)S(1)} %copy-done.1, f32[8,8,256]{2,1,0:T(8,128)S(1)} %copy-done.3, f32[55,8,256]{2,1,0:T(8,128)S(1)} %collective-permute-done.10.x_even, ...), custom_call_target="tpu_custom_call" | custom-call | flops 30000001024 | bytes 1000000 | tf_op jit(solution)/shard_map/pallas_call | solution.py:673
  45.8 0.1 collective-permute-done.12.y_even
  46.0 2.0 %collective-permute-done.13.y_odd = f32[18,512]{1,0:T(8,128)S(1)} collective-permute-done((f32[18,512]{1,0:T(8,128)S(1)}, f32[18,512]{1,0:T(8,128)S(1)}, u32[]{:S(2)}, u32[]{:S(2)}) %collective-permute-start.13) | collective-permute-done | bytes 36896 | tf_op jit(solution)/shard_map/ppermute | solution.py:558
  48.0 3.4 %collective-permute-start.16 = (f32[84,8,256]{2,1,0:T(8,128)S(1)}, f32[84,8,256]{2,1,0:T(8,128)S(1)}, u32[]{:S(2)}, u32[]{:S(2)}) collective-permute-start(f32[84,8,256]{2,1,0:T(8,128)S(1)} %get-tuple-element.140), channel_id=1, source_target_pairs={{0,1},{1,0},{2,3},{3,2},{4,5},{5,4},{6,7},{7,6},{8,9},{9,8},{10,11... | collective-permute-start | bytes 2064392 | tf_op jit(solution)/shard_map/ppermute | solution.py:558
  51.4 0.0 collective-permute-start.17
  51.4 0.2 convert_reduce_fusion
  51.6 1.2 %shard_map.128 = (f32[8,8,256]{2,1,0:T(8,128)S(1)}, f32[3,8,256]{2,1,0:T(8,128)S(1)}, f32[3,8,256]{2,1,0:T(8,128)S(1)}) custom-call(s32[6]{0:T(128)S(1)} %get-tuple-element.128._.flags, f32[16,512]{1,0:T(8,128)S(1)} %collective-permute-done.8.x_even, f32[16,512]{1,0:T(8,128)S(1)} %collective-permute-done.9.x_odd, ...), custom_call_target="tpu_custom_call" | custom-call | flops 1000000 | bytes 1000000 | tf_op jit(solution)/shard_map/pallas_call | solution.py:682
  52.8 0.1 collective-permute-start.14
  52.9 2.0 %collective-permute-start.15 = (f32[3,8,256]{2,1,0:T(8,128)S(1)}, f32[3,8,256]{2,1,0:T(8,128)S(1)}, u32[]{:S(2)}, u32[]{:S(2)}) collective-permute-start(f32[3,8,256]{2,1,0:T(8,128)S(1)} %get-tuple-element.139), channel_id=1, source_target_pairs={{0,240},{16,32},{32,16},{48,64},{64,48},{80,96},{96,80},{112,128},... | collective-permute-start | bytes 73736 | tf_op jit(solution)/shard_map/ppermute | solution.py:558
  54.9 2.5 %collective-permute-done.15 = f32[3,8,256]{2,1,0:T(8,128)S(1)} collective-permute-done((f32[3,8,256]{2,1,0:T(8,128)S(1)}, f32[3,8,256]{2,1,0:T(8,128)S(1)}, u32[]{:S(2)}, u32[]{:S(2)}) %collective-permute-start.15) | collective-permute-done | bytes 24608 | tf_op jit(solution)/shard_map/ppermute | solution.py:558
  57.4 8.3 %collective-permute-done.16.y_even = f32[84,8,256]{2,1,0:T(8,128)S(1)} collective-permute-done((f32[84,8,256]{2,1,0:T(8,128)S(1)}, f32[84,8,256]{2,1,0:T(8,128)S(1)}, u32[]{:S(2)}, u32[]{:S(2)}) %collective-permute-start.16) | collective-permute-done | bytes 688160 | tf_op jit(solution)/shard_map/ppermute | solution.py:558
  65.8 1.5 %collective-permute-done.17.y_odd = f32[84,8,256]{2,1,0:T(8,128)S(1)} collective-permute-done((f32[84,8,256]{2,1,0:T(8,128)S(1)}, f32[84,8,256]{2,1,0:T(8,128)S(1)}, u32[]{:S(2)}, u32[]{:S(2)}) %collective-permute-start.17) | collective-permute-done | bytes 688160 | tf_op jit(solution)/shard_map/ppermute | solution.py:558
  67.3 3.7 %collective-permute-start.18 = (f32[14,3,256]{2,1,0:T(4,128)S(1)}, f32[14,3,256]{2,1,0:T(4,128)S(1)}, u32[]{:S(2)}, u32[]{:S(2)}) collective-permute-start(f32[14,3,256]{2,1,0:T(4,128)S(1)} %get-tuple-element.163), channel_id=1, source_target_pairs={{0,1},{1,0},{2,3},{3,2},{4,5},{5,4},{6,7},{7,6},{8,9},{9,8},{10,11... | collective-permute-start | bytes 129032 | tf_op jit(solution)/shard_map/ppermute | solution.py:558
  71.0 2.2 %shard_map.129 = (bf16[26,12,16,256]{3,2,1,0:T(8,128)(2,1)S(1)}, f32[14,16,256]{2,1,0:T(8,128)S(1)}) custom-call(s32[6]{0:T(128)S(1)} %get-tuple-element.128._.flags, bf16[26,8,8,256]{3,2,1,0:T(8,128)(2,1)S(1)} %copy-done.1, f32[8,8,256]{2,1,0:T(8,128)S(1)} %copy-done.3, f32[55,8,256]{2,1,0:T(8,128)S(1)} %collective-permute-done.10.x_even, ...), custom_call_target="tpu_custom_call" | custom-call | flops 1000000 | bytes 1000000 | tf_op jit(solution)/shard_map/pallas_call | solution.py:697
  73.2 2.0 %collective-permute-done.19.fy_odd = f32[14,3,256]{2,1,0:T(4,128)S(1)} collective-permute-done((f32[14,3,256]{2,1,0:T(4,128)S(1)}, f32[14,3,256]{2,1,0:T(4,128)S(1)}, u32[]{:S(2)}, u32[]{:S(2)}) %collective-permute-start.19) | collective-permute-done | bytes 43040 | tf_op jit(solution)/shard_map/ppermute | solution.py:558
  75.2 3.5 %shard_map.130 = (f32[8,8,256]{2,1,0:T(8,128)}, f32[16,128]{1,0:T(8,128)S(1)}, f32[32,128]{1,0:T(8,128)S(1)}) custom-call(s32[6]{0:T(128)S(1)} %get-tuple-element.128._.flags, s32[16]{0:T(128)S(1)} %multiply_add_fusion.places, f32[14,8,256]{2,1,0:T(8,128)S(1)} %pad_maximum_fusion.fx_ref, f32[14,3,256]{2,1,0:T(4,128)S(1)} %collective-permute-done.18.fy_even, ...), custom_call_target="tpu_custom_call" | custom-call | flops 20000000 | bytes 1000000 | tf_op jit(solution)/shard_map/pallas_call | solution.py:705
  78.6 13.7 %all_to_all.22 = f32[16,2,128]{2,1,0:T(2,128)S(1)} all-to-all(f32[16,2,128]{2,1,0:T(2,128)S(1)} %bitcast.28), channel_id=1, replica_groups=mesh['group'=16,'dev'=16] {'dev'}, dimensions={0} | all-to-all | bytes 32768 | tf_op jit(solution)/shard_map/all_to_all | solution.py:719
  92.4 0.7 shard_map.131
  93.0 10.6 %all_to_all.23 = f32[16,2,128]{2,1,0:T(2,128)S(1)} all-to-all(f32[16,2,128]{2,1,0:T(2,128)S(1)} %bitcast.26), channel_id=1, replica_groups=mesh['group'=16,'dev'=16] {'dev'}, dimensions={0} | all-to-all | bytes 32768 | tf_op jit(solution)/shard_map/all_to_all | solution.py:723
  103.6 1.5 %shard_map.132 = (f32[4,4,128]{2,1,0:T(4,128)}, f32[4,4,128]{2,1,0:T(4,128)}) custom-call(s32[16]{0:T(128)S(1)} %multiply_add_fusion.places, f32[32,128]{1,0:T(8,128)S(1)} %bitcast.27, f32[16,128]{1,0:T(8,128)S(1)} %get-tuple-element.151.src_ref, f32[16,128]{1,0:T(8,128)S(1)} %bitcast.29, bf16[26,16,128]{2,1,0:T(8,128)(2,1)S(1)} %bitcast.24), custom_call_target="tpu_custom_call" | custom-call | flops 1000000 | bytes 1000000 | tf_op jit(solution)/shard_map/pallas_call | solution.py:724
  (50 shorter events, 0.3 us)
Async XLA Ops:
  1.7 8.4 %collective-permute-start = (f32[16,512]{1,0:T(8,128)S(1)}, f32[16,512]{1,0:T(8,128)S(1)}, u32[]{:S(2)}, u32[]{:S(2)}) collective-permute-start(f32[16,512]{1,0:T(8,128)S(1)} %get-tuple-element.161), channel_id=1, source_target_pairs={{0,16},{16,0},{32,48},{48,32},{64,80},{80,64},{96,112},{112,96},{1... | collective-permute-start | bytes 98312 | tf_op jit(solution)/shard_map/ppermute | solution.py:558
  1.8 11.1 %slice-start = ((s8[6815744]{0:T(1024)(128)(4,1)}), s8[4194304]{0:T(1024)(128)(4,1)S(1)}, s32[]{:S(2)}) async-start(s8[6815744]{0:T(1024)(128)(4,1)} %bitcast.21), calls=%async_computation.2 | async-start | bytes 8388608
  1.8 11.1 %slice-start.1 = ((s8[6815744]{0:T(1024)(128)(4,1)}), s8[2621440]{0:T(1024)(128)(4,1)S(1)}, s32[]{:S(2)}) async-start(s8[6815744]{0:T(1024)(128)(4,1)} %bitcast.21), calls=%async_computation.3 | async-start | bytes 5242880
  1.8 8.3 %collective-permute-start.1 = (f32[16,512]{1,0:T(8,128)S(1)}, f32[16,512]{1,0:T(8,128)S(1)}, u32[]{:S(2)}, u32[]{:S(2)}) collective-permute-start(f32[16,512]{1,0:T(8,128)S(1)} %get-tuple-element.160), channel_id=1, source_target_pairs={{0,240},{16,32},{32,16},{48,64},{64,48},{80,96},{96,80},{112,128},... | collective-permute-start | bytes 98312 | tf_op jit(solution)/shard_map/ppermute | solution.py:558
  7.8 1.0 copy-start.4
  8.8 1.0 copy-start.5
  10.2 7.4 %collective-permute-start.2 = (f32[18,512]{1,0:T(8,128)S(1)}, f32[18,512]{1,0:T(8,128)S(1)}, u32[]{:S(2)}, u32[]{:S(2)}) collective-permute-start(f32[18,512]{1,0:T(8,128)S(1)} %get-tuple-element.91), channel_id=1, source_target_pairs={{0,1},{1,0},{2,3},{3,2},{4,5},{5,4},{6,7},{7,6},{8,9},{9,8},{10,11... | collective-permute-start | bytes 110600 | tf_op jit(solution)/shard_map/ppermute | solution.py:558
  10.8 6.8 %collective-permute-start.3 = (f32[18,512]{1,0:T(8,128)S(1)}, f32[18,512]{1,0:T(8,128)S(1)}, u32[]{:S(2)}, u32[]{:S(2)}) collective-permute-start(f32[18,512]{1,0:T(8,128)S(1)} %get-tuple-element.92), channel_id=1, source_target_pairs={{0,15},{1,2},{2,1},{3,4},{4,3},{5,6},{6,5},{7,8},{8,7},{9,10},{10,... | collective-permute-start | bytes 110600 | tf_op jit(solution)/shard_map/ppermute | solution.py:558
  18.4 5.6 %collective-permute-start.4 = (f32[16,512]{1,0:T(8,128)S(1)}, f32[16,512]{1,0:T(8,128)S(1)}, u32[]{:S(2)}, u32[]{:S(2)}) collective-permute-start(f32[16,512]{1,0:T(8,128)S(1)} %get-tuple-element.101), channel_id=1, source_target_pairs={{0,16},{16,0},{32,48},{48,32},{64,80},{80,64},{96,112},{112,96},{1... | collective-permute-start | bytes 98312 | tf_op jit(solution)/shard_map/ppermute | solution.py:558
  18.5 5.5 %collective-permute-start.5 = (f32[16,512]{1,0:T(8,128)S(1)}, f32[16,512]{1,0:T(8,128)S(1)}, u32[]{:S(2)}, u32[]{:S(2)}) collective-permute-start(f32[16,512]{1,0:T(8,128)S(1)} %get-tuple-element.102), channel_id=1, source_target_pairs={{0,240},{16,32},{32,16},{48,64},{64,48},{80,96},{96,80},{112,128},... | collective-permute-start | bytes 98312 | tf_op jit(solution)/shard_map/ppermute | solution.py:558
  20.2 3.8 %copy-start.1 = (bf16[26,8,8,256]{3,2,1,0:T(8,128)(2,1)S(1)}, bf16[26,8,8,256]{3,2,1,0:T(8,128)(2,1)}, u32[]{:S(2)}) copy-start(bf16[26,8,8,256]{3,2,1,0:T(8,128)(2,1)} %w_ref.11) | copy-start | bytes 2555908
  20.2 3.8 %copy-start.3 = (f32[8,8,256]{2,1,0:T(8,128)S(1)}, f32[8,8,256]{2,1,0:T(8,128)}, u32[]{:S(2)}) copy-start(f32[8,8,256]{2,1,0:T(8,128)} %d_ref.7) | copy-start | bytes 196612
  24.8 15.8 %collective-permute-start.10 = (f32[55,8,256]{2,1,0:T(8,128)S(1)}, f32[55,8,256]{2,1,0:T(8,128)S(1)}, u32[]{:S(2)}, u32[]{:S(2)}) collective-permute-start(f32[55,8,256]{2,1,0:T(8,128)S(1)} %get-tuple-element.120), channel_id=1, source_target_pairs={{0,16},{16,0},{32,48},{48,32},{64,80},{80,64},{96,112},{112,96},{1... | collective-permute-start | bytes 1351688 | tf_op jit(solution)/shard_map/ppermute | solution.py:558
  24.9 15.7 %collective-permute-start.11 = (f32[55,8,256]{2,1,0:T(8,128)S(1)}, f32[55,8,256]{2,1,0:T(8,128)S(1)}, u32[]{:S(2)}, u32[]{:S(2)}) collective-permute-start(f32[55,8,256]{2,1,0:T(8,128)S(1)} %get-tuple-element.121), channel_id=1, source_target_pairs={{0,240},{16,32},{32,16},{48,64},{64,48},{80,96},{96,80},{112,128},... | collective-permute-start | bytes 1351688 | tf_op jit(solution)/shard_map/ppermute | solution.py:558
  26.3 6.0 %collective-permute-start.6 = (f32[18,512]{1,0:T(8,128)S(1)}, f32[18,512]{1,0:T(8,128)S(1)}, u32[]{:S(2)}, u32[]{:S(2)}) collective-permute-start(f32[18,512]{1,0:T(8,128)S(1)} %get-tuple-element.108), channel_id=1, source_target_pairs={{0,1},{1,0},{2,3},{3,2},{4,5},{5,4},{6,7},{7,6},{8,9},{9,8},{10,11... | collective-permute-start | bytes 110600 | tf_op jit(solution)/shard_map/ppermute | solution.py:558
  30.2 4.1 %collective-permute-start.7 = (f32[18,512]{1,0:T(8,128)S(1)}, f32[18,512]{1,0:T(8,128)S(1)}, u32[]{:S(2)}, u32[]{:S(2)}) collective-permute-start(f32[18,512]{1,0:T(8,128)S(1)} %get-tuple-element.109), channel_id=1, source_target_pairs={{0,15},{1,2},{2,1},{3,4},{4,3},{5,6},{6,5},{7,8},{8,7},{9,10},{10,... | collective-permute-start | bytes 110600 | tf_op jit(solution)/shard_map/ppermute | solution.py:558
  35.1 5.5 %collective-permute-start.8 = (f32[16,512]{1,0:T(8,128)S(1)}, f32[16,512]{1,0:T(8,128)S(1)}, u32[]{:S(2)}, u32[]{:S(2)}) collective-permute-start(f32[16,512]{1,0:T(8,128)S(1)} %get-tuple-element.116), channel_id=1, source_target_pairs={{0,16},{16,0},{32,48},{48,32},{64,80},{80,64},{96,112},{112,96},{1... | collective-permute-start | bytes 98312 | tf_op jit(solution)/shard_map/ppermute | solution.py:558
  35.2 5.4 %collective-permute-start.9 = (f32[16,512]{1,0:T(8,128)S(1)}, f32[16,512]{1,0:T(8,128)S(1)}, u32[]{:S(2)}, u32[]{:S(2)}) collective-permute-start(f32[16,512]{1,0:T(8,128)S(1)} %get-tuple-element.117), channel_id=1, source_target_pairs={{0,240},{16,32},{32,16},{48,64},{64,48},{80,96},{96,80},{112,128},... | collective-permute-start | bytes 98312 | tf_op jit(solution)/shard_map/ppermute | solution.py:558
  40.8 10.7 %copy-start.7 = (s32[1,1,16,1]{2,3,1,0:T(1,128)S(1)}, s32[1,1,16,1]{2,3,1,0:T(1,128)}, u32[]{:S(2)}) copy-start(s32[1,1,16,1]{2,3,1,0:T(1,128)} %param.16) | copy-start | bytes 196
  40.8 5.2 %collective-permute-start.12 = (f32[18,512]{1,0:T(8,128)S(1)}, f32[18,512]{1,0:T(8,128)S(1)}, u32[]{:S(2)}, u32[]{:S(2)}) collective-permute-start(f32[18,512]{1,0:T(8,128)S(1)} %get-tuple-element.126), channel_id=1, source_target_pairs={{0,1},{1,0},{2,3},{3,2},{4,5},{5,4},{6,7},{7,6},{8,9},{9,8},{10,11... | collective-permute-start | bytes 110600 | tf_op jit(solution)/shard_map/ppermute | solution.py:558
  43.9 4.1 %collective-permute-start.13 = (f32[18,512]{1,0:T(8,128)S(1)}, f32[18,512]{1,0:T(8,128)S(1)}, u32[]{:S(2)}, u32[]{:S(2)}) collective-permute-start(f32[18,512]{1,0:T(8,128)S(1)} %get-tuple-element.127), channel_id=1, source_target_pairs={{0,15},{1,2},{2,1},{3,4},{4,3},{5,6},{6,5},{7,8},{8,7},{9,10},{10,... | collective-permute-start | bytes 110600 | tf_op jit(solution)/shard_map/ppermute | solution.py:558
  48.0 17.8 %collective-permute-start.16 = (f32[84,8,256]{2,1,0:T(8,128)S(1)}, f32[84,8,256]{2,1,0:T(8,128)S(1)}, u32[]{:S(2)}, u32[]{:S(2)}) collective-permute-start(f32[84,8,256]{2,1,0:T(8,128)S(1)} %get-tuple-element.140), channel_id=1, source_target_pairs={{0,1},{1,0},{2,3},{3,2},{4,5},{5,4},{6,7},{7,6},{8,9},{9,8},{10,11... | collective-permute-start | bytes 2064392 | tf_op jit(solution)/shard_map/ppermute | solution.py:558
  51.4 15.8 %collective-permute-start.17 = (f32[84,8,256]{2,1,0:T(8,128)S(1)}, f32[84,8,256]{2,1,0:T(8,128)S(1)}, u32[]{:S(2)}, u32[]{:S(2)}) collective-permute-start(f32[84,8,256]{2,1,0:T(8,128)S(1)} %get-tuple-element.141), channel_id=1, source_target_pairs={{0,15},{1,2},{2,1},{3,4},{4,3},{5,6},{6,5},{7,8},{8,7},{9,10},{10,... | collective-permute-start | bytes 2064392 | tf_op jit(solution)/shard_map/ppermute | solution.py:558
  52.8 2.1 %collective-permute-start.14 = (f32[3,8,256]{2,1,0:T(8,128)S(1)}, f32[3,8,256]{2,1,0:T(8,128)S(1)}, u32[]{:S(2)}, u32[]{:S(2)}) collective-permute-start(f32[3,8,256]{2,1,0:T(8,128)S(1)} %get-tuple-element.138), channel_id=1, source_target_pairs={{0,16},{16,0},{32,48},{48,32},{64,80},{80,64},{96,112},{112,96},{1... | collective-permute-start | bytes 73736 | tf_op jit(solution)/shard_map/ppermute | solution.py:558
  52.9 4.5 %collective-permute-start.15 = (f32[3,8,256]{2,1,0:T(8,128)S(1)}, f32[3,8,256]{2,1,0:T(8,128)S(1)}, u32[]{:S(2)}, u32[]{:S(2)}) collective-permute-start(f32[3,8,256]{2,1,0:T(8,128)S(1)} %get-tuple-element.139), channel_id=1, source_target_pairs={{0,240},{16,32},{32,16},{48,64},{64,48},{80,96},{96,80},{112,128},... | collective-permute-start | bytes 73736 | tf_op jit(solution)/shard_map/ppermute | solution.py:558
  67.3 5.9 %collective-permute-start.18 = (f32[14,3,256]{2,1,0:T(4,128)S(1)}, f32[14,3,256]{2,1,0:T(4,128)S(1)}, u32[]{:S(2)}, u32[]{:S(2)}) collective-permute-start(f32[14,3,256]{2,1,0:T(4,128)S(1)} %get-tuple-element.163), channel_id=1, source_target_pairs={{0,1},{1,0},{2,3},{3,2},{4,5},{5,4},{6,7},{7,6},{8,9},{9,8},{10,11... | collective-permute-start | bytes 129032 | tf_op jit(solution)/shard_map/ppermute | solution.py:558
  71.0 4.2 %collective-permute-start.19 = (f32[14,3,256]{2,1,0:T(4,128)S(1)}, f32[14,3,256]{2,1,0:T(4,128)S(1)}, u32[]{:S(2)}, u32[]{:S(2)}) collective-permute-start(f32[14,3,256]{2,1,0:T(4,128)S(1)} %get-tuple-element.162), channel_id=1, source_target_pairs={{0,15},{1,2},{2,1},{3,4},{4,3},{5,6},{6,5},{7,8},{8,7},{9,10},{10,... | collective-permute-start | bytes 129032 | tf_op jit(solution)/shard_map/ppermute | solution.py:558
  71.0 21.4 %copy-start = (f32[1,1,32,128,128]{4,3,2,1,0:T(8,128)S(1)}, f32[1,1,32,128,128]{4,3,2,1,0:T(8,128)}, u32[]{:S(2)}) copy-start(f32[1,1,32,128,128]{4,3,2,1,0:T(8,128)} %param.17) | copy-start | bytes 6291460
  75.2 28.5 %copy-start.2 = (bf16[26,4,4,128]{3,2,1,0:T(4,128)(2,1)S(1)}, bf16[26,4,4,128]{3,2,1,0:T(4,128)(2,1)}, u32[]{:S(2)}) copy-start(bf16[26,4,4,128]{3,2,1,0:T(4,128)(2,1)} %param.15) | copy-start | bytes 319492
  75.2 28.5 %copy-start.6 = (f32[4,4,128]{2,1,0:T(4,128)S(1)}, f32[4,4,128]{2,1,0:T(4,128)}, u32[]{:S(2)}) copy-start(f32[4,4,128]{2,1,0:T(4,128)} %param.14) | copy-start | bytes 24580

commit v3 on v2

--- a/solution.py
+++ b/solution.py
@@ -653,6 +653,7 @@
         out_specs=(VMEM,) * 2,
         flops=LONG,
     )(late, coup_mid, diag_mid)
+    halo, _ = lax.optimization_barrier((halo, wx))
     wx = exchange("group", *wx)
     *new, x_even, x_odd = fix(flags, *halo, w_faces, v_faces, q_faces)
 
@@ -663,9 +664,8 @@
         in_specs=[VMEM] * 8,
         out_specs=(VMEM,) * 2,
         scratch_shapes=scratch + [pltpu.VMEM((hx * ny, nz), F32)],
-        **heavy,
     )(v, *new, start, q, coup_fine)
-    ends, g_mid, new, wx = lax.optimization_barrier((ends, g_mid, new, wx))
+    ends, g_mid, new = lax.optimization_barrier((ends, g_mid, new))
     messages = stage(new[2], new[3], ends)
     messages, late = lax.optimization_barrier((messages, flags))
     halo = ends + exchange("dev", *messages)
@@ -688,7 +688,6 @@
     )(flags, *halo, w_faces, g_mid)
 
     fx_even, fx_odd = exchange("group", fx_even, fx_odd)
-    fx_even, fx_odd, wy = lax.optimization_barrier((fx_even, fx_odd, wy))
     at_odd = on(X_ODD, hz)
     fx_lo, fx_hi = jnp.where(at_odd, fx_even, fx_odd), jnp.where(at_odd, fx_odd, fx_even)
     fx = jnp.concatenate([fx_lo, f_mid, fx_hi], axis=0)
@@ -700,6 +699,7 @@
         in_specs=[SMEM] + [VMEM] * 6,
         out_specs=(VMEM,) * 2,
         scratch_shapes=[pltpu.VMEM((hx + 4, ey, hz), F32)],
+        flops=LONG,
     )(flags, coup_mid, diag_mid, *wx, *wy)
     qx, qy, qz = hx // 2, hy // 2, hz // 2
     mid_iterate, source, outgoing = call(

time: 105 us -> 100 us (0.952)
  waiting for transfers between devices: 20.6 us -> 13 us
    ppermute x20, waiting for transfers between devices: 20.6 us -> 13 us  [exchange(): return (lax.ppermute(to_even, axis, even), lax.ppermute(to_odd, axis, odd))]
  transfers between devices with their start and end apart: 20 -> 20, of which waited for: 8 -> 7; matrix products, arithmetic and copies ran while one was open for 0% -> 0% of each run, Pallas kernels for 18% -> 19%
where the time goes in v3:
time: 100 us; the launch traced here: 99.1 us
  starting transfers between devices  30.7 us (31%)
  Pallas kernels  25.9 us (26%)
  blocking collectives  24.3 us (24%)
  waiting for transfers between devices  13 us (13%)
  local copies, waits for them, and re-layouts  3.04 us (3%)
  other arithmetic  1.25 us (1%)
  between operations  1 us (1%)
    ppermute x20, starting transfers between devices, exchange(): return (lax.ppermute(to_even, axis, even), lax.ppermute(to_odd, axis, odd))  30.7 us
    all_to_all x1, blocking collectives, shards(): lax.all_to_all(outgoing, 'dev', split_axis=0, concat_axis=0, tiled=True)  13.7 us
    ppermute x20, waiting for transfers between devices, exchange(): return (lax.ppermute(to_even, axis, even), lax.ppermute(to_odd, axis, odd))  13 us
    all_to_all x1, blocking collectives, shards(): lax.all_to_all(owned, 'dev', split_axis=0, concat_axis=0, tiled=True)  10.6 us
    pallas_call x1, Pallas kernels, shards(): call(fine_first, (fine, faces, faces, sds((4, 9, ny, nz), coup_fine.dtype...  4.59 us
    pallas_call x1, Pallas kernels, shards(): call(fine_last, (fine, sds((hx, hy, hz))), in_specs=[VMEM] * 8, out_specs...  4.14 us
    pallas_call x1, Pallas kernels, shards(): call(fine_next, (fine, faces), in_specs=[VMEM] * 8, out_specs=(VMEM,) * 2...  3.71 us
    pallas_call x1, Pallas kernels, shards(): call(mid_rounds, (sds((hx, hy, hz)), sds((qx * qy, qz)), sds((slots, cell...  3.46 us
  transfers between devices with their start and end apart: 20, of which 7 were waited for; matrix products, arithmetic and copies ran while one was open for 0% of the time, Pallas kernels for 19%

profile of v3, /device:TPU:2, one launch (start us, length us, event | category | flops | bytes accessed | tf_op | source)
XLA Modules:
  0.0 99.1 jit_solution(14940273502300671390)
XLA Ops:
  0.7 0.1 stack.27
  0.8 0.1 broadcast_in_dim.124
  0.9 0.8 bitcast_select_fusion
  1.7 5.4 %collective-permute-start.1 = (f32[16,512]{1,0:T(8,128)S(1)}, f32[16,512]{1,0:T(8,128)S(1)}, u32[]{:S(2)}, u32[]{:S(2)}) collective-permute-start(f32[16,512]{1,0:T(8,128)S(1)} %get-tuple-element.156), channel_id=1, source_target_pairs={{0,240},{16,32},{32,16},{48,64},{64,48},{80,96},{96,80},{112,128},... | collective-permute-start | bytes 98312 | tf_op jit(solution)/shard_map/ppermute | solution.py:558
  7.1 1.2 %copy-done.2 = f32[16,16,512]{2,1,0:T(8,128)S(1)} copy-done((f32[16,16,512]{2,1,0:T(8,128)S(1)}, f32[16,16,512]{2,1,0:T(8,128)}, u32[]{:S(2)}) %copy-start.2) | copy-done | bytes 524312
  8.3 1.6 %copy-done.3 = f32[16,16,512]{2,1,0:T(8,128)S(1)} copy-done((f32[16,16,512]{2,1,0:T(8,128)S(1)}, f32[16,16,512]{2,1,0:T(8,128)}, u32[]{:S(2)}) %copy-start.3) | copy-done | bytes 524312
  9.9 0.2 shard_map.120
  10.2 0.6 collective-permute-start.2
  10.9 2.2 %collective-permute-start.3 = (f32[18,512]{1,0:T(8,128)S(1)}, f32[18,512]{1,0:T(8,128)S(1)}, u32[]{:S(2)}, u32[]{:S(2)}) collective-permute-start(f32[18,512]{1,0:T(8,128)S(1)} %get-tuple-element.90), channel_id=1, source_target_pairs={{0,15},{1,2},{2,1},{3,4},{4,3},{5,6},{6,5},{7,8},{8,7},{9,10},{10,... | collective-permute-start | bytes 110600 | tf_op jit(solution)/shard_map/ppermute | solution.py:558
  13.0 4.6 %shard_map.121 = (f32[16,16,512]{2,1,0:T(8,128)S(1)}, f32[4,16,512]{2,1,0:T(8,128)S(1)}, f32[4,16,512]{2,1,0:T(8,128)S(1)}, bf16[4,9,16,512]{3,2,1,0:T(8,128)(2,1)S(1)}) custom-call(s32[6]{0:T(128)S(1)} %get-tuple-element.130._.flags, f32[16,16,512]{2,1,0:T(8,128)S(1)} %get-tuple-element.86.start_ref, f32[16,16,512]{2,1,0:T(8,128)S(1)} %get-tuple-element.87.q_ref, ...), custom_call_target="tpu_custom_call" | custom-call | flops 7864320 | bytes 8912896 | tf_op jit(solution)/shard_map/pallas_call | solution.py:618
  17.6 0.8 shard_map.122
  18.5 0.1 collective-permute-start.4
  18.6 1.1 %collective-permute-start.5 = (f32[16,512]{1,0:T(8,128)S(1)}, f32[16,512]{1,0:T(8,128)S(1)}, u32[]{:S(2)}, u32[]{:S(2)}) collective-permute-start(f32[16,512]{1,0:T(8,128)S(1)} %get-tuple-element.100), channel_id=1, source_target_pairs={{0,240},{16,32},{32,16},{48,64},{64,48},{80,96},{96,80},{112,128},... | collective-permute-start | bytes 98312 | tf_op jit(solution)/shard_map/ppermute | solution.py:558
  19.7 3.7 %shard_map.123 = (f32[16,16,512]{2,1,0:T(8,128)S(1)}, f32[4,16,512]{2,1,0:T(8,128)S(1)}) custom-call(f32[16,16,512]{2,1,0:T(8,128)S(1)} %get-tuple-element.88.v_ref, f32[16,512]{1,0:T(8,128)S(1)} %get-tuple-element.94.xlo, f32[16,512]{1,0:T(8,128)S(1)} %get-tuple-element.95.xhi, f32[16,512]{1,0:T(8,128)S(1)} %get-tuple-element.104.ylo, ...), custom_call_target="tpu_custom_call" | custom-call | flops 7864320 | bytes 8912896 | tf_op jit(solution)/shard_map/pallas_call | solution.py:636
  23.5 0.0 copy-start.7
  23.5 4.0 %collective-permute-start.6 = (f32[18,512]{1,0:T(8,128)S(1)}, f32[18,512]{1,0:T(8,128)S(1)}, u32[]{:S(2)}, u32[]{:S(2)}) collective-permute-start(f32[18,512]{1,0:T(8,128)S(1)} %get-tuple-element.106), channel_id=1, source_target_pairs={{0,1},{1,0},{2,3},{3,2},{4,5},{5,4},{6,7},{7,6},{8,9},{9,8},{10,11... | collective-permute-start | bytes 110600 | tf_op jit(solution)/shard_map/ppermute | solution.py:558
  27.5 0.7 shard_map.124
  28.2 1.3 %collective-permute-done.6.y_even = f32[18,512]{1,0:T(8,128)S(1)} collective-permute-done((f32[18,512]{1,0:T(8,128)S(1)}, f32[18,512]{1,0:T(8,128)S(1)}, u32[]{:S(2)}, u32[]{:S(2)}) %collective-permute-start.6) | collective-permute-done | bytes 36896 | tf_op jit(solution)/shard_map/ppermute | solution.py:558
  29.5 2.0 %collective-permute-done.7.y_odd = f32[18,512]{1,0:T(8,128)S(1)} collective-permute-done((f32[18,512]{1,0:T(8,128)S(1)}, f32[18,512]{1,0:T(8,128)S(1)}, u32[]{:S(2)}, u32[]{:S(2)}) %collective-permute-start.7) | collective-permute-done | bytes 36896 | tf_op jit(solution)/shard_map/ppermute | solution.py:558
  31.6 0.8 shard_map.125
  32.4 0.1 collective-permute-start.8
  32.5 1.7 %collective-permute-start.9 = (f32[16,512]{1,0:T(8,128)S(1)}, f32[16,512]{1,0:T(8,128)S(1)}, u32[]{:S(2)}, u32[]{:S(2)}) collective-permute-start(f32[16,512]{1,0:T(8,128)S(1)} %get-tuple-element.122), channel_id=1, source_target_pairs={{0,240},{16,32},{32,16},{48,64},{64,48},{80,96},{96,80},{112,128},... | collective-permute-start | bytes 98312 | tf_op jit(solution)/shard_map/ppermute | solution.py:558
  34.2 0.2 convert_reduce_fusion
  34.4 0.1 collective-permute-start.12
  34.5 1.4 %collective-permute-start.13 = (f32[55,8,256]{2,1,0:T(8,128)S(1)}, f32[55,8,256]{2,1,0:T(8,128)S(1)}, u32[]{:S(2)}, u32[]{:S(2)}) collective-permute-start(f32[55,8,256]{2,1,0:T(8,128)S(1)} %get-tuple-element.110), channel_id=1, source_target_pairs={{0,240},{16,32},{32,16},{48,64},{64,48},{80,96},{96,80},{112,128},... | collective-permute-start | bytes 1351688 | tf_op jit(solution)/shard_map/ppermute | solution.py:558
  35.9 4.1 %shard_map.126 = (f32[16,16,512]{2,1,0:T(8,128)}, f32[8,8,256]{2,1,0:T(8,128)S(1)}) custom-call(f32[16,16,512]{2,1,0:T(8,128)S(1)} %get-tuple-element.98.v_ref, f32[16,512]{1,0:T(8,128)S(1)} %get-tuple-element.116.xlo, f32[16,512]{1,0:T(8,128)S(1)} %get-tuple-element.117.xhi, f32[16,512]{1,0:T(8,128)S(1)} %get-tuple-element.126.ylo, ...), custom_call_target="tpu_custom_call" | custom-call | flops 1000000 | bytes 1000000 | tf_op jit(solution)/shard_map/pallas_call | solution.py:661
  40.1 3.5 %collective-permute-start.10 = (f32[18,512]{1,0:T(8,128)S(1)}, f32[18,512]{1,0:T(8,128)S(1)}, u32[]{:S(2)}, u32[]{:S(2)}) collective-permute-start(f32[18,512]{1,0:T(8,128)S(1)} %get-tuple-element.128), channel_id=1, source_target_pairs={{0,1},{1,0},{2,3},{3,2},{4,5},{5,4},{6,7},{7,6},{8,9},{9,8},{10,11... | collective-permute-start | bytes 110600 | tf_op jit(solution)/shard_map/ppermute | solution.py:558
  43.6 1.9 %shard_map.127 = (f32[84,8,256]{2,1,0:T(8,128)S(1)}, f32[84,8,256]{2,1,0:T(8,128)S(1)}) custom-call(s32[6]{0:T(128)S(1)} %get-tuple-element.130._.flags, bf16[26,8,8,256]{3,2,1,0:T(8,128)(2,1)S(1)} %copy-done.5, f32[8,8,256]{2,1,0:T(8,128)S(1)} %copy-done.6, f32[55,8,256]{2,1,0:T(8,128)S(1)} %collective-permute-done.12.x_even, ...), custom_call_target="tpu_custom_call" | custom-call | flops 30000001024 | bytes 1000000 | tf_op jit(solution)/shard_map/pallas_call | solution.py:673
  45.6 0.1 collective-permute-done.10.y_even
  45.7 2.0 %collective-permute-done.11.y_odd = f32[18,512]{1,0:T(8,128)S(1)} collective-permute-done((f32[18,512]{1,0:T(8,128)S(1)}, f32[18,512]{1,0:T(8,128)S(1)}, u32[]{:S(2)}, u32[]{:S(2)}) %collective-permute-start.11) | collective-permute-done | bytes 36896 | tf_op jit(solution)/shard_map/ppermute | solution.py:558
  47.7 3.4 %collective-permute-start.18 = (f32[84,8,256]{2,1,0:T(8,128)S(1)}, f32[84,8,256]{2,1,0:T(8,128)S(1)}, u32[]{:S(2)}, u32[]{:S(2)}) collective-permute-start(f32[84,8,256]{2,1,0:T(8,128)S(1)} %get-tuple-element.141), channel_id=1, source_target_pairs={{0,1},{1,0},{2,3},{3,2},{4,5},{5,4},{6,7},{7,6},{8,9},{9,8},{10,11... | collective-permute-start | bytes 2064392 | tf_op jit(solution)/shard_map/ppermute | solution.py:558
  51.1 1.2 %shard_map.128 = (f32[8,8,256]{2,1,0:T(8,128)S(1)}, f32[3,8,256]{2,1,0:T(8,128)S(1)}, f32[3,8,256]{2,1,0:T(8,128)S(1)}) custom-call(s32[6]{0:T(128)S(1)} %get-tuple-element.130._.flags, f32[16,512]{1,0:T(8,128)S(1)} %collective-permute-done.8.x_even, f32[16,512]{1,0:T(8,128)S(1)} %collective-permute-done.9.x_odd, ...), custom_call_target="tpu_custom_call" | custom-call | flops 1000000 | bytes 1000000 | tf_op jit(solution)/shard_map/pallas_call | solution.py:682
  52.3 0.1 collective-permute-start.14
  52.4 1.6 %collective-permute-start.15 = (f32[3,8,256]{2,1,0:T(8,128)S(1)}, f32[3,8,256]{2,1,0:T(8,128)S(1)}, u32[]{:S(2)}, u32[]{:S(2)}) collective-permute-start(f32[3,8,256]{2,1,0:T(8,128)S(1)} %get-tuple-element.139), channel_id=1, source_target_pairs={{0,240},{16,32},{32,16},{48,64},{64,48},{80,96},{96,80},{112,128},... | collective-permute-start | bytes 73736 | tf_op jit(solution)/shard_map/ppermute | solution.py:558
  54.0 2.9 %collective-permute-done.15 = f32[3,8,256]{2,1,0:T(8,128)S(1)} collective-permute-done((f32[3,8,256]{2,1,0:T(8,128)S(1)}, f32[3,8,256]{2,1,0:T(8,128)S(1)}, u32[]{:S(2)}, u32[]{:S(2)}) %collective-permute-start.15) | collective-permute-done | bytes 24608 | tf_op jit(solution)/shard_map/ppermute | solution.py:558
  57.0 2.1 %collective-permute-start.17 = (f32[14,3,256]{2,1,0:T(4,128)S(1)}, f32[14,3,256]{2,1,0:T(4,128)S(1)}, u32[]{:S(2)}, u32[]{:S(2)}) collective-permute-start(f32[14,3,256]{2,1,0:T(4,128)S(1)} %get-tuple-element.158), channel_id=1, source_target_pairs={{0,15},{1,2},{2,1},{3,4},{4,3},{5,6},{6,5},{7,8},{8,7},{9,10},{10,... | collective-permute-start | bytes 129032 | tf_op jit(solution)/shard_map/ppermute | solution.py:558
  59.1 3.3 %collective-permute-start.16 = (f32[14,3,256]{2,1,0:T(4,128)S(1)}, f32[14,3,256]{2,1,0:T(4,128)S(1)}, u32[]{:S(2)}, u32[]{:S(2)}) collective-permute-start(f32[14,3,256]{2,1,0:T(4,128)S(1)} %get-tuple-element.159), channel_id=1, source_target_pairs={{0,1},{1,0},{2,3},{3,2},{4,5},{5,4},{6,7},{7,6},{8,9},{9,8},{10,11... | collective-permute-start | bytes 129032 | tf_op jit(solution)/shard_map/ppermute | solution.py:558
  62.5 3.1 %collective-permute-done.18.y_even = f32[84,8,256]{2,1,0:T(8,128)S(1)} collective-permute-done((f32[84,8,256]{2,1,0:T(8,128)S(1)}, f32[84,8,256]{2,1,0:T(8,128)S(1)}, u32[]{:S(2)}, u32[]{:S(2)}) %collective-permute-start.18) | collective-permute-done | bytes 688160 | tf_op jit(solution)/shard_map/ppermute | solution.py:558
  65.6 1.5 %collective-permute-done.19.y_odd = f32[84,8,256]{2,1,0:T(8,128)S(1)} collective-permute-done((f32[84,8,256]{2,1,0:T(8,128)S(1)}, f32[84,8,256]{2,1,0:T(8,128)S(1)}, u32[]{:S(2)}, u32[]{:S(2)}) %collective-permute-start.19) | collective-permute-done | bytes 688160 | tf_op jit(solution)/shard_map/ppermute | solution.py:558
  67.0 2.2 %shard_map.129 = (bf16[26,12,16,256]{3,2,1,0:T(8,128)(2,1)S(1)}, f32[14,16,256]{2,1,0:T(8,128)S(1)}) custom-call(s32[6]{0:T(128)S(1)} %get-tuple-element.130._.flags, bf16[26,8,8,256]{3,2,1,0:T(8,128)(2,1)S(1)} %copy-done.5, f32[8,8,256]{2,1,0:T(8,128)S(1)} %copy-done.6, f32[55,8,256]{2,1,0:T(8,128)S(1)} %collective-permute-done.12.x_even, ...), custom_call_target="tpu_custom_call" | custom-call | flops 30000001024 | bytes 1000000 | tf_op jit(solution)/shard_map/pallas_call | solution.py:696
  69.2 0.0 copy-start
  69.2 0.0 copy-start.1
  69.2 0.0 copy-start.4
  69.2 3.5 %shard_map.130 = (f32[8,8,256]{2,1,0:T(8,128)}, f32[16,128]{1,0:T(8,128)S(1)}, f32[32,128]{1,0:T(8,128)S(1)}) custom-call(s32[6]{0:T(128)S(1)} %get-tuple-element.130._.flags, s32[16]{0:T(128)S(1)} %multiply_add_fusion.places, f32[14,8,256]{2,1,0:T(8,128)S(1)} %pad_maximum_fusion.fx_ref, f32[14,3,256]{2,1,0:T(4,128)S(1)} %collective-permute-done.16.fy_even, ...), custom_call_target="tpu_custom_call" | custom-call | flops 20000000 | bytes 1000000 | tf_op jit(solution)/shard_map/pallas_call | solution.py:705
  72.7 13.7 %all_to_all.22 = f32[16,2,128]{2,1,0:T(2,128)S(1)} all-to-all(f32[16,2,128]{2,1,0:T(2,128)S(1)} %bitcast.28), channel_id=1, replica_groups=mesh['group'=16,'dev'=16] {'dev'}, dimensions={0} | all-to-all | bytes 32768 | tf_op jit(solution)/shard_map/all_to_all | solution.py:719
  86.4 0.7 shard_map.131
  87.0 10.6 %all_to_all.23 = f32[16,2,128]{2,1,0:T(2,128)S(1)} all-to-all(f32[16,2,128]{2,1,0:T(2,128)S(1)} %bitcast.26), channel_id=1, replica_groups=mesh['group'=16,'dev'=16] {'dev'}, dimensions={0} | all-to-all | bytes 32768 | tf_op jit(solution)/shard_map/all_to_all | solution.py:723
  97.6 1.5 %shard_map.132 = (f32[4,4,128]{2,1,0:T(4,128)}, f32[4,4,128]{2,1,0:T(4,128)}) custom-call(s32[16]{0:T(128)S(1)} %multiply_add_fusion.places, f32[32,128]{1,0:T(8,128)S(1)} %bitcast.27, f32[16,128]{1,0:T(8,128)S(1)} %get-tuple-element.147.src_ref, f32[16,128]{1,0:T(8,128)S(1)} %bitcast.29, bf16[26,16,128]{2,1,0:T(8,128)(2,1)S(1)} %bitcast.24), custom_call_target="tpu_custom_call" | custom-call | flops 1000000 | bytes 1000000 | tf_op jit(solution)/shard_map/pallas_call | solution.py:724
  (50 shorter events, 0.3 us)
Async XLA Ops:
  1.7 8.4 %collective-permute-start.1 = (f32[16,512]{1,0:T(8,128)S(1)}, f32[16,512]{1,0:T(8,128)S(1)}, u32[]{:S(2)}, u32[]{:S(2)}) collective-permute-start(f32[16,512]{1,0:T(8,128)S(1)} %get-tuple-element.156), channel_id=1, source_target_pairs={{0,240},{16,32},{32,16},{48,64},{64,48},{80,96},{96,80},{112,128},... | collective-permute-start | bytes 98312 | tf_op jit(solution)/shard_map/ppermute | solution.py:558
  7.1 5.9 %slice-start = ((s8[6815744]{0:T(1024)(128)(4,1)}), s8[4194304]{0:T(1024)(128)(4,1)S(1)}, s32[]{:S(2)}) async-start(s8[6815744]{0:T(1024)(128)(4,1)} %bitcast.21), calls=%async_computation.2 | async-start | bytes 8388608
  7.1 5.9 %slice-start.1 = ((s8[6815744]{0:T(1024)(128)(4,1)}), s8[2621440]{0:T(1024)(128)(4,1)S(1)}, s32[]{:S(2)}) async-start(s8[6815744]{0:T(1024)(128)(4,1)} %bitcast.21), calls=%async_computation.3 | async-start | bytes 5242880
  7.1 3.0 %collective-permute-start = (f32[16,512]{1,0:T(8,128)S(1)}, f32[16,512]{1,0:T(8,128)S(1)}, u32[]{:S(2)}, u32[]{:S(2)}) collective-permute-start(f32[16,512]{1,0:T(8,128)S(1)} %get-tuple-element.157), channel_id=1, source_target_pairs={{0,16},{16,0},{32,48},{48,32},{64,80},{80,64},{96,112},{112,96},{1... | collective-permute-start | bytes 98312 | tf_op jit(solution)/shard_map/ppermute | solution.py:558
  7.1 1.2 %copy-start.2 = (f32[16,16,512]{2,1,0:T(8,128)S(1)}, f32[16,16,512]{2,1,0:T(8,128)}, u32[]{:S(2)}) copy-start(f32[16,16,512]{2,1,0:T(8,128)} %f_ref.1) | copy-start | bytes 1572868
  8.3 1.6 %copy-start.3 = (f32[16,16,512]{2,1,0:T(8,128)S(1)}, f32[16,16,512]{2,1,0:T(8,128)}, u32[]{:S(2)}) copy-start(f32[16,16,512]{2,1,0:T(8,128)} %d_ref.4) | copy-start | bytes 1572868
  10.2 7.4 %collective-permute-start.2 = (f32[18,512]{1,0:T(8,128)S(1)}, f32[18,512]{1,0:T(8,128)S(1)}, u32[]{:S(2)}, u32[]{:S(2)}) collective-permute-start(f32[18,512]{1,0:T(8,128)S(1)} %get-tuple-element.89), channel_id=1, source_target_pairs={{0,1},{1,0},{2,3},{3,2},{4,5},{5,4},{6,7},{7,6},{8,9},{9,8},{10,11... | collective-permute-start | bytes 110600 | tf_op jit(solution)/shard_map/ppermute | solution.py:558
  10.9 6.8 %collective-permute-start.3 = (f32[18,512]{1,0:T(8,128)S(1)}, f32[18,512]{1,0:T(8,128)S(1)}, u32[]{:S(2)}, u32[]{:S(2)}) collective-permute-start(f32[18,512]{1,0:T(8,128)S(1)} %get-tuple-element.90), channel_id=1, source_target_pairs={{0,15},{1,2},{2,1},{3,4},{4,3},{5,6},{6,5},{7,8},{8,7},{9,10},{10,... | collective-permute-start | bytes 110600 | tf_op jit(solution)/shard_map/ppermute | solution.py:558
  18.5 4.9 %collective-permute-start.4 = (f32[16,512]{1,0:T(8,128)S(1)}, f32[16,512]{1,0:T(8,128)S(1)}, u32[]{:S(2)}, u32[]{:S(2)}) collective-permute-start(f32[16,512]{1,0:T(8,128)S(1)} %get-tuple-element.99), channel_id=1, source_target_pairs={{0,16},{16,0},{32,48},{48,32},{64,80},{80,64},{96,112},{112,96},{1... | collective-permute-start | bytes 98312 | tf_op jit(solution)/shard_map/ppermute | solution.py:558
  18.6 4.8 %collective-permute-start.5 = (f32[16,512]{1,0:T(8,128)S(1)}, f32[16,512]{1,0:T(8,128)S(1)}, u32[]{:S(2)}, u32[]{:S(2)}) collective-permute-start(f32[16,512]{1,0:T(8,128)S(1)} %get-tuple-element.100), channel_id=1, source_target_pairs={{0,240},{16,32},{32,16},{48,64},{64,48},{80,96},{96,80},{112,128},... | collective-permute-start | bytes 98312 | tf_op jit(solution)/shard_map/ppermute | solution.py:558
  19.7 7.8 %copy-start.5 = (bf16[26,8,8,256]{3,2,1,0:T(8,128)(2,1)S(1)}, bf16[26,8,8,256]{3,2,1,0:T(8,128)(2,1)}, u32[]{:S(2)}) copy-start(bf16[26,8,8,256]{3,2,1,0:T(8,128)(2,1)} %w_ref.11) | copy-start | bytes 2555908
  19.7 7.8 %copy-start.6 = (f32[8,8,256]{2,1,0:T(8,128)S(1)}, f32[8,8,256]{2,1,0:T(8,128)}, u32[]{:S(2)}) copy-start(f32[8,8,256]{2,1,0:T(8,128)} %d_ref.7) | copy-start | bytes 196612
  23.5 10.7 %copy-start.7 = (s32[1,1,16,1]{2,3,1,0:T(1,128)S(1)}, s32[1,1,16,1]{2,3,1,0:T(1,128)}, u32[]{:S(2)}) copy-start(s32[1,1,16,1]{2,3,1,0:T(1,128)} %param.16) | copy-start | bytes 196
  23.5 6.0 %collective-permute-start.6 = (f32[18,512]{1,0:T(8,128)S(1)}, f32[18,512]{1,0:T(8,128)S(1)}, u32[]{:S(2)}, u32[]{:S(2)}) collective-permute-start(f32[18,512]{1,0:T(8,128)S(1)} %get-tuple-element.106), channel_id=1, source_target_pairs={{0,1},{1,0},{2,3},{3,2},{4,5},{5,4},{6,7},{7,6},{8,9},{9,8},{10,11... | collective-permute-start | bytes 110600 | tf_op jit(solution)/shard_map/ppermute | solution.py:558
  27.5 4.1 %collective-permute-start.7 = (f32[18,512]{1,0:T(8,128)S(1)}, f32[18,512]{1,0:T(8,128)S(1)}, u32[]{:S(2)}, u32[]{:S(2)}) collective-permute-start(f32[18,512]{1,0:T(8,128)S(1)} %get-tuple-element.107), channel_id=1, source_target_pairs={{0,15},{1,2},{2,1},{3,4},{4,3},{5,6},{6,5},{7,8},{8,7},{9,10},{10,... | collective-permute-start | bytes 110600 | tf_op jit(solution)/shard_map/ppermute | solution.py:558
  32.4 7.6 %collective-permute-start.8 = (f32[16,512]{1,0:T(8,128)S(1)}, f32[16,512]{1,0:T(8,128)S(1)}, u32[]{:S(2)}, u32[]{:S(2)}) collective-permute-start(f32[16,512]{1,0:T(8,128)S(1)} %get-tuple-element.121), channel_id=1, source_target_pairs={{0,16},{16,0},{32,48},{48,32},{64,80},{80,64},{96,112},{112,96},{1... | collective-permute-start | bytes 98312 | tf_op jit(solution)/shard_map/ppermute | solution.py:558
  32.5 7.6 %collective-permute-start.9 = (f32[16,512]{1,0:T(8,128)S(1)}, f32[16,512]{1,0:T(8,128)S(1)}, u32[]{:S(2)}, u32[]{:S(2)}) collective-permute-start(f32[16,512]{1,0:T(8,128)S(1)} %get-tuple-element.122), channel_id=1, source_target_pairs={{0,240},{16,32},{32,16},{48,64},{64,48},{80,96},{96,80},{112,128},... | collective-permute-start | bytes 98312 | tf_op jit(solution)/shard_map/ppermute | solution.py:558
  34.4 9.3 %collective-permute-start.12 = (f32[55,8,256]{2,1,0:T(8,128)S(1)}, f32[55,8,256]{2,1,0:T(8,128)S(1)}, u32[]{:S(2)}, u32[]{:S(2)}) collective-permute-start(f32[55,8,256]{2,1,0:T(8,128)S(1)} %get-tuple-element.109), channel_id=1, source_target_pairs={{0,16},{16,0},{32,48},{48,32},{64,80},{80,64},{96,112},{112,96},{1... | collective-permute-start | bytes 1351688 | tf_op jit(solution)/shard_map/ppermute | solution.py:558
  34.5 9.2 %collective-permute-start.13 = (f32[55,8,256]{2,1,0:T(8,128)S(1)}, f32[55,8,256]{2,1,0:T(8,128)S(1)}, u32[]{:S(2)}, u32[]{:S(2)}) collective-permute-start(f32[55,8,256]{2,1,0:T(8,128)S(1)} %get-tuple-element.110), channel_id=1, source_target_pairs={{0,240},{16,32},{32,16},{48,64},{64,48},{80,96},{96,80},{112,128},... | collective-permute-start | bytes 1351688 | tf_op jit(solution)/shard_map/ppermute | solution.py:558
  40.1 5.6 %collective-permute-start.10 = (f32[18,512]{1,0:T(8,128)S(1)}, f32[18,512]{1,0:T(8,128)S(1)}, u32[]{:S(2)}, u32[]{:S(2)}) collective-permute-start(f32[18,512]{1,0:T(8,128)S(1)} %get-tuple-element.128), channel_id=1, source_target_pairs={{0,1},{1,0},{2,3},{3,2},{4,5},{5,4},{6,7},{7,6},{8,9},{9,8},{10,11... | collective-permute-start | bytes 110600 | tf_op jit(solution)/shard_map/ppermute | solution.py:558
  43.6 4.1 %collective-permute-start.11 = (f32[18,512]{1,0:T(8,128)S(1)}, f32[18,512]{1,0:T(8,128)S(1)}, u32[]{:S(2)}, u32[]{:S(2)}) collective-permute-start(f32[18,512]{1,0:T(8,128)S(1)} %get-tuple-element.129), channel_id=1, source_target_pairs={{0,15},{1,2},{2,1},{3,4},{4,3},{5,6},{6,5},{7,8},{8,7},{9,10},{10,... | collective-permute-start | bytes 110600 | tf_op jit(solution)/shard_map/ppermute | solution.py:558
  47.7 17.8 %collective-permute-start.18 = (f32[84,8,256]{2,1,0:T(8,128)S(1)}, f32[84,8,256]{2,1,0:T(8,128)S(1)}, u32[]{:S(2)}, u32[]{:S(2)}) collective-permute-start(f32[84,8,256]{2,1,0:T(8,128)S(1)} %get-tuple-element.141), channel_id=1, source_target_pairs={{0,1},{1,0},{2,3},{3,2},{4,5},{5,4},{6,7},{7,6},{8,9},{9,8},{10,11... | collective-permute-start | bytes 2064392 | tf_op jit(solution)/shard_map/ppermute | solution.py:558
  51.1 15.9 %collective-permute-start.19 = (f32[84,8,256]{2,1,0:T(8,128)S(1)}, f32[84,8,256]{2,1,0:T(8,128)S(1)}, u32[]{:S(2)}, u32[]{:S(2)}) collective-permute-start(f32[84,8,256]{2,1,0:T(8,128)S(1)} %get-tuple-element.142), channel_id=1, source_target_pairs={{0,15},{1,2},{2,1},{3,4},{4,3},{5,6},{6,5},{7,8},{8,7},{9,10},{10,... | collective-permute-start | bytes 2064392 | tf_op jit(solution)/shard_map/ppermute | solution.py:558
  52.3 1.7 %collective-permute-start.14 = (f32[3,8,256]{2,1,0:T(8,128)S(1)}, f32[3,8,256]{2,1,0:T(8,128)S(1)}, u32[]{:S(2)}, u32[]{:S(2)}) collective-permute-start(f32[3,8,256]{2,1,0:T(8,128)S(1)} %get-tuple-element.138), channel_id=1, source_target_pairs={{0,16},{16,0},{32,48},{48,32},{64,80},{80,64},{96,112},{112,96},{1... | collective-permute-start | bytes 73736 | tf_op jit(solution)/shard_map/ppermute | solution.py:558
  52.4 4.5 %collective-permute-start.15 = (f32[3,8,256]{2,1,0:T(8,128)S(1)}, f32[3,8,256]{2,1,0:T(8,128)S(1)}, u32[]{:S(2)}, u32[]{:S(2)}) collective-permute-start(f32[3,8,256]{2,1,0:T(8,128)S(1)} %get-tuple-element.139), channel_id=1, source_target_pairs={{0,240},{16,32},{32,16},{48,64},{64,48},{80,96},{96,80},{112,128},... | collective-permute-start | bytes 73736 | tf_op jit(solution)/shard_map/ppermute | solution.py:558
  57.0 12.2 %collective-permute-start.17 = (f32[14,3,256]{2,1,0:T(4,128)S(1)}, f32[14,3,256]{2,1,0:T(4,128)S(1)}, u32[]{:S(2)}, u32[]{:S(2)}) collective-permute-start(f32[14,3,256]{2,1,0:T(4,128)S(1)} %get-tuple-element.158), channel_id=1, source_target_pairs={{0,15},{1,2},{2,1},{3,4},{4,3},{5,6},{6,5},{7,8},{8,7},{9,10},{10,... | collective-permute-start | bytes 129032 | tf_op jit(solution)/shard_map/ppermute | solution.py:558
  59.1 10.1 %collective-permute-start.16 = (f32[14,3,256]{2,1,0:T(4,128)S(1)}, f32[14,3,256]{2,1,0:T(4,128)S(1)}, u32[]{:S(2)}, u32[]{:S(2)}) collective-permute-start(f32[14,3,256]{2,1,0:T(4,128)S(1)} %get-tuple-element.159), channel_id=1, source_target_pairs={{0,1},{1,0},{2,3},{3,2},{4,5},{5,4},{6,7},{7,6},{8,9},{9,8},{10,11... | collective-permute-start | bytes 129032 | tf_op jit(solution)/shard_map/ppermute | solution.py:558
  69.2 17.2 %copy-start = (f32[1,1,32,128,128]{4,3,2,1,0:T(8,128)S(1)}, f32[1,1,32,128,128]{4,3,2,1,0:T(8,128)}, u32[]{:S(2)}) copy-start(f32[1,1,32,128,128]{4,3,2,1,0:T(8,128)} %param.17) | copy-start | bytes 6291460
  69.2 28.4 %copy-start.1 = (bf16[26,4,4,128]{3,2,1,0:T(4,128)(2,1)S(1)}, bf16[26,4,4,128]{3,2,1,0:T(4,128)(2,1)}, u32[]{:S(2)}) copy-start(bf16[26,4,4,128]{3,2,1,0:T(4,128)(2,1)} %param.15) | copy-start | bytes 319492
  69.2 28.4 %copy-start.4 = (f32[4,4,128]{2,1,0:T(4,128)S(1)}, f32[4,4,128]{2,1,0:T(4,128)}, u32[]{:S(2)}) copy-start(f32[4,4,128]{2,1,0:T(4,128)} %param.14) | copy-start | bytes 24580

commit v4 on v3

--- a/solution.py
+++ b/solution.py
@@ -677,7 +677,9 @@
         out_specs=(VMEM,) * 2,
         flops=LONG,
     )(late, coup_mid, diag_mid, *wx)
-    halo, wy = lax.optimization_barrier((halo, wy))
+    *ends, y_even, y_odd = halo
+    y_even, wy = lax.optimization_barrier((y_even, wy))
+    halo = (*ends, y_even, y_odd)
     wy = exchange("dev", *wy)
     f_mid, fx_even, fx_odd = call(
         fine_halo_last,

time: 100 us -> 99.2 us (level)
  no operation moved by 1% of the time
where the time goes in v4:
time: 99.2 us; the launch traced here: 98.9 us
  starting transfers between devices  30.4 us (31%)
  Pallas kernels  25.9 us (26%)
  blocking collectives  24.5 us (25%)
  waiting for transfers between devices  12.7 us (13%)
  local copies, waits for them, and re-layouts  3.04 us (3%)
  other arithmetic  1.25 us (1%)
  between operations  1 us (1%)
    ppermute x20, starting transfers between devices, exchange(): return (lax.ppermute(to_even, axis, even), lax.ppermute(to_odd, axis, odd))  30.4 us
    all_to_all x1, blocking collectives, shards(): lax.all_to_all(outgoing, 'dev', split_axis=0, concat_axis=0, tiled=True)  14 us
    ppermute x20, waiting for transfers between devices, exchange(): return (lax.ppermute(to_even, axis, even), lax.ppermute(to_odd, axis, odd))  12.7 us
    all_to_all x1, blocking collectives, shards(): lax.all_to_all(owned, 'dev', split_axis=0, concat_axis=0, tiled=True)  10.6 us
    pallas_call x1, Pallas kernels, shards(): call(fine_first, (fine, faces, faces, sds((4, 9, ny, nz), coup_fine.dtype...  4.59 us
    pallas_call x1, Pallas kernels, shards(): call(fine_last, (fine, sds((hx, hy, hz))), in_specs=[VMEM] * 8, out_specs...  4.14 us
    pallas_call x1, Pallas kernels, shards(): call(fine_next, (fine, faces), in_specs=[VMEM] * 8, out_specs=(VMEM,) * 2...  3.71 us
    pallas_call x1, Pallas kernels, shards(): call(mid_rounds, (sds((hx, hy, hz)), sds((qx * qy, qz)), sds((slots, cell...  3.46 us
  transfers between devices with their start and end apart: 20, of which 7 were waited for; matrix products, arithmetic and copies ran while one was open for 0% of the time, Pallas kernels for 19%

profile of v4, /device:TPU:2, one launch (start us, length us, event | category | flops | bytes accessed | tf_op | source)
XLA Modules:
  0.0 98.9 jit_solution(10011764501298283800)
XLA Ops:
  0.7 0.1 stack.27
  0.8 0.1 broadcast_in_dim.124
  0.9 0.8 bitcast_select_fusion
  1.7 5.4 %collective-permute-start.1 = (f32[16,512]{1,0:T(8,128)S(1)}, f32[16,512]{1,0:T(8,128)S(1)}, u32[]{:S(2)}, u32[]{:S(2)}) collective-permute-start(f32[16,512]{1,0:T(8,128)S(1)} %get-tuple-element.150), channel_id=1, source_target_pairs={{0,240},{16,32},{32,16},{48,64},{64,48},{80,96},{96,80},{112,128},... | collective-permute-start | bytes 98312 | tf_op jit(solution)/shard_map/ppermute | solution.py:558
  7.1 1.2 %copy-done.2 = f32[16,16,512]{2,1,0:T(8,128)S(1)} copy-done((f32[16,16,512]{2,1,0:T(8,128)S(1)}, f32[16,16,512]{2,1,0:T(8,128)}, u32[]{:S(2)}) %copy-start.2) | copy-done | bytes 524312
  8.3 1.6 %copy-done.3 = f32[16,16,512]{2,1,0:T(8,128)S(1)} copy-done((f32[16,16,512]{2,1,0:T(8,128)S(1)}, f32[16,16,512]{2,1,0:T(8,128)}, u32[]{:S(2)}) %copy-start.3) | copy-done | bytes 524312
  9.9 0.2 shard_map.120
  10.2 0.6 collective-permute-start.2
  10.9 2.2 %collective-permute-start.3 = (f32[18,512]{1,0:T(8,128)S(1)}, f32[18,512]{1,0:T(8,128)S(1)}, u32[]{:S(2)}, u32[]{:S(2)}) collective-permute-start(f32[18,512]{1,0:T(8,128)S(1)} %get-tuple-element.87), channel_id=1, source_target_pairs={{0,15},{1,2},{2,1},{3,4},{4,3},{5,6},{6,5},{7,8},{8,7},{9,10},{10,... | collective-permute-start | bytes 110600 | tf_op jit(solution)/shard_map/ppermute | solution.py:558
  13.0 4.6 %shard_map.121 = (f32[16,16,512]{2,1,0:T(8,128)S(1)}, f32[4,16,512]{2,1,0:T(8,128)S(1)}, f32[4,16,512]{2,1,0:T(8,128)S(1)}, bf16[4,9,16,512]{3,2,1,0:T(8,128)(2,1)S(1)}) custom-call(s32[6]{0:T(128)S(1)} %get-tuple-element.126._.flags, f32[16,16,512]{2,1,0:T(8,128)S(1)} %get-tuple-element.83.start_ref, f32[16,16,512]{2,1,0:T(8,128)S(1)} %get-tuple-element.84.q_ref, ...), custom_call_target="tpu_custom_call" | custom-call | flops 7864320 | bytes 8912896 | tf_op jit(solution)/shard_map/pallas_call | solution.py:618
  17.6 0.8 shard_map.122
  18.5 0.1 collective-permute-start.4
  18.6 1.1 %collective-permute-start.5 = (f32[16,512]{1,0:T(8,128)S(1)}, f32[16,512]{1,0:T(8,128)S(1)}, u32[]{:S(2)}, u32[]{:S(2)}) collective-permute-start(f32[16,512]{1,0:T(8,128)S(1)} %get-tuple-element.97), channel_id=1, source_target_pairs={{0,240},{16,32},{32,16},{48,64},{64,48},{80,96},{96,80},{112,128},... | collective-permute-start | bytes 98312 | tf_op jit(solution)/shard_map/ppermute | solution.py:558
  19.7 3.7 %shard_map.123 = (f32[16,16,512]{2,1,0:T(8,128)S(1)}, f32[4,16,512]{2,1,0:T(8,128)S(1)}) custom-call(f32[16,16,512]{2,1,0:T(8,128)S(1)} %get-tuple-element.85.v_ref, f32[16,512]{1,0:T(8,128)S(1)} %get-tuple-element.91.xlo, f32[16,512]{1,0:T(8,128)S(1)} %get-tuple-element.92.xhi, f32[16,512]{1,0:T(8,128)S(1)} %get-tuple-element.101.ylo, ...), custom_call_target="tpu_custom_call" | custom-call | flops 7864320 | bytes 8912896 | tf_op jit(solution)/shard_map/pallas_call | solution.py:636
  23.5 0.0 copy-start.7
  23.5 4.0 %collective-permute-start.6 = (f32[18,512]{1,0:T(8,128)S(1)}, f32[18,512]{1,0:T(8,128)S(1)}, u32[]{:S(2)}, u32[]{:S(2)}) collective-permute-start(f32[18,512]{1,0:T(8,128)S(1)} %get-tuple-element.103), channel_id=1, source_target_pairs={{0,1},{1,0},{2,3},{3,2},{4,5},{5,4},{6,7},{7,6},{8,9},{9,8},{10,11... | collective-permute-start | bytes 110600 | tf_op jit(solution)/shard_map/ppermute | solution.py:558
  27.5 0.7 shard_map.124
  28.2 1.3 %collective-permute-done.6.y_even = f32[18,512]{1,0:T(8,128)S(1)} collective-permute-done((f32[18,512]{1,0:T(8,128)S(1)}, f32[18,512]{1,0:T(8,128)S(1)}, u32[]{:S(2)}, u32[]{:S(2)}) %collective-permute-start.6) | collective-permute-done | bytes 36896 | tf_op jit(solution)/shard_map/ppermute | solution.py:558
  29.5 2.0 %collective-permute-done.7.y_odd = f32[18,512]{1,0:T(8,128)S(1)} collective-permute-done((f32[18,512]{1,0:T(8,128)S(1)}, f32[18,512]{1,0:T(8,128)S(1)}, u32[]{:S(2)}, u32[]{:S(2)}) %collective-permute-start.7) | collective-permute-done | bytes 36896 | tf_op jit(solution)/shard_map/ppermute | solution.py:558
  31.6 0.8 shard_map.125
  32.4 0.1 collective-permute-start.8
  32.5 1.7 %collective-permute-start.9 = (f32[16,512]{1,0:T(8,128)S(1)}, f32[16,512]{1,0:T(8,128)S(1)}, u32[]{:S(2)}, u32[]{:S(2)}) collective-permute-start(f32[16,512]{1,0:T(8,128)S(1)} %get-tuple-element.119), channel_id=1, source_target_pairs={{0,240},{16,32},{32,16},{48,64},{64,48},{80,96},{96,80},{112,128},... | collective-permute-start | bytes 98312 | tf_op jit(solution)/shard_map/ppermute | solution.py:558
  34.2 0.2 convert_reduce_fusion
  34.4 0.1 collective-permute-start.11
  34.5 1.4 %collective-permute-start.12 = (f32[55,8,256]{2,1,0:T(8,128)S(1)}, f32[55,8,256]{2,1,0:T(8,128)S(1)}, u32[]{:S(2)}, u32[]{:S(2)}) collective-permute-start(f32[55,8,256]{2,1,0:T(8,128)S(1)} %get-tuple-element.107), channel_id=1, source_target_pairs={{0,240},{16,32},{32,16},{48,64},{64,48},{80,96},{96,80},{112,128},... | collective-permute-start | bytes 1351688 | tf_op jit(solution)/shard_map/ppermute | solution.py:558
  35.9 4.1 %shard_map.126 = (f32[16,16,512]{2,1,0:T(8,128)}, f32[8,8,256]{2,1,0:T(8,128)S(1)}) custom-call(f32[16,16,512]{2,1,0:T(8,128)S(1)} %get-tuple-element.95.v_ref, f32[16,512]{1,0:T(8,128)S(1)} %get-tuple-element.113.xlo, f32[16,512]{1,0:T(8,128)S(1)} %get-tuple-element.114.xhi, f32[16,512]{1,0:T(8,128)S(1)} %get-tuple-element.123.ylo, ...), custom_call_target="tpu_custom_call" | custom-call | flops 1000000 | bytes 1000000 | tf_op jit(solution)/shard_map/pallas_call | solution.py:661
  40.1 3.5 %collective-permute-start.10 = (f32[18,512]{1,0:T(8,128)S(1)}, f32[18,512]{1,0:T(8,128)S(1)}, u32[]{:S(2)}, u32[]{:S(2)}) collective-permute-start(f32[18,512]{1,0:T(8,128)S(1)} %get-tuple-element.125), channel_id=1, source_target_pairs={{0,1},{1,0},{2,3},{3,2},{4,5},{5,4},{6,7},{7,6},{8,9},{9,8},{10,11... | collective-permute-start | bytes 110600 | tf_op jit(solution)/shard_map/ppermute | solution.py:558
  43.6 1.9 %shard_map.127 = (f32[84,8,256]{2,1,0:T(8,128)S(1)}, f32[84,8,256]{2,1,0:T(8,128)S(1)}) custom-call(s32[6]{0:T(128)S(1)} %get-tuple-element.126._.flags, bf16[26,8,8,256]{3,2,1,0:T(8,128)(2,1)S(1)} %copy-done.5, f32[8,8,256]{2,1,0:T(8,128)S(1)} %copy-done.6, f32[55,8,256]{2,1,0:T(8,128)S(1)} %collective-permute-done.11.x_even, ...), custom_call_target="tpu_custom_call" | custom-call | flops 30000001024 | bytes 1000000 | tf_op jit(solution)/shard_map/pallas_call | solution.py:673
  45.6 0.1 collective-permute-done.10.y_even
  45.7 3.6 %collective-permute-start.18 = (f32[84,8,256]{2,1,0:T(8,128)S(1)}, f32[84,8,256]{2,1,0:T(8,128)S(1)}, u32[]{:S(2)}, u32[]{:S(2)}) collective-permute-start(f32[84,8,256]{2,1,0:T(8,128)S(1)} %get-tuple-element.135), channel_id=1, source_target_pairs={{0,1},{1,0},{2,3},{3,2},{4,5},{5,4},{6,7},{7,6},{8,9},{9,8},{10,11... | collective-permute-start | bytes 2064392 | tf_op jit(solution)/shard_map/ppermute | solution.py:558
  49.3 1.2 %shard_map.128 = (f32[8,8,256]{2,1,0:T(8,128)S(1)}, f32[3,8,256]{2,1,0:T(8,128)S(1)}, f32[3,8,256]{2,1,0:T(8,128)S(1)}) custom-call(s32[6]{0:T(128)S(1)} %get-tuple-element.126._.flags, f32[16,512]{1,0:T(8,128)S(1)} %collective-permute-done.8.x_even, f32[16,512]{1,0:T(8,128)S(1)} %collective-permute-done.9.x_odd, ...), custom_call_target="tpu_custom_call" | custom-call | flops 1000000 | bytes 1000000 | tf_op jit(solution)/shard_map/pallas_call | solution.py:684
  50.5 0.1 collective-permute-start.14
  50.6 0.9 collective-permute-start.15
  51.5 0.3 collective-permute-done.14
  51.8 3.4 %collective-permute-done.15 = f32[3,8,256]{2,1,0:T(8,128)S(1)} collective-permute-done((f32[3,8,256]{2,1,0:T(8,128)S(1)}, f32[3,8,256]{2,1,0:T(8,128)S(1)}, u32[]{:S(2)}, u32[]{:S(2)}) %collective-permute-start.15) | collective-permute-done | bytes 24608 | tf_op jit(solution)/shard_map/ppermute | solution.py:558
  55.2 2.1 %collective-permute-start.17 = (f32[14,3,256]{2,1,0:T(4,128)S(1)}, f32[14,3,256]{2,1,0:T(4,128)S(1)}, u32[]{:S(2)}, u32[]{:S(2)}) collective-permute-start(f32[14,3,256]{2,1,0:T(4,128)S(1)} %get-tuple-element.152), channel_id=1, source_target_pairs={{0,15},{1,2},{2,1},{3,4},{4,3},{5,6},{6,5},{7,8},{8,7},{9,10},{10,... | collective-permute-start | bytes 129032 | tf_op jit(solution)/shard_map/ppermute | solution.py:558
  57.3 3.6 %collective-permute-start.16 = (f32[14,3,256]{2,1,0:T(4,128)S(1)}, f32[14,3,256]{2,1,0:T(4,128)S(1)}, u32[]{:S(2)}, u32[]{:S(2)}) collective-permute-start(f32[14,3,256]{2,1,0:T(4,128)S(1)} %get-tuple-element.153), channel_id=1, source_target_pairs={{0,1},{1,0},{2,3},{3,2},{4,5},{5,4},{6,7},{7,6},{8,9},{9,8},{10,11... | collective-permute-start | bytes 129032 | tf_op jit(solution)/shard_map/ppermute | solution.py:558
  60.9 4.1 %collective-permute-done.18.y_even = f32[84,8,256]{2,1,0:T(8,128)S(1)} collective-permute-done((f32[84,8,256]{2,1,0:T(8,128)S(1)}, f32[84,8,256]{2,1,0:T(8,128)S(1)}, u32[]{:S(2)}, u32[]{:S(2)}) %collective-permute-start.18) | collective-permute-done | bytes 688160 | tf_op jit(solution)/shard_map/ppermute | solution.py:558
  65.0 1.5 %collective-permute-done.19.y_odd = f32[84,8,256]{2,1,0:T(8,128)S(1)} collective-permute-done((f32[84,8,256]{2,1,0:T(8,128)S(1)}, f32[84,8,256]{2,1,0:T(8,128)S(1)}, u32[]{:S(2)}, u32[]{:S(2)}) %collective-permute-start.19) | collective-permute-done | bytes 688160 | tf_op jit(solution)/shard_map/ppermute | solution.py:558
  66.5 2.2 %shard_map.129 = (bf16[26,12,16,256]{3,2,1,0:T(8,128)(2,1)S(1)}, f32[14,16,256]{2,1,0:T(8,128)S(1)}) custom-call(s32[6]{0:T(128)S(1)} %get-tuple-element.126._.flags, bf16[26,8,8,256]{3,2,1,0:T(8,128)(2,1)S(1)} %copy-done.5, f32[8,8,256]{2,1,0:T(8,128)S(1)} %copy-done.6, f32[55,8,256]{2,1,0:T(8,128)S(1)} %collective-permute-done.11.x_even, ...), custom_call_target="tpu_custom_call" | custom-call | flops 30000001024 | bytes 1000000 | tf_op jit(solution)/shard_map/pallas_call | solution.py:698
  68.7 0.0 copy-start
  68.7 0.0 copy-start.1
  68.7 0.0 copy-start.4
  68.7 3.5 %shard_map.130 = (f32[8,8,256]{2,1,0:T(8,128)}, f32[16,128]{1,0:T(8,128)S(1)}, f32[32,128]{1,0:T(8,128)S(1)}) custom-call(s32[6]{0:T(128)S(1)} %get-tuple-element.126._.flags, s32[16]{0:T(128)S(1)} %multiply_add_fusion.places, f32[14,8,256]{2,1,0:T(8,128)S(1)} %pad_maximum_fusion.fx_ref, f32[14,3,256]{2,1,0:T(4,128)S(1)} %collective-permute-done.16.fy_even, ...), custom_call_target="tpu_custom_call" | custom-call | flops 20000000 | bytes 1000000 | tf_op jit(solution)/shard_map/pallas_call | solution.py:707
  72.2 14.0 %all_to_all.22 = f32[16,2,128]{2,1,0:T(2,128)S(1)} all-to-all(f32[16,2,128]{2,1,0:T(2,128)S(1)} %bitcast.28), channel_id=1, replica_groups=mesh['group'=16,'dev'=16] {'dev'}, dimensions={0} | all-to-all | bytes 32768 | tf_op jit(solution)/shard_map/all_to_all | solution.py:721
  86.1 0.7 shard_map.131
  86.8 10.6 %all_to_all.23 = f32[16,2,128]{2,1,0:T(2,128)S(1)} all-to-all(f32[16,2,128]{2,1,0:T(2,128)S(1)} %bitcast.26), channel_id=1, replica_groups=mesh['group'=16,'dev'=16] {'dev'}, dimensions={0} | all-to-all | bytes 32768 | tf_op jit(solution)/shard_map/all_to_all | solution.py:725
  97.4 1.5 %shard_map.132 = (f32[4,4,128]{2,1,0:T(4,128)}, f32[4,4,128]{2,1,0:T(4,128)}) custom-call(s32[16]{0:T(128)S(1)} %multiply_add_fusion.places, f32[32,128]{1,0:T(8,128)S(1)} %bitcast.27, f32[16,128]{1,0:T(8,128)S(1)} %get-tuple-element.141.src_ref, f32[16,128]{1,0:T(8,128)S(1)} %bitcast.29, bf16[26,16,128]{2,1,0:T(8,128)(2,1)S(1)} %bitcast.24), custom_call_target="tpu_custom_call" | custom-call | flops 1000000 | bytes 1000000 | tf_op jit(solution)/shard_map/pallas_call | solution.py:726
  (50 shorter events, 0.3 us)
Async XLA Ops:
  1.7 8.4 %collective-permute-start.1 = (f32[16,512]{1,0:T(8,128)S(1)}, f32[16,512]{1,0:T(8,128)S(1)}, u32[]{:S(2)}, u32[]{:S(2)}) collective-permute-start(f32[16,512]{1,0:T(8,128)S(1)} %get-tuple-element.150), channel_id=1, source_target_pairs={{0,240},{16,32},{32,16},{48,64},{64,48},{80,96},{96,80},{112,128},... | collective-permute-start | bytes 98312 | tf_op jit(solution)/shard_map/ppermute | solution.py:558
  7.1 5.9 %slice-start = ((s8[6815744]{0:T(1024)(128)(4,1)}), s8[4194304]{0:T(1024)(128)(4,1)S(1)}, s32[]{:S(2)}) async-start(s8[6815744]{0:T(1024)(128)(4,1)} %bitcast.21), calls=%async_computation.2 | async-start | bytes 8388608
  7.1 5.9 %slice-start.1 = ((s8[6815744]{0:T(1024)(128)(4,1)}), s8[2621440]{0:T(1024)(128)(4,1)S(1)}, s32[]{:S(2)}) async-start(s8[6815744]{0:T(1024)(128)(4,1)} %bitcast.21), calls=%async_computation.3 | async-start | bytes 5242880
  7.1 3.0 %collective-permute-start = (f32[16,512]{1,0:T(8,128)S(1)}, f32[16,512]{1,0:T(8,128)S(1)}, u32[]{:S(2)}, u32[]{:S(2)}) collective-permute-start(f32[16,512]{1,0:T(8,128)S(1)} %get-tuple-element.151), channel_id=1, source_target_pairs={{0,16},{16,0},{32,48},{48,32},{64,80},{80,64},{96,112},{112,96},{1... | collective-permute-start | bytes 98312 | tf_op jit(solution)/shard_map/ppermute | solution.py:558
  7.1 1.2 %copy-start.2 = (f32[16,16,512]{2,1,0:T(8,128)S(1)}, f32[16,16,512]{2,1,0:T(8,128)}, u32[]{:S(2)}) copy-start(f32[16,16,512]{2,1,0:T(8,128)} %f_ref.1) | copy-start | bytes 1572868
  8.3 1.6 %copy-start.3 = (f32[16,16,512]{2,1,0:T(8,128)S(1)}, f32[16,16,512]{2,1,0:T(8,128)}, u32[]{:S(2)}) copy-start(f32[16,16,512]{2,1,0:T(8,128)} %d_ref.4) | copy-start | bytes 1572868
  10.2 7.4 %collective-permute-start.2 = (f32[18,512]{1,0:T(8,128)S(1)}, f32[18,512]{1,0:T(8,128)S(1)}, u32[]{:S(2)}, u32[]{:S(2)}) collective-permute-start(f32[18,512]{1,0:T(8,128)S(1)} %get-tuple-element.86), channel_id=1, source_target_pairs={{0,1},{1,0},{2,3},{3,2},{4,5},{5,4},{6,7},{7,6},{8,9},{9,8},{10,11... | collective-permute-start | bytes 110600 | tf_op jit(solution)/shard_map/ppermute | solution.py:558
  10.9 6.8 %collective-permute-start.3 = (f32[18,512]{1,0:T(8,128)S(1)}, f32[18,512]{1,0:T(8,128)S(1)}, u32[]{:S(2)}, u32[]{:S(2)}) collective-permute-start(f32[18,512]{1,0:T(8,128)S(1)} %get-tuple-element.87), channel_id=1, source_target_pairs={{0,15},{1,2},{2,1},{3,4},{4,3},{5,6},{6,5},{7,8},{8,7},{9,10},{10,... | collective-permute-start | bytes 110600 | tf_op jit(solution)/shard_map/ppermute | solution.py:558
  18.5 4.9 %collective-permute-start.4 = (f32[16,512]{1,0:T(8,128)S(1)}, f32[16,512]{1,0:T(8,128)S(1)}, u32[]{:S(2)}, u32[]{:S(2)}) collective-permute-start(f32[16,512]{1,0:T(8,128)S(1)} %get-tuple-element.96), channel_id=1, source_target_pairs={{0,16},{16,0},{32,48},{48,32},{64,80},{80,64},{96,112},{112,96},{1... | collective-permute-start | bytes 98312 | tf_op jit(solution)/shard_map/ppermute | solution.py:558
  18.6 4.8 %collective-permute-start.5 = (f32[16,512]{1,0:T(8,128)S(1)}, f32[16,512]{1,0:T(8,128)S(1)}, u32[]{:S(2)}, u32[]{:S(2)}) collective-permute-start(f32[16,512]{1,0:T(8,128)S(1)} %get-tuple-element.97), channel_id=1, source_target_pairs={{0,240},{16,32},{32,16},{48,64},{64,48},{80,96},{96,80},{112,128},... | collective-permute-start | bytes 98312 | tf_op jit(solution)/shard_map/ppermute | solution.py:558
  19.7 7.8 %copy-start.5 = (bf16[26,8,8,256]{3,2,1,0:T(8,128)(2,1)S(1)}, bf16[26,8,8,256]{3,2,1,0:T(8,128)(2,1)}, u32[]{:S(2)}) copy-start(bf16[26,8,8,256]{3,2,1,0:T(8,128)(2,1)} %w_ref.11) | copy-start | bytes 2555908
  19.7 7.8 %copy-start.6 = (f32[8,8,256]{2,1,0:T(8,128)S(1)}, f32[8,8,256]{2,1,0:T(8,128)}, u32[]{:S(2)}) copy-start(f32[8,8,256]{2,1,0:T(8,128)} %d_ref.7) | copy-start | bytes 196612
  23.5 10.7 %copy-start.7 = (s32[1,1,16,1]{2,3,1,0:T(1,128)S(1)}, s32[1,1,16,1]{2,3,1,0:T(1,128)}, u32[]{:S(2)}) copy-start(s32[1,1,16,1]{2,3,1,0:T(1,128)} %param.16) | copy-start | bytes 196
  23.5 6.0 %collective-permute-start.6 = (f32[18,512]{1,0:T(8,128)S(1)}, f32[18,512]{1,0:T(8,128)S(1)}, u32[]{:S(2)}, u32[]{:S(2)}) collective-permute-start(f32[18,512]{1,0:T(8,128)S(1)} %get-tuple-element.103), channel_id=1, source_target_pairs={{0,1},{1,0},{2,3},{3,2},{4,5},{5,4},{6,7},{7,6},{8,9},{9,8},{10,11... | collective-permute-start | bytes 110600 | tf_op jit(solution)/shard_map/ppermute | solution.py:558
  27.5 4.1 %collective-permute-start.7 = (f32[18,512]{1,0:T(8,128)S(1)}, f32[18,512]{1,0:T(8,128)S(1)}, u32[]{:S(2)}, u32[]{:S(2)}) collective-permute-start(f32[18,512]{1,0:T(8,128)S(1)} %get-tuple-element.104), channel_id=1, source_target_pairs={{0,15},{1,2},{2,1},{3,4},{4,3},{5,6},{6,5},{7,8},{8,7},{9,10},{10,... | collective-permute-start | bytes 110600 | tf_op jit(solution)/shard_map/ppermute | solution.py:558
  32.4 7.6 %collective-permute-start.8 = (f32[16,512]{1,0:T(8,128)S(1)}, f32[16,512]{1,0:T(8,128)S(1)}, u32[]{:S(2)}, u32[]{:S(2)}) collective-permute-start(f32[16,512]{1,0:T(8,128)S(1)} %get-tuple-element.118), channel_id=1, source_target_pairs={{0,16},{16,0},{32,48},{48,32},{64,80},{80,64},{96,112},{112,96},{1... | collective-permute-start | bytes 98312 | tf_op jit(solution)/shard_map/ppermute | solution.py:558
  32.5 7.6 %collective-permute-start.9 = (f32[16,512]{1,0:T(8,128)S(1)}, f32[16,512]{1,0:T(8,128)S(1)}, u32[]{:S(2)}, u32[]{:S(2)}) collective-permute-start(f32[16,512]{1,0:T(8,128)S(1)} %get-tuple-element.119), channel_id=1, source_target_pairs={{0,240},{16,32},{32,16},{48,64},{64,48},{80,96},{96,80},{112,128},... | collective-permute-start | bytes 98312 | tf_op jit(solution)/shard_map/ppermute | solution.py:558
  34.4 9.3 %collective-permute-start.11 = (f32[55,8,256]{2,1,0:T(8,128)S(1)}, f32[55,8,256]{2,1,0:T(8,128)S(1)}, u32[]{:S(2)}, u32[]{:S(2)}) collective-permute-start(f32[55,8,256]{2,1,0:T(8,128)S(1)} %get-tuple-element.106), channel_id=1, source_target_pairs={{0,16},{16,0},{32,48},{48,32},{64,80},{80,64},{96,112},{112,96},{1... | collective-permute-start | bytes 1351688 | tf_op jit(solution)/shard_map/ppermute | solution.py:558
  34.5 9.2 %collective-permute-start.12 = (f32[55,8,256]{2,1,0:T(8,128)S(1)}, f32[55,8,256]{2,1,0:T(8,128)S(1)}, u32[]{:S(2)}, u32[]{:S(2)}) collective-permute-start(f32[55,8,256]{2,1,0:T(8,128)S(1)} %get-tuple-element.107), channel_id=1, source_target_pairs={{0,240},{16,32},{32,16},{48,64},{64,48},{80,96},{96,80},{112,128},... | collective-permute-start | bytes 1351688 | tf_op jit(solution)/shard_map/ppermute | solution.py:558
  40.1 5.6 %collective-permute-start.10 = (f32[18,512]{1,0:T(8,128)S(1)}, f32[18,512]{1,0:T(8,128)S(1)}, u32[]{:S(2)}, u32[]{:S(2)}) collective-permute-start(f32[18,512]{1,0:T(8,128)S(1)} %get-tuple-element.125), channel_id=1, source_target_pairs={{0,1},{1,0},{2,3},{3,2},{4,5},{5,4},{6,7},{7,6},{8,9},{9,8},{10,11... | collective-permute-start | bytes 110600 | tf_op jit(solution)/shard_map/ppermute | solution.py:558
  43.6 5.7 %collective-permute-start.13 = (f32[18,512]{1,0:T(8,128)S(1)}, f32[18,512]{1,0:T(8,128)S(1)}, u32[]{:S(2)}, u32[]{:S(2)}) collective-permute-start(f32[18,512]{1,0:T(8,128)S(1)} %get-tuple-element.130), channel_id=1, source_target_pairs={{0,15},{1,2},{2,1},{3,4},{4,3},{5,6},{6,5},{7,8},{8,7},{9,10},{10,... | collective-permute-start | bytes 110600 | tf_op jit(solution)/shard_map/ppermute | solution.py:558
  45.7 19.3 %collective-permute-start.18 = (f32[84,8,256]{2,1,0:T(8,128)S(1)}, f32[84,8,256]{2,1,0:T(8,128)S(1)}, u32[]{:S(2)}, u32[]{:S(2)}) collective-permute-start(f32[84,8,256]{2,1,0:T(8,128)S(1)} %get-tuple-element.135), channel_id=1, source_target_pairs={{0,1},{1,0},{2,3},{3,2},{4,5},{5,4},{6,7},{7,6},{8,9},{9,8},{10,11... | collective-permute-start | bytes 2064392 | tf_op jit(solution)/shard_map/ppermute | solution.py:558
  49.3 17.2 %collective-permute-start.19 = (f32[84,8,256]{2,1,0:T(8,128)S(1)}, f32[84,8,256]{2,1,0:T(8,128)S(1)}, u32[]{:S(2)}, u32[]{:S(2)}) collective-permute-start(f32[84,8,256]{2,1,0:T(8,128)S(1)} %get-tuple-element.136), channel_id=1, source_target_pairs={{0,15},{1,2},{2,1},{3,4},{4,3},{5,6},{6,5},{7,8},{8,7},{9,10},{10,... | collective-permute-start | bytes 2064392 | tf_op jit(solution)/shard_map/ppermute | solution.py:558
  50.5 1.3 %collective-permute-start.14 = (f32[3,8,256]{2,1,0:T(8,128)S(1)}, f32[3,8,256]{2,1,0:T(8,128)S(1)}, u32[]{:S(2)}, u32[]{:S(2)}) collective-permute-start(f32[3,8,256]{2,1,0:T(8,128)S(1)} %get-tuple-element.132), channel_id=1, source_target_pairs={{0,16},{16,0},{32,48},{48,32},{64,80},{80,64},{96,112},{112,96},{1... | collective-permute-start | bytes 73736 | tf_op jit(solution)/shard_map/ppermute | solution.py:558
  50.6 4.5 %collective-permute-start.15 = (f32[3,8,256]{2,1,0:T(8,128)S(1)}, f32[3,8,256]{2,1,0:T(8,128)S(1)}, u32[]{:S(2)}, u32[]{:S(2)}) collective-permute-start(f32[3,8,256]{2,1,0:T(8,128)S(1)} %get-tuple-element.133), channel_id=1, source_target_pairs={{0,240},{16,32},{32,16},{48,64},{64,48},{80,96},{96,80},{112,128},... | collective-permute-start | bytes 73736 | tf_op jit(solution)/shard_map/ppermute | solution.py:558
  55.2 13.5 %collective-permute-start.17 = (f32[14,3,256]{2,1,0:T(4,128)S(1)}, f32[14,3,256]{2,1,0:T(4,128)S(1)}, u32[]{:S(2)}, u32[]{:S(2)}) collective-permute-start(f32[14,3,256]{2,1,0:T(4,128)S(1)} %get-tuple-element.152), channel_id=1, source_target_pairs={{0,15},{1,2},{2,1},{3,4},{4,3},{5,6},{6,5},{7,8},{8,7},{9,10},{10,... | collective-permute-start | bytes 129032 | tf_op jit(solution)/shard_map/ppermute | solution.py:558
  57.3 11.4 %collective-permute-start.16 = (f32[14,3,256]{2,1,0:T(4,128)S(1)}, f32[14,3,256]{2,1,0:T(4,128)S(1)}, u32[]{:S(2)}, u32[]{:S(2)}) collective-permute-start(f32[14,3,256]{2,1,0:T(4,128)S(1)} %get-tuple-element.153), channel_id=1, source_target_pairs={{0,1},{1,0},{2,3},{3,2},{4,5},{5,4},{6,7},{7,6},{8,9},{9,8},{10,11... | collective-permute-start | bytes 129032 | tf_op jit(solution)/shard_map/ppermute | solution.py:558
  68.7 17.5 %copy-start = (f32[1,1,32,128,128]{4,3,2,1,0:T(8,128)S(1)}, f32[1,1,32,128,128]{4,3,2,1,0:T(8,128)}, u32[]{:S(2)}) copy-start(f32[1,1,32,128,128]{4,3,2,1,0:T(8,128)} %param.17) | copy-start | bytes 6291460
  68.7 28.7 %copy-start.1 = (bf16[26,4,4,128]{3,2,1,0:T(4,128)(2,1)S(1)}, bf16[26,4,4,128]{3,2,1,0:T(4,128)(2,1)}, u32[]{:S(2)}) copy-start(bf16[26,4,4,128]{3,2,1,0:T(4,128)(2,1)} %param.15) | copy-start | bytes 319492
  68.7 28.7 %copy-start.4 = (f32[4,4,128]{2,1,0:T(4,128)S(1)}, f32[4,4,128]{2,1,0:T(4,128)}, u32[]{:S(2)}) copy-start(f32[4,4,128]{2,1,0:T(4,128)} %param.14) | copy-start | bytes 24580
